TPU v7x, 32 devices: a whole 2x2x4 slice. The times are simulated.
32 devices in a mesh: gx: 4 (over y, x), gy: 8 (over z, core).
Axes of the slice: x: 2, y: 2, z: 4, core: 2. Of those that a mesh axis runs over, the one named last changes fastest.
Arguments:
- object_field: float32 [2, 2, 2048, 1024], P(None, None, 'gy', 'gx'), may hold values from -5 to 5
- probe: float32 [2, 256, 256], replicated, may hold values from -6 to 6
- positions: int32 [16, 4, 2], P('gy', 'gx'), may hold values from 0 to 256, as said below
- residual: bfloat16 [16, 4, 2, 256, 256], P('gy', 'gx'), may hold values from -6 to 6
- saved_wave: bfloat16 [16, 4, 2, 256, 256], P('gy', 'gx'), may hold values from -6 to 6
Outputs:
- new_object: float32 [2, 2, 2048, 1024], P(None, None, 'gy', 'gx')
Inputs may be any that keep to these rules, and one draw needn't show every extreme that they name: `positions`: row and column of each position's window corner in a frame whose anchor lies 128 cells above and to the left of its tile's first cell, so that the window stays within 128 cells of the tile; position p of a tile lies near row 128 and column 128 * (1 + p mod 2) of that frame.
All inputs are finite; a program needn't handle non-finite values.
Results may differ from a plain program's by a relative error of at most 0.0003.
Values sent between devices are 32-bit elements; how exact they have to be, the bound alone decides.
No kernel may reach another device: no remote copies, remote signals or barrier semaphores. Data moves between devices by JAX's collectives and lax.ppermute only.
A program may use at most 64 MiB of HBM per device.

v0:
```python
import math

import jax
import jax.numpy as jnp
from jax import lax
from jax.sharding import PartitionSpec as P

fresnel_rate = 200.0
ridge = 0.5


def padded(block, sides, width):
    for axis, dim in sides:
        count = lax.axis_size(axis)
        forward = [(i, i + 1) for i in range(count - 1)]
        backward = [(target, source) for source, target in forward]
        low = lax.ppermute(
            lax.slice_in_dim(block, block.shape[dim] - width, None, axis=dim), axis, forward
        )
        high = lax.ppermute(lax.slice_in_dim(block, 0, width, axis=dim), axis, backward)
        block = jnp.concatenate([low, block, high], axis=dim)
    return block


def from_behind(value, axis, steps):
    count = lax.axis_size(axis)
    leading, last = (max(0, -steps), min(count, count - steps))
    return lax.ppermute(value, axis, [(source, source + steps) for source in range(leading, last)])


def kernel_conj(size):
    index = jnp.arange(size, dtype=jnp.int32)
    freq = ((index + size // 2) % size - size // 2).astype(jnp.float32) / size
    phase = fresnel_rate * (freq[:, None] ** 2 + freq[None, :] ** 2)
    return (jnp.cos(phase), jnp.sin(phase))


def block_tables(size, inverse):
    index = jnp.arange(size, dtype=jnp.int32)
    product = index[:, None] * index[None, :] % size
    angle = product.astype(jnp.float32) * (2.0 * math.pi / size)
    scale = 1.0 / math.sqrt(size)
    table_re = jnp.cos(angle) * scale
    table_im = -jnp.sin(angle) * scale
    if inverse:
        table_im = -table_im
    left_table = jnp.stack([jnp.stack([table_re, -table_im]), jnp.stack([table_im, table_re])])
    right_table = jnp.stack([jnp.stack([table_re, table_im]), jnp.stack([-table_im, table_re])])
    return (left_table, right_table)


def transform(fields, inverse):
    left_table, right_table = block_tables(fields.shape[-1], inverse)
    inner = jnp.einsum("abjk,pbkl->pajl", left_table, fields, precision=lax.Precision.HIGHEST)
    return jnp.einsum("pbjk,bakl->pajl", inner, right_table, precision=lax.Precision.HIGHEST)


def shards(object_field, probe, positions, residual, saved_wave):
    window = probe.shape[-1]
    margin = window // 2
    spots = positions.reshape(-1, 2)
    spot_count = spots.shape[0]
    second = object_field[1]
    second_ext = padded(second, (("gx", 2), ("gy", 1)), margin)
    detector = residual.reshape(spot_count, 2, window, window).astype(jnp.float32)
    wave = saved_wave.reshape(spot_count, 2, window, window).astype(jnp.float32)
    anchor = jnp.zeros((), jnp.int32)
    patches = jnp.stack(
        [
            lax.dynamic_slice(
                second_ext, (anchor, spots[number, 0], spots[number, 1]), (2, window, window)
            )
            for number in range(spot_count)
        ]
    )
    field = transform(detector, True)
    field_re = field[:, 0]
    field_im = field[:, 1]
    patch_re = patches[:, 0]
    patch_im = patches[:, 1]
    chi = jnp.stack(
        [patch_re * field_re + patch_im * field_im, patch_re * field_im - patch_im * field_re],
        axis=1,
    )
    spec = transform(chi, False)
    kernel_re, kernel_im = kernel_conj(window)
    spec_re = spec[:, 0]
    spec_im = spec[:, 1]
    moved = jnp.stack(
        [kernel_re * spec_re - kernel_im * spec_im, kernel_re * spec_im + kernel_im * spec_re],
        axis=1,
    )
    back = transform(moved, True)
    back_re = back[:, 0]
    back_im = back[:, 1]
    probe_re = probe[0]
    probe_im = probe[1]
    first_re = probe_re * back_re + probe_im * back_im
    first_im = probe_re * back_im - probe_im * back_re
    wave_re = wave[:, 0]
    wave_im = wave[:, 1]
    second_re = wave_re * field_re + wave_im * field_im
    second_im = wave_re * field_im - wave_im * field_re
    light = probe_re * probe_re + probe_im * probe_im
    parts = [first_re, first_im, second_re, second_im]
    planes = jnp.stack(parts + [jnp.broadcast_to(light, first_re.shape)], axis=1)
    channels = planes.shape[1]
    summed = jnp.zeros((channels, 2 * window, 2 * window), jnp.float32)
    for number in range(spot_count):
        corner = (anchor, spots[number, 0], spots[number, 1])
        current = lax.dynamic_slice(summed, corner, (channels, window, window))
        summed = lax.dynamic_update_slice(summed, current + planes[number], corner)
    from_rows = []
    for direction in (1, -1):
        edge_rows = summed[:, 3 * margin :, :] if direction == 1 else summed[:, :margin, :]
        from_rows.append(from_behind(edge_rows, "gy", direction))
    row_total = summed[:, margin : 3 * margin, :] + jnp.concatenate(from_rows, axis=1)
    from_columns = []
    for direction in (1, -1):
        edge_columns = row_total[:, :, 3 * margin :] if direction == 1 else row_total[:, :, :margin]
        from_columns.append(from_behind(edge_columns, "gx", direction))
    total = row_total[:, :, margin : 3 * margin] + jnp.concatenate(from_columns, axis=2)
    light_tile = total[4]
    grads = total[:4].reshape(2, 2, window, window)
    return object_field - grads / (light_tile + ridge)


def solution(mesh):
    placed = (
        P(None, None, "gy", "gx"),
        P(),
        P("gy", "gx", None),
        P("gy", "gx", None, None, None),
        P("gy", "gx", None, None, None),
    )
    return jax.shard_map(
        shards, mesh=mesh, in_specs=placed, out_specs=P(None, None, "gy", "gx"), check_vma=False
    )
```

profile of v0, /device:TPU:11, one launch (start us, length us, event | category | flops | bytes accessed | tf_op | source)
XLA Modules:
  0.0 150.3 jit_solution(10878024354502926020)
XLA Ops:
  0.0 1.2 slice_bitcast_fusion.2
  1.2 3.1 %collective-permute-start = (f32[2,256,128]{2,1,0:T(8,128)S(1)}, f32[2,256,128]{2,1,0:T(8,128)S(1)}, u32[]{:S(2)}, u32[]{:S(2)}) collective-permute-start(f32[2,256,128]{2,1,0:T(8,128)S(1)} %get-tuple-element.19), channel_id=1, source_target_pairs={{0,8},{8,16},{16,24},{1,9},{9,17},{17,25},{2,10},{10,18},{18,26},{... | collective-permute-start | bytes 786440 | tf_op jit(solution)/shard_map/ppermute | solution.py:17
  4.4 2.2 %collective-permute-start.1 = (f32[2,256,128]{2,1,0:T(8,128)S(1)}, f32[2,256,128]{2,1,0:T(8,128)S(1)}, u32[]{:S(2)}, u32[]{:S(2)}) collective-permute-start(f32[2,256,128]{2,1,0:T(8,128)S(1)} %get-tuple-element.20), channel_id=1, source_target_pairs={{8,0},{16,8},{24,16},{9,1},{17,9},{25,17},{10,2},{18,10},{26,18},{... | collective-permute-start | bytes 786440 | tf_op jit(solution)/shard_map/ppermute | solution.py:20
  6.5 1.0 fusion.23
  7.5 1.1 negate_multiply_fusion
  8.6 0.1 fusion.11
  8.8 0.0 copy-start.2
  8.8 1.0 convolution_bitcast_fusion.5
  9.9 0.0 copy-start.18
  9.9 1.9 %convolution_bitcast_fusion.4 = f32[2,2,256,256]{2,3,0,1:T(8,128)S(1)} fusion(f32[2,2,256,256,1]{3,2,1,0,4:T(8,128)S(1)} %convolution_bitcast_fusion.5, f32[1,2,256,256]{2,3,0,1:T(8,128)S(1)} %get-tuple-element.22, f32[1,2,256,256]{2,3,0,1:T(8,128)S(1)} %get-tuple-element.25), kind=kOutput, calls=%fused_computation.6 | convolution fusion | flops 1610874880 | bytes 3145728 | tf_op jit(solution)/shard_map/pbjk,bakl->pajl/dot_general | solution.py:55
  11.8 0.7 fusion.35
  12.5 0.0 copy-start.17
  12.5 0.0 collective-permute-done
  12.5 4.3 %collective-permute-done.1 = f32[2,256,128]{2,1,0:T(8,128)S(1)} collective-permute-done((f32[2,256,128]{2,1,0:T(8,128)S(1)}, f32[2,256,128]{2,1,0:T(8,128)S(1)}, u32[]{:S(2)}, u32[]{:S(2)}) %collective-permute-start.1) | collective-permute-done | bytes 262176 | tf_op jit(solution)/shard_map/ppermute | solution.py:20
  16.9 0.1 pad_maximum_fusion.2
  17.0 1.1 fusion.33
  18.1 4.6 %collective-permute-start.2 = (f32[2,128,512]{2,1,0:T(8,128)}, f32[2,128,512]{2,1,0:T(8,128)}, u32[]{:S(2)}, u32[]{:S(2)}) collective-permute-start(f32[2,128,512]{2,1,0:T(8,128)} %get-tuple-element.15), channel_id=1, source_target_pairs={{0,1},{1,2},{2,3},{3,4},{4,5},{5,6},{6,7},{8,9},{9,10},{10,11},{11... | collective-permute-start | bytes 1572872 | tf_op jit(solution)/shard_map/ppermute | solution.py:17
  22.7 1.9 %collective-permute-start.3 = (f32[2,128,512]{2,1,0:T(8,128)}, f32[2,128,512]{2,1,0:T(8,128)}, u32[]{:S(2)}, u32[]{:S(2)}) collective-permute-start(f32[2,128,512]{2,1,0:T(8,128)} %get-tuple-element.16), channel_id=1, source_target_pairs={{1,0},{2,1},{3,2},{4,3},{5,4},{6,5},{7,6},{9,8},{10,9},{11,10},{12... | collective-permute-start | bytes 1572872 | tf_op jit(solution)/shard_map/ppermute | solution.py:20
  29.7 0.9 copy.13
  30.6 1.0 copy.12
  31.6 0.1 copy.6
  31.7 0.9 copy.11
  35.1 2.0 %fusion.19 = (f32[256,256]{0,1:T(8,128)}, f32[256,256]{0,1:T(8,128)}) fusion(f32[256]{0:T(256)S(1)} %fusion.27), kind=kLoop, calls=%fused_computation.61 | loop fusion | flops 131072 | bytes 525312 | tf_op jit(solution)/shard_map/cos | solution.py:35
  37.1 1.1 bitcast_convert_fusion
  38.3 0.0 collective-permute-done.3
  38.3 1.8 %pad_maximum_fusion = f32[2,512,512]{2,1,0:T(8,128)S(1)} fusion(f32[2,128,512]{2,1,0:T(8,128)} %collective-permute-done.3, f32[2,256,128]{2,1,0:T(8,128)} %copy-done.16, f32[2,256,256]{2,1,0:T(8,128)} %copy-done.8, f32[2,256,128]{2,1,0:T(8,128)} %copy-done.15, f32[2,128,512]{2,1,0:T(8,128)} %collective-permute-done.2), kind=kLoop, calls=%fused_computation.1 | loop fusion | flops 2097152 | bytes 4194304 | tf_op jit(solution)/shard_map/concatenate | solution.py:21
  40.0 1.3 constant_dynamic-slice_fusion.1
  41.4 2.0 %copy.8 = f32[2,256,256]{1,2,0:T(8,128)} copy(f32[2,256,256]{2,1,0:T(8,128)} %get-tuple-element.11) | data formatting | bytes 1048576 | tf_op jit(solution)/shard_map/dynamic_slice | solution.py:70
  43.4 2.1 %copy.9 = f32[2,256,256]{1,2,0:T(8,128)} copy(f32[2,256,256]{2,1,0:T(8,128)} %get-tuple-element.12) | data formatting | bytes 1048576 | tf_op jit(solution)/shard_map/dynamic_slice | solution.py:70
  45.5 1.6 %multiply_add_fusion.1 = (f32[2,1,256,256]{2,3,0,1:T(8,128)S(1)}, f32[2,1,256,256]{2,3,0,1:T(8,128)S(1)}) fusion(f32[2,2,256,256]{2,3,0,1:T(8,128)S(1)} %convolution_bitcast_fusion.4, f32[1,2,256,256]{2,3,0,1:T(8,128)} %bitcast.113, f32[1,2,256,256]{2,3,0,1:T(8,128)} %bitcast.112), kind=kLoop, calls=%fused_computation.46 | loop fusion | flops 1179648 | bytes 3145728 | tf_op jit(solution)/shard_map/add | solution.py:82
  47.1 0.0 copy-start.3
  47.1 0.0 copy-done.7
  47.1 1.9 %convolution_bitcast_fusion.3 = f32[2,2,256,256,1]{3,2,1,0,4:T(8,128)S(1)} fusion(f32[1,2,256,256]{2,3,0,1:T(8,128)S(1)} %copy-done.5, f32[1,2,256,256]{2,3,0,1:T(8,128)S(1)} %copy-done.7, f32[2,1,256,256]{2,3,0,1:T(8,128)S(1)} %get-tuple-element.10, f32[2,1,256,256]{2,3,0,1:T(8,128)S(1)} %get-tuple-element.9), kind=kOutput, calls=%fused_computation.5 | convolution fusion | flops 1611137024 | bytes 3145728 | tf_op jit(solution)/shard_map/abjk,pbkl->pajl/dot_general | solution.py:54
  49.1 1.9 %convolution_bitcast_fusion.2 = f32[2,2,256,256]{2,3,0,1:T(8,128)S(1)} fusion(f32[2,2,256,256,1]{3,2,1,0,4:T(8,128)S(1)} %convolution_bitcast_fusion.3, f32[1,2,256,256]{2,3,1,0:T(8,128)S(1)} %copy-done.3, f32[1,2,256,256]{2,3,1,0:T(8,128)S(1)} %get-tuple-element.21), kind=kOutput, calls=%fused_computation.4 | convolution fusion | flops 1610874880 | bytes 3145728 | tf_op jit(solution)/shard_map/pbjk,bakl->pajl/dot_general | solution.py:55
  51.0 0.1 multiply_subtract_fusion
  51.1 1.9 %convolution_bitcast_fusion.1 = f32[2,2,256,256,1]{3,2,1,0,4:T(8,128)S(1)} fusion(f32[1,2,256,256]{2,3,1,0:T(8,128)S(1)} %copy-done.3, f32[1,2,256,256]{2,3,1,0:T(8,128)S(1)} %get-tuple-element.21, f32[2,1,256,256]{2,3,0,1:T(8,128)S(1)} %get-tuple-element.14, f32[2,1,256,256]{2,3,0,1:T(8,128)S(1)} %get-tuple-element.13), kind=kOutput, calls=%fused_computation.3 | convolution fusion | flops 1611137024 | bytes 3145728 | tf_op jit(solution)/shard_map/abjk,pbkl->pajl/dot_general | solution.py:54
  53.0 1.9 %convolution_bitcast_fusion = f32[2,2,256,256]{2,3,0,1:T(8,128)S(1)} fusion(f32[2,2,256,256,1]{3,2,1,0,4:T(8,128)S(1)} %convolution_bitcast_fusion.1, f32[1,2,256,256]{2,3,0,1:T(8,128)S(1)} %copy-done.5, f32[1,2,256,256]{2,3,0,1:T(8,128)S(1)} %copy-done.7), kind=kOutput, calls=%fused_computation.2 | convolution fusion | flops 1610874880 | bytes 3145728 | tf_op jit(solution)/shard_map/pbjk,bakl->pajl/dot_general | solution.py:55
  54.9 0.1 add_dynamic-update-slice_fusion.1
  55.0 0.1 subtract_dynamic-update-slice_fusion.1
  55.1 0.1 add_dynamic-update-slice_fusion
  55.3 0.1 subtract_dynamic-update-slice_fusion
  55.4 0.7 copy-done.12
  56.1 1.5 copy-done.9
  57.6 0.1 slice_bitcast_fusion.1
  57.7 3.0 %broadcast_in_dim.2 = f32[5,512,512]{1,2,0:T(8,128)} broadcast(f32[]{:T(128)} %constant.39.clone.1), dimensions={} | broadcast | bytes 5242884 | tf_op jit(solution)/shard_map/broadcast_in_dim | solution.py:108
  60.7 14.8 %dynamic_update_slice.6 = f32[5,512,512]{1,2,0:T(8,128)} dynamic-update-slice(f32[5,512,512]{1,2,0:T(8,128)} %broadcast_in_dim.2, f32[5,256,256]{1,2,0:T(8,128)S(1)} %slice_bitcast_fusion.1, s32[]{:T(128)} %constant.40.clone.1, s32[]{:T(128)S(6)} %select_n.81, s32[]{:T(128)S(6)} %select_n.82) | dynamic-update-slice | bytes 2621444 | tf_op jit(solution)/shard_map/dynamic_update_slice | solution.py:112
  75.5 2.4 %fusion = f32[5,256,256]{1,2,0:T(8,128)S(1)} fusion(f32[2,5,256,256]{2,3,0,1:T(8,128)} %copy-done.9, f32[5,512,512]{1,2,0:T(8,128)} %dynamic_update_slice.6, s32[]{:T(128)S(6)} %select_n.83, s32[]{:T(128)S(6)} %select_n.84), kind=kLoop, calls=%fused_computation.10 | loop fusion | flops 327680 | bytes 3932168 | tf_op jit(solution)/shard_map/add | solution.py:112
  77.9 13.7 %dynamic_update_slice.7 = f32[5,512,512]{1,2,0:T(8,128)} dynamic-update-slice(f32[5,512,512]{1,2,0:T(8,128)} %dynamic_update_slice.6, f32[5,256,256]{1,2,0:T(8,128)S(1)} %fusion, s32[]{:T(128)} %constant.40.clone.1, s32[]{:T(128)S(6)} %select_n.83, s32[]{:T(128)S(6)} %select_n.84) | dynamic-update-slice | bytes 2621444 | tf_op jit(solution)/shard_map/dynamic_update_slice | solution.py:112
  91.6 2.0 %fusion.31 = (f32[5,128,512]{1,2,0:T(8,128)S(1)}, f32[5,128,512]{1,2,0:T(8,128)S(1)}) fusion(f32[5,512,512]{1,2,0:T(8,128)} %dynamic_update_slice.7), kind=kLoop, calls=%fused_computation.81 | loop fusion | bytes 5242880 | tf_op jit(solution)/shard_map/slice | solution.py:115
  93.7 4.6 %collective-permute-start.4 = (f32[5,128,512]{1,2,0:T(8,128)S(1)}, f32[5,128,512]{1,2,0:T(8,128)S(1)}, u32[]{:S(2)}, u32[]{:S(2)}) collective-permute-start(f32[5,128,512]{1,2,0:T(8,128)S(1)} %get-tuple-element.5), channel_id=1, source_target_pairs={{0,1},{1,2},{2,3},{3,4},{4,5},{5,6},{6,7},{8,9},{9,10},{10,11},{11... | collective-permute-start | bytes 3932168 | tf_op jit(solution)/shard_map/ppermute | solution.py:28
  98.3 1.9 %collective-permute-start.5 = (f32[5,128,512]{1,2,0:T(8,128)S(1)}, f32[5,128,512]{1,2,0:T(8,128)S(1)}, u32[]{:S(2)}, u32[]{:S(2)}) collective-permute-start(f32[5,128,512]{1,2,0:T(8,128)S(1)} %get-tuple-element.6), channel_id=1, source_target_pairs={{1,0},{2,1},{3,2},{4,3},{5,4},{6,5},{7,6},{9,8},{10,9},{11,10},{12... | collective-permute-start | bytes 3932168 | tf_op jit(solution)/shard_map/ppermute | solution.py:28
  100.2 12.6 %collective-permute-done.4 = f32[5,128,512]{1,2,0:T(8,128)S(1)} collective-permute-done((f32[5,128,512]{1,2,0:T(8,128)S(1)}, f32[5,128,512]{1,2,0:T(8,128)S(1)}, u32[]{:S(2)}, u32[]{:S(2)}) %collective-permute-start.4) | collective-permute-done | bytes 1310752 | tf_op jit(solution)/shard_map/ppermute | solution.py:28
  112.8 4.4 %collective-permute-done.5 = f32[5,128,512]{1,2,0:T(8,128)S(1)} collective-permute-done((f32[5,128,512]{1,2,0:T(8,128)S(1)}, f32[5,128,512]{1,2,0:T(8,128)S(1)}, u32[]{:S(2)}, u32[]{:S(2)}) %collective-permute-start.5) | collective-permute-done | bytes 1310752 | tf_op jit(solution)/shard_map/ppermute | solution.py:28
  117.2 0.4 slice_add_fusion
  117.6 0.1 fusion.32
  117.7 1.9 %collective-permute-start.6 = (f32[5,256,128]{1,2,0:T(8,128)S(1)}, f32[5,256,128]{1,2,0:T(8,128)S(1)}, u32[]{:S(2)}, u32[]{:S(2)}) collective-permute-start(f32[5,256,128]{1,2,0:T(8,128)S(1)} %get-tuple-element.7), channel_id=1, source_target_pairs={{0,8},{8,16},{16,24},{1,9},{9,17},{17,25},{2,10},{10,18},{18,26},{... | collective-permute-start | bytes 1966088 | tf_op jit(solution)/shard_map/ppermute | solution.py:28
  119.7 3.4 %collective-permute-start.7 = (f32[5,256,128]{1,2,0:T(8,128)S(1)}, f32[5,256,128]{1,2,0:T(8,128)S(1)}, u32[]{:S(2)}, u32[]{:S(2)}) collective-permute-start(f32[5,256,128]{1,2,0:T(8,128)S(1)} %get-tuple-element.8), channel_id=1, source_target_pairs={{8,0},{16,8},{24,16},{9,1},{17,9},{25,17},{10,2},{18,10},{26,18},{... | collective-permute-start | bytes 1966088 | tf_op jit(solution)/shard_map/ppermute | solution.py:28
  123.1 11.2 %collective-permute-done.6 = f32[5,256,128]{1,2,0:T(8,128)S(1)} collective-permute-done((f32[5,256,128]{1,2,0:T(8,128)S(1)}, f32[5,256,128]{1,2,0:T(8,128)S(1)}, u32[]{:S(2)}, u32[]{:S(2)}) %collective-permute-start.6) | collective-permute-done | bytes 655392 | tf_op jit(solution)/shard_map/ppermute | solution.py:28
  134.2 12.9 %collective-permute-done.7 = f32[5,256,128]{1,2,0:T(8,128)S(1)} collective-permute-done((f32[5,256,128]{1,2,0:T(8,128)S(1)}, f32[5,256,128]{1,2,0:T(8,128)S(1)}, u32[]{:S(2)}, u32[]{:S(2)}) %collective-permute-start.7) | collective-permute-done | bytes 655392 | tf_op jit(solution)/shard_map/ppermute | solution.py:28
  147.1 0.2 slice_add_fusion.1
  147.4 0.1 slice.150
  147.5 0.3 copy.16
  147.8 0.1 copy.15
  147.9 2.4 %divide_subtract_fusion = f32[2,2,256,256]{3,2,1,0:T(8,128)} fusion(f32[2,2,256,256]{3,2,1,0:T(8,128)} %param.5, f32[2,2,256,256]{3,2,1,0:T(8,128)S(1)} %copy.16, f32[256,256]{1,0:T(8,128)S(1)} %copy.15), kind=kLoop, calls=%fused_computation.25 | loop fusion | flops 524288 | bytes 3407872 | tf_op jit(solution)/shard_map/sub | solution.py:125
  (38 shorter events, 0.2 us)
Async XLA Ops:
  0.0 8.8 %copy-start = (bf16[2,1,2,256,256]{4,3,2,1,0:T(8,128)(2,1)S(1)}, bf16[2,1,2,256,256]{4,3,2,1,0:T(8,128)(2,1)}, u32[]{:S(2)}) copy-start(bf16[2,1,2,256,256]{4,3,2,1,0:T(8,128)(2,1)} %param.8) | copy-start | bytes 1572868
  0.0 8.6 %copy-start.11 = (f32[2,256,256]{2,1,0:T(8,128)S(1)}, f32[2,256,256]{2,1,0:T(8,128)}, u32[]{:S(2)}) copy-start(f32[2,256,256]{2,1,0:T(8,128)} %param.6) | copy-start | bytes 1572868
  1.2 15.7 %copy-start.8 = (f32[2,256,256]{2,1,0:T(8,128)}, f32[2,256,256]{2,1,0:T(8,128)S(1)}, u32[]{:S(2)}) copy-start(f32[2,256,256]{2,1,0:T(8,128)S(1)} %slice_bitcast_fusion.2) | copy-start | bytes 1572868
  1.2 11.3 %collective-permute-start = (f32[2,256,128]{2,1,0:T(8,128)S(1)}, f32[2,256,128]{2,1,0:T(8,128)S(1)}, u32[]{:S(2)}, u32[]{:S(2)}) collective-permute-start(f32[2,256,128]{2,1,0:T(8,128)S(1)} %get-tuple-element.19), channel_id=1, source_target_pairs={{0,8},{8,16},{16,24},{1,9},{9,17},{17,25},{2,10},{10,18},{18,26},{... | collective-permute-start | bytes 786440 | tf_op jit(solution)/shard_map/ppermute | solution.py:17
  4.4 12.5 %collective-permute-start.1 = (f32[2,256,128]{2,1,0:T(8,128)S(1)}, f32[2,256,128]{2,1,0:T(8,128)S(1)}, u32[]{:S(2)}, u32[]{:S(2)}) collective-permute-start(f32[2,256,128]{2,1,0:T(8,128)S(1)} %get-tuple-element.20), channel_id=1, source_target_pairs={{8,0},{16,8},{24,16},{9,1},{17,9},{25,17},{10,2},{18,10},{26,18},{... | collective-permute-start | bytes 786440 | tf_op jit(solution)/shard_map/ppermute | solution.py:20
  8.8 3.0 %copy-start.2 = (f32[1,2,256,256]{2,3,1,0:T(8,128)}, f32[1,2,256,256]{2,3,1,0:T(8,128)S(1)}, u32[]{:S(2)}) copy-start(f32[1,2,256,256]{2,3,1,0:T(8,128)S(1)} %get-tuple-element.26) | copy-start | bytes 1572868
  8.8 3.0 %copy-start.4 = (f32[1,2,256,256]{2,3,0,1:T(8,128)}, f32[1,2,256,256]{2,3,0,1:T(8,128)S(1)}, u32[]{:S(2)}) copy-start(f32[1,2,256,256]{2,3,0,1:T(8,128)S(1)} %get-tuple-element.22) | copy-start | bytes 1572868
  8.8 3.0 %copy-start.6 = (f32[1,2,256,256]{2,3,0,1:T(8,128)}, f32[1,2,256,256]{2,3,0,1:T(8,128)S(1)}, u32[]{:S(2)}) copy-start(f32[1,2,256,256]{2,3,0,1:T(8,128)S(1)} %get-tuple-element.25) | copy-start | bytes 1572868
  9.9 1.9 %copy-start.18 = (s32[2,1,2]{2,1,0:T(1,128)S(1)}, s32[2,1,2]{2,1,0:T(1,128)}, u32[]{:S(2)}) copy-start(s32[2,1,2]{2,1,0:T(1,128)} %param.7) | copy-start | bytes 52
  12.5 18.1 %copy-start.17 = (bf16[2,1,2,256,256]{4,3,2,1,0:T(8,128)(2,1)S(1)}, bf16[2,1,2,256,256]{4,3,2,1,0:T(8,128)(2,1)}, u32[]{:S(2)}) copy-start(bf16[2,1,2,256,256]{4,3,2,1,0:T(8,128)(2,1)} %param.9) | copy-start | bytes 1572868
  12.5 5.5 %copy-start.15 = (f32[2,256,128]{2,1,0:T(8,128)}, f32[2,256,128]{2,1,0:T(8,128)S(1)}, u32[]{:S(2)}) copy-start(f32[2,256,128]{2,1,0:T(8,128)S(1)} %collective-permute-done) | copy-start | bytes 786436
  16.9 1.2 copy-start.16
  18.1 20.2 %collective-permute-start.2 = (f32[2,128,512]{2,1,0:T(8,128)}, f32[2,128,512]{2,1,0:T(8,128)}, u32[]{:S(2)}, u32[]{:S(2)}) collective-permute-start(f32[2,128,512]{2,1,0:T(8,128)} %get-tuple-element.15), channel_id=1, source_target_pairs={{0,1},{1,2},{2,3},{3,4},{4,5},{5,6},{6,7},{8,9},{9,10},{10,11},{11... | collective-permute-start | bytes 1572872 | tf_op jit(solution)/shard_map/ppermute | solution.py:17
  22.7 15.6 %collective-permute-start.3 = (f32[2,128,512]{2,1,0:T(8,128)}, f32[2,128,512]{2,1,0:T(8,128)}, u32[]{:S(2)}, u32[]{:S(2)}) collective-permute-start(f32[2,128,512]{2,1,0:T(8,128)} %get-tuple-element.16), channel_id=1, source_target_pairs={{1,0},{2,1},{3,2},{4,3},{5,4},{6,5},{7,6},{9,8},{10,9},{11,10},{12... | collective-permute-start | bytes 1572872 | tf_op jit(solution)/shard_map/ppermute | solution.py:20
  45.5 1.6 %copy-start.5 = (f32[1,2,256,256]{2,3,0,1:T(8,128)S(1)}, f32[1,2,256,256]{2,3,0,1:T(8,128)}, u32[]{:S(2)}) copy-start(f32[1,2,256,256]{2,3,0,1:T(8,128)} %copy-done.4) | copy-start | bytes 1572868
  45.5 1.7 %copy-start.7 = (f32[1,2,256,256]{2,3,0,1:T(8,128)S(1)}, f32[1,2,256,256]{2,3,0,1:T(8,128)}, u32[]{:S(2)}) copy-start(f32[1,2,256,256]{2,3,0,1:T(8,128)} %copy-done.6) | copy-start | bytes 1572868
  47.1 2.0 %copy-start.3 = (f32[1,2,256,256]{2,3,1,0:T(8,128)S(1)}, f32[1,2,256,256]{2,3,1,0:T(8,128)}, u32[]{:S(2)}) copy-start(f32[1,2,256,256]{2,3,1,0:T(8,128)} %copy-done.2) | copy-start | bytes 1572868
  49.1 1.9 %copy-start.13 = (f32[256,256]{0,1:T(8,128)S(1)}, f32[256,256]{0,1:T(8,128)}, u32[]{:S(2)}) copy-start(f32[256,256]{0,1:T(8,128)} %get-tuple-element.27) | copy-start | bytes 786436
  49.1 1.9 %copy-start.14 = (f32[256,256]{0,1:T(8,128)S(1)}, f32[256,256]{0,1:T(8,128)}, u32[]{:S(2)}) copy-start(f32[256,256]{0,1:T(8,128)} %get-tuple-element.28) | copy-start | bytes 786436
  53.0 1.9 %copy-start.10 = (f32[256,256]{0,1:T(8,128)S(1)}, f32[256,256]{0,1:T(8,128)}, u32[]{:S(2)}) copy-start(f32[256,256]{0,1:T(8,128)} %copy.11) | copy-start | bytes 786436
  55.1 1.0 copy-start.12
  56.1 1.5 %copy-start.9 = (f32[2,5,256,256]{2,3,0,1:T(8,128)}, f32[2,5,256,256]{2,3,0,1:T(8,128)S(1)}, u32[]{:S(2)}) copy-start(f32[2,5,256,256]{2,3,0,1:T(8,128)S(1)} %broadcast_dynamic-update-slice_fusion) | copy-start | bytes 7864324
  91.6 25.6 %copy-start.1 = (f32[5,512,512]{1,2,0:T(8,128)S(1)}, f32[5,512,512]{1,2,0:T(8,128)}, u32[]{:S(2)}) copy-start(f32[5,512,512]{1,2,0:T(8,128)} %dynamic_update_slice.7) | copy-start | bytes 15728644
  93.7 19.1 %collective-permute-start.4 = (f32[5,128,512]{1,2,0:T(8,128)S(1)}, f32[5,128,512]{1,2,0:T(8,128)S(1)}, u32[]{:S(2)}, u32[]{:S(2)}) collective-permute-start(f32[5,128,512]{1,2,0:T(8,128)S(1)} %get-tuple-element.5), channel_id=1, source_target_pairs={{0,1},{1,2},{2,3},{3,4},{4,5},{5,6},{6,7},{8,9},{9,10},{10,11},{11... | collective-permute-start | bytes 3932168 | tf_op jit(solution)/shard_map/ppermute | solution.py:28
  98.3 18.9 %collective-permute-start.5 = (f32[5,128,512]{1,2,0:T(8,128)S(1)}, f32[5,128,512]{1,2,0:T(8,128)S(1)}, u32[]{:S(2)}, u32[]{:S(2)}) collective-permute-start(f32[5,128,512]{1,2,0:T(8,128)S(1)} %get-tuple-element.6), channel_id=1, source_target_pairs={{1,0},{2,1},{3,2},{4,3},{5,4},{6,5},{7,6},{9,8},{10,9},{11,10},{12... | collective-permute-start | bytes 3932168 | tf_op jit(solution)/shard_map/ppermute | solution.py:28
  117.7 16.5 %collective-permute-start.6 = (f32[5,256,128]{1,2,0:T(8,128)S(1)}, f32[5,256,128]{1,2,0:T(8,128)S(1)}, u32[]{:S(2)}, u32[]{:S(2)}) collective-permute-start(f32[5,256,128]{1,2,0:T(8,128)S(1)} %get-tuple-element.7), channel_id=1, source_target_pairs={{0,8},{8,16},{16,24},{1,9},{9,17},{17,25},{2,10},{10,18},{18,26},{... | collective-permute-start | bytes 1966088 | tf_op jit(solution)/shard_map/ppermute | solution.py:28
  119.7 27.4 %collective-permute-start.7 = (f32[5,256,128]{1,2,0:T(8,128)S(1)}, f32[5,256,128]{1,2,0:T(8,128)S(1)}, u32[]{:S(2)}, u32[]{:S(2)}) collective-permute-start(f32[5,256,128]{1,2,0:T(8,128)S(1)} %get-tuple-element.8), channel_id=1, source_target_pairs={{8,0},{16,8},{24,16},{9,1},{17,9},{25,17},{10,2},{18,10},{26,18},{... | collective-permute-start | bytes 1966088 | tf_op jit(solution)/shard_map/ppermute | solution.py:28
where the time goes:
time: 153 us; the launch traced here: 150 us
  local copies, waits for them, and re-layouts  47.9 us (31%)
  waiting for transfers between devices  45.4 us (30%)
  starting transfers between devices  23.7 us (15%)
  other arithmetic  14.9 us (10%)
  matrix products  10.4 us (7%)
  between operations  8.11 us (5%)
    ppermute x4, waiting for transfers between devices, from_behind(): lax.ppermute(value, axis, [(source, source + steps) for source in range(l...  41 us
    dynamic_update_slice x2, local copies, waits for them, and re-layouts, shards(): summed = lax.dynamic_update_slice(summed, current + planes[number], corner)  28.6 us
    ppermute x4, starting transfers between devices, from_behind(): lax.ppermute(value, axis, [(source, source + steps) for source in range(l...  11.8 us
    ppermute x2, starting transfers between devices, padded(): lax.ppermute(lax.slice_in_dim(block, block.shape[dim] - width, None, axis...  7.75 us
    dot_general x3, matrix products, transform(): jnp.einsum('pbjk,bakl->pajl', inner, right_table, precision=lax.Precision...  5.59 us
    dynamic_slice x3, local copies, waits for them, and re-layouts, shards(): lax.dynamic_slice(second_ext, (anchor, spots[number, 0], spots[number, 1]...  5.44 us
    dot_general x3, matrix products, transform(): jnp.einsum('abjk,pbkl->pajl', left_table, fields, precision=lax.Precision...  4.83 us
    ppermute x2, waiting for transfers between devices, padded(): lax.ppermute(lax.slice_in_dim(block, 0, width, axis=dim), axis, backward)  4.34 us
  transfers between devices with their start and end apart: 8, of which 5 were waited for; matrix products, arithmetic and copies ran while one was open for 8% of the time, Pallas kernels for 0%

commit v1 on v0

v1 whole, which is shorter than its diff:
```python
import functools

import jax
import jax.numpy as jnp
import ml_dtypes
import numpy as np
from jax import lax
from jax.experimental import pallas as pl
from jax.experimental.pallas import tpu as pltpu
from jax.sharding import PartitionSpec as P

fresnel_rate = 200.0
ridge = 0.5
CHUNK = 32
F32 = jnp.float32
BF16 = jnp.bfloat16


def real_blocks(matrix):
    right = np.block([[matrix.real, matrix.imag], [-matrix.imag, matrix.real]])
    left = np.block([[matrix.real, -matrix.imag], [matrix.imag, matrix.real]])
    return right, left


def two_parts(table):
    high = table.astype(np.float32).astype(ml_dtypes.bfloat16)
    low = (table - high.astype(np.float64)).astype(ml_dtypes.bfloat16)
    return high, low


@functools.lru_cache(maxsize=None)
def tables(size):
    index = np.arange(size)
    inverse = np.exp(2j * np.pi * (np.outer(index, index) % size) / size) / np.sqrt(size)
    freq = ((index + size // 2) % size - size // 2) / size
    move = inverse @ np.diag(np.exp(1j * fresnel_rate * freq**2)) @ inverse.conj()
    out = []
    for matrix in (inverse, move):
        for table in real_blocks(matrix):
            out.extend(two_parts(table))
    return tuple(out)


def swap_pairs(count, first):
    pairs = []
    for low in range(first, count - 1, 2):
        pairs += [(low, low + 1), (low + 1, low)]
    return pairs


def swapped(value, axis, first):
    return lax.ppermute(value, axis, swap_pairs(lax.axis_size(axis), first))


def dot(a, b):
    return jnp.dot(a, b, preferred_element_type=F32)


def split(value):
    high = value.astype(BF16)
    return high, (value - high.astype(F32)).astype(BF16)


def place(waves, corners, out_first, out_second, out_middle, odd, window):
    half = window // 2

    def rows(base, lower, store):
        for start in range(0, half, CHUNK):
            at = pl.multiple_of(base + start, CHUNK)
            row = lax.broadcasted_iota(jnp.int32, (CHUNK, window), 0) + at
            col = lax.broadcasted_iota(jnp.int32, (CHUNK, window), 1)
            masks = []
            for r, c in corners:
                inside = (row < r) == (lower == 1)
                masks.append((inside & (col >= c), inside & (col < c)))
            for plane in range(len(waves)):
                left = right = None
                for number, (in_left, in_right) in enumerate(masks):
                    value = waves[plane][number, pl.ds(at, CHUNK), :]
                    a = jnp.where(in_left, value, 0.0)
                    b = jnp.where(in_right, value, 0.0)
                    left = a if left is None else left + a
                    right = b if right is None else right + b
                store(plane, start, left, right)

    def writer(ref, offset):
        def store(plane, start, left, right):
            ref[plane, offset + start : offset + start + CHUNK, :window] = left
            ref[plane, offset + start : offset + start + CHUNK, window:] = right

        return store

    rows((1 - odd) * half, 1 - odd, writer(out_first, 0))
    rows(odd * half, odd, writer(out_second, 0))
    rows(half, 0, writer(out_middle, 0))
    rows(0, 1, writer(out_middle, half))


def prepare(
    pos, residual, wave, probe, rt_hi, rt_lo, lt_hi, lt_lo,
    field, probes, first, second, middle,
    twice, inner_hi, inner_lo, outer, grads,
):
    window = probe.shape[-1]
    count = residual.shape[0]
    odd = lax.rem(lax.axis_index("gy"), 2)
    corners = [(pos[number, 0, 0], pos[number, 0, 1]) for number in range(count)]

    def rolled(value_at, corner, store):
        r, c = corner
        for start in range(0, window, CHUNK):
            value = pltpu.roll(value_at(start), c, 1)
            twice[start : start + CHUNK] = value
            twice[window + start : window + start + CHUNK] = value
        twice[2 * window :] = twice[:8]
        rest = lax.rem(window - r, 8)
        back = lax.rem(CHUNK + 8 - rest, CHUNK + 8)
        for start in range(0, window, CHUNK):
            value = twice[pl.ds(pl.multiple_of(window - r - rest + start, 8), CHUNK + 8), :]
            store(start, pltpu.roll(value, back, 0)[:CHUNK])

    for number in range(count):
        detector_re = residual[number, 0, 0]
        detector_im = residual[number, 0, 1]
        table_hi, table_lo = rt_hi[...], rt_lo[...]
        line = dot(detector_re, table_hi[:window]) + dot(detector_im, table_hi[window:])
        line += dot(detector_re, table_lo[:window]) + dot(detector_im, table_lo[window:])
        high, low = split(line)
        inner_hi[:window, number * window : (number + 1) * window] = high[:, :window]
        inner_hi[window:, number * window : (number + 1) * window] = high[:, window:]
        inner_lo[:window, number * window : (number + 1) * window] = low[:, :window]
        inner_lo[window:, number * window : (number + 1) * window] = low[:, window:]
    outer[...] = dot(lt_hi[...], inner_hi[...]) + dot(lt_lo[...], inner_hi[...]) + dot(lt_hi[...], inner_lo[...])

    for number, corner in enumerate(corners):
        for part in range(2):

            def from_outer(start):
                return outer[
                    part * window + start : part * window + start + CHUNK, number * window : (number + 1) * window
                ]

            def to_field(start, value):
                field[number, part, start : start + CHUNK] = value

            rolled(from_outer, corner, to_field)

            def from_probe(start):
                return probe[part, start : start + CHUNK]

            def to_probes(start, value):
                probes[number, part, start : start + CHUNK] = value

            rolled(from_probe, corner, to_probes)

        for part in range(2):

            def from_wave(start):
                return wave[number, 0, part, start : start + CHUNK].astype(F32)

            def to_grads(start, value):
                grads[part, number, start : start + CHUNK] = value

            rolled(from_wave, corner, to_grads)
        for start in range(0, window, CHUNK):
            rows = slice(start, start + CHUNK)
            wave_re, wave_im = grads[0, number, rows], grads[1, number, rows]
            field_re, field_im = field[number, 0, rows], field[number, 1, rows]
            grads[0, number, rows] = wave_re * field_re + wave_im * field_im
            grads[1, number, rows] = wave_re * field_im - wave_im * field_re
            probe_re, probe_im = probes[number, 0, rows], probes[number, 1, rows]
            grads[2, number, rows] = probe_re * probe_re + probe_im * probe_im
    place([grads.at[0], grads.at[1], grads.at[2]], corners, first, second, middle, odd, window)


def widen(second, from_first, from_second, first, second_out, middle):
    half = from_first.shape[-1]
    odd_x = lax.rem(lax.axis_index("gx"), 2)
    odd_y = lax.rem(lax.axis_index("gy"), 2)
    planes = second.shape[0]
    for plane in range(planes):
        middle[plane, :, half : 3 * half] = second[plane]
        middle[plane, :, pl.ds(pl.multiple_of((1 - odd_x) * 3 * half, half), half)] = from_first[plane]
        middle[plane, :, pl.ds(pl.multiple_of(odd_x * 3 * half, half), half)] = from_second[plane]
        first[plane] = middle[plane, pl.ds(pl.multiple_of((1 - odd_y) * half, half), half), :]
        second_out[plane] = middle[plane, pl.ds(pl.multiple_of(odd_y * half, half), half), :]


def propagate(
    pos, field, probes, middle_in, from_first, from_second, rm_hi, rm_lo, lm_hi, lm_lo,
    first, second, middle,
    chi_hi, chi_lo, inner_hi, inner_lo, outer, grads,
):
    window = field.shape[-1]
    half = window // 2
    count = field.shape[0]
    odd = lax.rem(lax.axis_index("gy"), 2)
    corners = [(pos[number, 0, 0], pos[number, 0, 1]) for number in range(count)]

    for start in range(0, window, CHUNK):
        rows = slice(start, start + CHUNK)
        row = lax.broadcasted_iota(jnp.int32, (CHUNK, window), 0) + start
        col = lax.broadcasted_iota(jnp.int32, (CHUNK, window), 1)
        upper, lower = [], []
        for part in range(2):
            if start < half:
                upper.append(jnp.where(odd == 1, from_first[part, rows], from_second[part, rows]))
                lower.append(middle_in[part, half + start : half + start + CHUNK])
            else:
                shifted = slice(start - half, start - half + CHUNK)
                upper.append(middle_in[part, shifted])
                lower.append(jnp.where(odd == 1, from_second[part, shifted], from_first[part, shifted]))
        for number, (r, c) in enumerate(corners):
            low_row, low_col = row < r, col < c
            patch = []
            for part in range(2):
                above = jnp.where(low_col, upper[part][:, window:], upper[part][:, :window])
                below = jnp.where(low_col, lower[part][:, window:], lower[part][:, :window])
                patch.append(jnp.where(low_row, below, above))
            field_re, field_im = field[number, 0, rows], field[number, 1, rows]
            at = slice(number * window + start, number * window + start + CHUNK)
            high, low = split(patch[0] * field_re + patch[1] * field_im)
            chi_hi[at, :window] = high
            chi_lo[at, :window] = low
            high, low = split(patch[0] * field_im - patch[1] * field_re)
            chi_hi[at, window:] = high
            chi_lo[at, window:] = low

    for number in range(count):
        rows = slice(number * window, (number + 1) * window)
        line = dot(chi_hi[rows], rm_hi[...]) + dot(chi_hi[rows], rm_lo[...]) + dot(chi_lo[rows], rm_hi[...])
        high, low = split(line)
        inner_hi[:window, rows] = high[:, :window]
        inner_hi[window:, rows] = high[:, window:]
        inner_lo[:window, rows] = low[:, :window]
        inner_lo[window:, rows] = low[:, window:]
    outer[...] = dot(lm_hi[...], inner_hi[...]) + dot(lm_lo[...], inner_hi[...]) + dot(lm_hi[...], inner_lo[...])

    for number in range(count):
        cols = slice(number * window, (number + 1) * window)
        for start in range(0, window, CHUNK):
            rows = slice(start, start + CHUNK)
            probe_re, probe_im = probes[number, 0, rows], probes[number, 1, rows]
            back_re = outer[start : start + CHUNK, cols]
            back_im = outer[window + start : window + start + CHUNK, cols]
            grads[0, number, rows] = probe_re * back_re + probe_im * back_im
            grads[1, number, rows] = probe_re * back_im - probe_im * back_re
    place([grads.at[0], grads.at[1]], corners, first, second, middle, odd, window)


def narrow(middle, from_first, from_second, first, second, centre):
    half = first.shape[-1]
    odd_x = lax.rem(lax.axis_index("gx"), 2)
    odd_y = lax.rem(lax.axis_index("gy"), 2)
    for plane in range(middle.shape[0]):
        for start in range(0, half, CHUNK):
            rows = slice(start, start + CHUNK)
            for received, base in ((from_first, (1 - odd_y) * half), (from_second, odd_y * half)):
                at = pl.ds(pl.multiple_of(base + start, CHUNK), CHUNK)
                total = middle[plane, at, :] + received[plane, rows]
                left, right = total[:, :half], total[:, 3 * half :]
                centre[plane, at, :] = total[:, half : 3 * half]
                first[plane, at, :] = jnp.where(odd_x == 1, left, right)
                second[plane, at, :] = jnp.where(odd_x == 1, right, left)


def joined(centre, from_first, from_second, plane, rows, odd_x):
    half = from_first.shape[-1]
    one, two = from_first[plane, rows], from_second[plane, rows]
    left = centre[plane, rows, :half] + jnp.where(odd_x == 1, one, two)
    right = centre[plane, rows, half:] + jnp.where(odd_x == 1, two, one)
    return left, right


def update(object_field, centre2, first2, second2, centre1, first1, second1, out):
    half = first2.shape[-1]
    window = centre2.shape[-1]
    odd_x = lax.rem(lax.axis_index("gx"), 2)
    for start in range(0, window, CHUNK):
        rows = slice(start, start + CHUNK)
        light = joined(centre2, first2, second2, 2, rows, odd_x)
        scale = [1.0 / (value + ridge) for value in light]
        for number, refs in enumerate(((centre1, first1, second1), (centre2, first2, second2))):
            for part in range(2):
                sides = joined(*refs, part, rows, odd_x)
                for side, cols in enumerate((slice(0, half), slice(half, None))):
                    out[number, part, rows, cols] = object_field[number, part, rows, cols] - sides[side] * scale[side]


VMEM = pl.BlockSpec(memory_space=pltpu.VMEM)
SMEM = pl.BlockSpec(memory_space=pltpu.SMEM)


def call(body, outs, in_specs, args, scratch=(), flops=0, name=None):
    moved = sum(x.size * x.dtype.itemsize for x in args) + sum(4 * int(np.prod(s)) for s in outs)
    return pl.pallas_call(
        body,
        out_shape=[jax.ShapeDtypeStruct(shape, F32) for shape in outs],
        in_specs=in_specs,
        out_specs=[VMEM] * len(outs),
        scratch_shapes=list(scratch),
        compiler_params=pltpu.CompilerParams(vmem_limit_bytes=40 * 1024 * 1024),
        cost_estimate=pl.CostEstimate(flops=flops, bytes_accessed=moved, transcendentals=0),
        name=name,
    )(*args)


def shards(object_field, probe, positions, residual, saved_wave):
    window = probe.shape[-1]
    half = window // 2
    count = positions.shape[0]
    odd_x = lax.rem(lax.axis_index("gx"), 2)
    rt_hi, rt_lo, lt_hi, lt_lo, rm_hi, rm_lo, lm_hi, lm_lo = (jnp.asarray(t) for t in tables(window))

    second = object_field[1]
    left, right = second[:, :, :half], second[:, :, half:]
    halo_first = swapped(jnp.where(odd_x == 1, left, right), "gx", 0)
    halo_second = swapped(jnp.where(odd_x == 1, right, left), "gx", 1)

    def pieces(planes):
        return [(planes, half, 2 * window), (planes, half, 2 * window), (planes, window, 2 * window)]

    def frame_scratch(planes):
        wide = (2 * window, count * window)
        return [
            pltpu.VMEM(wide, BF16),
            pltpu.VMEM(wide, BF16),
            pltpu.VMEM(wide, F32),
            pltpu.VMEM((planes, count, window, window), F32),
        ]

    fields, probes, up2, down2, middle2 = call(
        prepare,
        [(count, 2, window, window)] * 2 + pieces(3),
        [SMEM] + [VMEM] * 7,
        (positions, residual, saved_wave, probe, rt_hi, rt_lo, lt_hi, lt_lo),
        [pltpu.VMEM((2 * window + 8, window), F32)] + frame_scratch(3),
        flops=count * 5 * 2 * 4 * window**3,
        name="prepare",
    )
    from_up2 = swapped(up2, "gy", 0)
    from_down2 = swapped(down2, "gy", 1)

    up0, down0, wide0 = call(
        widen,
        pieces(2),
        [VMEM] * 3,
        (second, halo_first, halo_second),
        name="widen",
    )
    from_up0 = swapped(up0, "gy", 0)
    from_down0 = swapped(down0, "gy", 1)

    def strips(planes):
        return [(planes, window, half), (planes, window, half), (planes, window, window)]

    first2, second2, centre2 = call(
        narrow, strips(3), [VMEM] * 3, (middle2, from_up2, from_down2), name="narrow2"
    )
    got_first2 = swapped(first2, "gx", 0)
    got_second2 = swapped(second2, "gx", 1)

    up1, down1, middle1 = call(
        propagate,
        pieces(2),
        [SMEM] + [VMEM] * 9,
        (positions, fields, probes, wide0, from_up0, from_down0, rm_hi, rm_lo, lm_hi, lm_lo),
        [pltpu.VMEM((count * window, 2 * window), BF16)] * 2 + frame_scratch(2),
        flops=count * 6 * 2 * 4 * window**3,
        name="propagate",
    )
    from_up1 = swapped(up1, "gy", 0)
    from_down1 = swapped(down1, "gy", 1)
    first1, second1, centre1 = call(
        narrow, strips(2), [VMEM] * 3, (middle1, from_up1, from_down1), name="narrow1"
    )
    got_first1 = swapped(first1, "gx", 0)
    got_second1 = swapped(second1, "gx", 1)
    (new_object,) = call(
        update,
        [object_field.shape],
        [VMEM] * 7,
        (object_field, centre2, got_first2, got_second2, centre1, got_first1, got_second1),
        name="update",
    )
    return new_object


def solution(mesh):
    placed = (
        P(None, None, "gy", "gx"),
        P(),
        P("gy", "gx", None),
        P("gy", "gx", None, None, None),
        P("gy", "gx", None, None, None),
    )
    return jax.shard_map(
        shards, mesh=mesh, in_specs=placed, out_specs=P(None, None, "gy", "gx"), check_vma=False
    )
```

time: 153 us -> 71.4 us (0.47)
  local copies, waits for them, and re-layouts: 47.9 us -> 2.32 us
  other arithmetic: 14.9 us -> 0.04 us
  matrix products: 10.4 us -> 0 us
  Pallas kernels: 0 us -> 9.52 us
  between operations: 8.11 us -> 0.3 us
  waiting for transfers between devices: 45.4 us -> 38.1 us
  starting transfers between devices: 23.7 us -> 19.9 us
    dynamic_update_slice x2 -> x0, local copies, waits for them, and re-layouts: 28.6 us -> none  [shards(): summed = lax.dynamic_update_slice(summed, current + planes[number], corner)]
    dot_general x6 -> x0, matrix products: 10.4 us -> none  [the longest x3 5.59 us: transform(): jnp.einsum('pbjk,bakl->pajl', inner, right_table, precision=lax.Precision...]
    pallas_call x0 -> x6, Pallas kernels: none -> 9.52 us  [call(): pl.pallas_call(body, out_shape=[jax.ShapeDtypeStruct(shape, F32) for shap...]
    ppermute x8 -> x12, waiting for transfers between devices: 45.4 us -> 38.1 us  [swapped(): return lax.ppermute(value, axis, swap_pairs(lax.axis_size(axis), first))]
    dynamic_slice x3 -> x0, local copies, waits for them, and re-layouts: 5.44 us -> none  [shards(): lax.dynamic_slice(second_ext, (anchor, spots[number, 0], spots[number, 1]...]
    add x6 -> x0, other arithmetic: 4.7 us -> none  [the longest x1 2.38 us: shards(): summed = lax.dynamic_update_slice(summed, current + planes[number], corner)]
    slice x6 -> x0, local copies, waits for them, and re-layouts: 3.99 us -> none  [the longest x1 2.05 us: shards(): summed[:, 3 * margin:, :]]
    ppermute x8 -> x12, starting transfers between devices: 23.7 us -> 19.9 us  [swapped(): return lax.ppermute(value, axis, swap_pairs(lax.axis_size(axis), first))]
  transfers between devices with their start and end apart: 8 -> 12, of which waited for: 5 -> 8; matrix products, arithmetic and copies ran while one was open for 8% -> 0% of each run, Pallas kernels for 0% -> 12%
where the time goes in v1:
time: 71.4 us; the launch traced here: 70.2 us
  waiting for transfers between devices  38.1 us (53%)
  starting transfers between devices  19.9 us (28%)
  Pallas kernels  9.52 us (13%)
  local copies, waits for them, and re-layouts  2.32 us (3%)
    ppermute x12, waiting for transfers between devices, swapped(): return lax.ppermute(value, axis, swap_pairs(lax.axis_size(axis), first))  38.1 us
    ppermute x12, starting transfers between devices, swapped(): return lax.ppermute(value, axis, swap_pairs(lax.axis_size(axis), first))  19.9 us
    pallas_call x6, Pallas kernels, call(): pl.pallas_call(body, out_shape=[jax.ShapeDtypeStruct(shape, F32) for shap...  9.52 us
  transfers between devices with their start and end apart: 12, of which 8 were waited for; matrix products, arithmetic and copies ran while one was open for 0% of the time, Pallas kernels for 12%

profile of v1, /device:TPU:11, one launch (start us, length us, event | category | flops | bytes accessed | tf_op | source)
XLA Modules:
  0.0 70.2 jit_solution(8134408815484610237)
XLA Ops:
  0.0 0.0 copy-start.5
  0.0 0.0 copy-start.6
  0.0 0.0 copy-start.7
  0.0 0.0 copy-start.8
  0.0 0.0 copy-start.9
  0.0 0.0 copy-start.10
  0.0 1.2 %slice_bitcast_fusion.second = f32[2,256,256]{2,1,0:T(8,128)S(1)} fusion(f32[2,2,256,256]{3,2,1,0:T(8,128)} %object_field.1), kind=kLoop, calls=%fused_computation | loop fusion | bytes 1048576 | tf_op jit(solution)/shard_map/squeeze | solution.py:315
  1.3 0.0 copy-start.11
  1.3 0.3 collective-permute-start.4
  1.7 4.1 %collective-permute-start.5 = (f32[2,256,128]{2,1,0:T(8,128)S(1)}, f32[2,256,128]{2,1,0:T(8,128)S(1)}, u32[]{:S(2)}, u32[]{:S(2)}) collective-permute-start(f32[2,256,128]{2,1,0:T(8,128)S(1)} %get-tuple-element.39), channel_id=1, source_target_pairs={{8,16},{16,8},{9,17},{17,9},{10,18},{18,10},{11,19},{19,11},{12,20... | collective-permute-start | bytes 786440 | tf_op jit(solution)/shard_map/ppermute | solution.py:52
  5.7 2.8 %collective-permute-done.4.from_first = f32[2,256,128]{2,1,0:T(8,128)S(1)} collective-permute-done((f32[2,256,128]{2,1,0:T(8,128)S(1)}, f32[2,256,128]{2,1,0:T(8,128)S(1)}, u32[]{:S(2)}, u32[]{:S(2)}) %collective-permute-start.4) | collective-permute-done | bytes 262176 | tf_op jit(solution)/shard_map/ppermute | solution.py:52
  8.6 6.6 %collective-permute-done.5.from_second = f32[2,256,128]{2,1,0:T(8,128)S(1)} collective-permute-done((f32[2,256,128]{2,1,0:T(8,128)S(1)}, f32[2,256,128]{2,1,0:T(8,128)S(1)}, u32[]{:S(2)}, u32[]{:S(2)}) %collective-permute-start.5) | collective-permute-done | bytes 262176 | tf_op jit(solution)/shard_map/ppermute | solution.py:52
  15.2 0.2 widen.1
  15.3 1.6 %collective-permute-start.6 = (f32[2,128,512]{2,1,0:T(8,128)S(1)}, f32[2,128,512]{2,1,0:T(8,128)S(1)}, u32[]{:S(2)}, u32[]{:S(2)}) collective-permute-start(f32[2,128,512]{2,1,0:T(8,128)S(1)} %get-tuple-element.31), channel_id=1, source_target_pairs={{0,1},{1,0},{2,3},{3,2},{4,5},{5,4},{6,7},{7,6},{8,9},{9,8},{10,11... | collective-permute-start | bytes 1572872 | tf_op jit(solution)/shard_map/ppermute | solution.py:52
  16.9 0.0 copy-start.1
  16.9 0.0 copy-start.2
  16.9 0.0 copy-start.3
  17.0 0.0 copy-start.4
  17.0 3.3 %collective-permute-start.7 = (f32[2,128,512]{2,1,0:T(8,128)S(1)}, f32[2,128,512]{2,1,0:T(8,128)S(1)}, u32[]{:S(2)}, u32[]{:S(2)}) collective-permute-start(f32[2,128,512]{2,1,0:T(8,128)S(1)} %get-tuple-element.32), channel_id=1, source_target_pairs={{1,2},{2,1},{3,4},{4,3},{5,6},{6,5},{9,10},{10,9},{11,12},{12,11},... | collective-permute-start | bytes 1572872 | tf_op jit(solution)/shard_map/ppermute | solution.py:52
  20.2 0.0 copy-done.5
  20.2 0.0 copy-done.6
  20.3 0.0 copy-done.7
  20.3 0.0 copy-done.8
  20.3 0.0 copy-done.9
  20.3 0.0 copy-done.10
  20.3 0.0 copy-done.11
  20.3 0.0 copy-start.12
  20.3 1.0 %copy-done.12 = bf16[512,512]{1,0:T(8,128)(2,1)S(1)} copy-done((bf16[512,512]{1,0:T(8,128)(2,1)S(1)}, bf16[512,512]{1,0:T(8,128)(2,1)}, u32[]{:S(2)}) %copy-start.12) | copy-done | bytes 524312
  21.4 4.4 %prepare.1 = (f32[2,2,256,256]{3,2,1,0:T(8,128)S(1)}, f32[2,2,256,256]{3,2,1,0:T(8,128)S(1)}, f32[3,128,512]{2,1,0:T(8,128)S(1)}, f32[3,128,512]{2,1,0:T(8,128)S(1)}, f32[3,256,512]{2,1,0:T(8,128)S(1)}) custom-call(s32[2,1,2]{2,1,0:T(1,128)S(1)} %copy-done.5, bf16[2,1,2,256,256]{4,3,2,1,0:T(8,128)(2,1)S(1)} %copy-done.6, ...), custom_call_target="tpu_custom_call" | custom-call | flops 1342177280 | bytes 8912912 | tf_op jit(solution)/shard_map/prepare/pallas_call | solution.py:296
  25.8 0.1 collective-permute-start
  25.9 3.6 %collective-permute-start.1 = (f32[3,128,512]{2,1,0:T(8,128)S(1)}, f32[3,128,512]{2,1,0:T(8,128)S(1)}, u32[]{:S(2)}, u32[]{:S(2)}) collective-permute-start(f32[3,128,512]{2,1,0:T(8,128)S(1)} %get-tuple-element.24), channel_id=1, source_target_pairs={{1,2},{2,1},{3,4},{4,3},{5,6},{6,5},{9,10},{10,9},{11,12},{12,11},... | collective-permute-start | bytes 2359304 | tf_op jit(solution)/shard_map/ppermute | solution.py:52
  29.5 0.0 collective-permute-done.6.from_first
  29.5 0.0 collective-permute-done.7.from_second
  29.5 0.0 copy-done.1
  29.5 0.0 copy-done.2
  29.5 0.0 copy-done.3
  29.5 0.0 copy-done.4
  29.5 3.4 %propagate.1 = (f32[2,128,512]{2,1,0:T(8,128)S(1)}, f32[2,128,512]{2,1,0:T(8,128)S(1)}, f32[2,256,512]{2,1,0:T(8,128)S(1)}) custom-call(s32[2,1,2]{2,1,0:T(1,128)S(1)} %copy-done.5, f32[2,2,256,256]{3,2,1,0:T(8,128)S(1)} %get-tuple-element.28.field, f32[2,2,256,256]{3,2,1,0:T(8,128)S(1)} %get-tuple-element.29.probes, ...), custom_call_target="tpu_custom_call" | custom-call | flops 1610612736 | bytes 8388624 | tf_op jit(solution)/shard_map/propagate/pallas_call | solution.py:296
  32.9 0.1 collective-permute-start.8
  33.0 2.4 %collective-permute-start.9 = (f32[2,128,512]{2,1,0:T(8,128)S(1)}, f32[2,128,512]{2,1,0:T(8,128)S(1)}, u32[]{:S(2)}, u32[]{:S(2)}) collective-permute-start(f32[2,128,512]{2,1,0:T(8,128)S(1)} %get-tuple-element.35), channel_id=1, source_target_pairs={{1,2},{2,1},{3,4},{4,3},{5,6},{6,5},{9,10},{10,9},{11,12},{12,11},... | collective-permute-start | bytes 1572872 | tf_op jit(solution)/shard_map/ppermute | solution.py:52
  35.4 0.0 collective-permute-done.from_first
  35.4 4.0 %collective-permute-done.1.from_second = f32[3,128,512]{2,1,0:T(8,128)S(1)} collective-permute-done((f32[3,128,512]{2,1,0:T(8,128)S(1)}, f32[3,128,512]{2,1,0:T(8,128)S(1)}, u32[]{:S(2)}, u32[]{:S(2)}) %collective-permute-start.1) | collective-permute-done | bytes 786464 | tf_op jit(solution)/shard_map/ppermute | solution.py:52
  39.5 0.2 narrow2.1
  39.7 0.0 copy-start
  39.7 0.1 collective-permute-start.2
  39.8 2.2 %collective-permute-start.3 = (f32[3,256,128]{2,1,0:T(8,128)S(1)}, f32[3,256,128]{2,1,0:T(8,128)S(1)}, u32[]{:S(2)}, u32[]{:S(2)}) collective-permute-start(f32[3,256,128]{2,1,0:T(8,128)S(1)} %get-tuple-element.27), channel_id=1, source_target_pairs={{8,16},{16,8},{9,17},{17,9},{10,18},{18,10},{11,19},{19,11},{12,20... | collective-permute-start | bytes 1179656 | tf_op jit(solution)/shard_map/ppermute | solution.py:52
  42.0 0.0 collective-permute-done.8.from_first
  42.0 3.1 %collective-permute-done.9.from_second = f32[2,128,512]{2,1,0:T(8,128)S(1)} collective-permute-done((f32[2,128,512]{2,1,0:T(8,128)S(1)}, f32[2,128,512]{2,1,0:T(8,128)S(1)}, u32[]{:S(2)}, u32[]{:S(2)}) %collective-permute-start.9) | collective-permute-done | bytes 524320 | tf_op jit(solution)/shard_map/ppermute | solution.py:52
  45.1 0.1 narrow1.1
  45.2 0.1 collective-permute-start.10
  45.3 2.1 %collective-permute-start.11 = (f32[2,256,128]{2,1,0:T(8,128)S(1)}, f32[2,256,128]{2,1,0:T(8,128)S(1)}, u32[]{:S(2)}, u32[]{:S(2)}) collective-permute-start(f32[2,256,128]{2,1,0:T(8,128)S(1)} %get-tuple-element.38), channel_id=1, source_target_pairs={{8,16},{16,8},{9,17},{17,9},{10,18},{18,10},{11,19},{19,11},{12,20... | collective-permute-start | bytes 786440 | tf_op jit(solution)/shard_map/ppermute | solution.py:52
  47.4 2.9 %collective-permute-done.2.first2 = f32[3,256,128]{2,1,0:T(8,128)S(1)} collective-permute-done((f32[3,256,128]{2,1,0:T(8,128)S(1)}, f32[3,256,128]{2,1,0:T(8,128)S(1)}, u32[]{:S(2)}, u32[]{:S(2)}) %collective-permute-start.2) | collective-permute-done | bytes 393248 | tf_op jit(solution)/shard_map/ppermute | solution.py:52
  50.3 7.5 %collective-permute-done.3.second2 = f32[3,256,128]{2,1,0:T(8,128)S(1)} collective-permute-done((f32[3,256,128]{2,1,0:T(8,128)S(1)}, f32[3,256,128]{2,1,0:T(8,128)S(1)}, u32[]{:S(2)}, u32[]{:S(2)}) %collective-permute-start.3) | collective-permute-done | bytes 393248 | tf_op jit(solution)/shard_map/ppermute | solution.py:52
  57.8 4.7 %collective-permute-done.10.first1 = f32[2,256,128]{2,1,0:T(8,128)S(1)} collective-permute-done((f32[2,256,128]{2,1,0:T(8,128)S(1)}, f32[2,256,128]{2,1,0:T(8,128)S(1)}, u32[]{:S(2)}, u32[]{:S(2)}) %collective-permute-start.10) | collective-permute-done | bytes 262176 | tf_op jit(solution)/shard_map/ppermute | solution.py:52
  62.5 6.5 %collective-permute-done.11.second1 = f32[2,256,128]{2,1,0:T(8,128)S(1)} collective-permute-done((f32[2,256,128]{2,1,0:T(8,128)S(1)}, f32[2,256,128]{2,1,0:T(8,128)S(1)}, u32[]{:S(2)}, u32[]{:S(2)}) %collective-permute-start.11) | collective-permute-done | bytes 262176 | tf_op jit(solution)/shard_map/ppermute | solution.py:52
  69.0 0.0 copy-done
  69.0 1.2 %update.1 = f32[2,2,256,256]{3,2,1,0:T(8,128)} custom-call(f32[2,2,256,256]{3,2,1,0:T(8,128)S(1)} %copy-done, f32[3,256,256]{2,1,0:T(8,128)S(1)} %get-tuple-element.25.centre2, f32[3,256,128]{2,1,0:T(8,128)S(1)} %collective-permute-done.2.first2, f32[3,256,128]{2,1,0:T(8,128)S(1)} %collective-permute-done.3.second2, ...), custom_call_target="tpu_custom_call" | custom-call | bytes 4718592 | tf_op jit(solution)/shard_map/update/pallas_call | solution.py:296
  (1 shorter events, 0.0 us)
Async XLA Ops:
  0.0 20.2 %copy-start.5 = (s32[2,1,2]{2,1,0:T(1,128)S(1)}, s32[2,1,2]{2,1,0:T(1,128)}, u32[]{:S(2)}) copy-start(s32[2,1,2]{2,1,0:T(1,128)} %pos.3) | copy-start | bytes 52
  0.0 20.2 %copy-start.6 = (bf16[2,1,2,256,256]{4,3,2,1,0:T(8,128)(2,1)S(1)}, bf16[2,1,2,256,256]{4,3,2,1,0:T(8,128)(2,1)}, u32[]{:S(2)}) copy-start(bf16[2,1,2,256,256]{4,3,2,1,0:T(8,128)(2,1)} %residual.1) | copy-start | bytes 1572868
  0.0 20.3 %copy-start.7 = (bf16[2,1,2,256,256]{4,3,2,1,0:T(8,128)(2,1)S(1)}, bf16[2,1,2,256,256]{4,3,2,1,0:T(8,128)(2,1)}, u32[]{:S(2)}) copy-start(bf16[2,1,2,256,256]{4,3,2,1,0:T(8,128)(2,1)} %wave.1) | copy-start | bytes 1572868
  0.0 20.3 %copy-start.8 = (f32[2,256,256]{2,1,0:T(8,128)S(1)}, f32[2,256,256]{2,1,0:T(8,128)}, u32[]{:S(2)}) copy-start(f32[2,256,256]{2,1,0:T(8,128)} %probe.1) | copy-start | bytes 1572868
  0.0 20.3 %copy-start.9 = (bf16[512,512]{1,0:T(8,128)(2,1)S(1)}, bf16[512,512]{1,0:T(8,128)(2,1)}, u32[]{:S(2)}) copy-start(bf16[512,512]{1,0:T(8,128)(2,1)} %constant.27.clone.rt_hi) | copy-start | bytes 1572868
  0.0 20.3 %copy-start.10 = (bf16[512,512]{1,0:T(8,128)(2,1)S(1)}, bf16[512,512]{1,0:T(8,128)(2,1)}, u32[]{:S(2)}) copy-start(bf16[512,512]{1,0:T(8,128)(2,1)} %constant.28.clone.rt_lo) | copy-start | bytes 1572868
  1.3 19.0 %copy-start.11 = (bf16[512,512]{1,0:T(8,128)(2,1)S(1)}, bf16[512,512]{1,0:T(8,128)(2,1)}, u32[]{:S(2)}) copy-start(bf16[512,512]{1,0:T(8,128)(2,1)} %constant.29.clone.lt_hi) | copy-start | bytes 1572868
  1.3 7.2 %collective-permute-start.4 = (f32[2,256,128]{2,1,0:T(8,128)S(1)}, f32[2,256,128]{2,1,0:T(8,128)S(1)}, u32[]{:S(2)}, u32[]{:S(2)}) collective-permute-start(f32[2,256,128]{2,1,0:T(8,128)S(1)} %get-tuple-element.40), channel_id=1, source_target_pairs={{0,8},{8,0},{16,24},{24,16},{1,9},{9,1},{17,25},{25,17},{2,10},{10... | collective-permute-start | bytes 786440 | tf_op jit(solution)/shard_map/ppermute | solution.py:52
  1.7 13.5 %collective-permute-start.5 = (f32[2,256,128]{2,1,0:T(8,128)S(1)}, f32[2,256,128]{2,1,0:T(8,128)S(1)}, u32[]{:S(2)}, u32[]{:S(2)}) collective-permute-start(f32[2,256,128]{2,1,0:T(8,128)S(1)} %get-tuple-element.39), channel_id=1, source_target_pairs={{8,16},{16,8},{9,17},{17,9},{10,18},{18,10},{11,19},{19,11},{12,20... | collective-permute-start | bytes 786440 | tf_op jit(solution)/shard_map/ppermute | solution.py:52
  15.3 14.1 %collective-permute-start.6 = (f32[2,128,512]{2,1,0:T(8,128)S(1)}, f32[2,128,512]{2,1,0:T(8,128)S(1)}, u32[]{:S(2)}, u32[]{:S(2)}) collective-permute-start(f32[2,128,512]{2,1,0:T(8,128)S(1)} %get-tuple-element.31), channel_id=1, source_target_pairs={{0,1},{1,0},{2,3},{3,2},{4,5},{5,4},{6,7},{7,6},{8,9},{9,8},{10,11... | collective-permute-start | bytes 1572872 | tf_op jit(solution)/shard_map/ppermute | solution.py:52
  16.9 12.5 %copy-start.1 = (bf16[512,512]{1,0:T(8,128)(2,1)S(1)}, bf16[512,512]{1,0:T(8,128)(2,1)}, u32[]{:S(2)}) copy-start(bf16[512,512]{1,0:T(8,128)(2,1)} %constant.31.clone.rm_hi) | copy-start | bytes 1572868
  16.9 12.5 %copy-start.2 = (bf16[512,512]{1,0:T(8,128)(2,1)S(1)}, bf16[512,512]{1,0:T(8,128)(2,1)}, u32[]{:S(2)}) copy-start(bf16[512,512]{1,0:T(8,128)(2,1)} %constant.32.clone.rm_lo) | copy-start | bytes 1572868
  16.9 12.6 %copy-start.3 = (bf16[512,512]{1,0:T(8,128)(2,1)S(1)}, bf16[512,512]{1,0:T(8,128)(2,1)}, u32[]{:S(2)}) copy-start(bf16[512,512]{1,0:T(8,128)(2,1)} %constant.33.clone.lm_hi) | copy-start | bytes 1572868
  17.0 12.6 %copy-start.4 = (bf16[512,512]{1,0:T(8,128)(2,1)S(1)}, bf16[512,512]{1,0:T(8,128)(2,1)}, u32[]{:S(2)}) copy-start(bf16[512,512]{1,0:T(8,128)(2,1)} %constant.34.clone.lm_lo) | copy-start | bytes 1572868
  17.0 12.5 %collective-permute-start.7 = (f32[2,128,512]{2,1,0:T(8,128)S(1)}, f32[2,128,512]{2,1,0:T(8,128)S(1)}, u32[]{:S(2)}, u32[]{:S(2)}) collective-permute-start(f32[2,128,512]{2,1,0:T(8,128)S(1)} %get-tuple-element.32), channel_id=1, source_target_pairs={{1,2},{2,1},{3,4},{4,3},{5,6},{6,5},{9,10},{10,9},{11,12},{12,11},... | collective-permute-start | bytes 1572872 | tf_op jit(solution)/shard_map/ppermute | solution.py:52
  20.3 1.0 %copy-start.12 = (bf16[512,512]{1,0:T(8,128)(2,1)S(1)}, bf16[512,512]{1,0:T(8,128)(2,1)}, u32[]{:S(2)}) copy-start(bf16[512,512]{1,0:T(8,128)(2,1)} %constant.30.clone.lt_lo) | copy-start | bytes 1572868
  25.8 9.6 %collective-permute-start = (f32[3,128,512]{2,1,0:T(8,128)S(1)}, f32[3,128,512]{2,1,0:T(8,128)S(1)}, u32[]{:S(2)}, u32[]{:S(2)}) collective-permute-start(f32[3,128,512]{2,1,0:T(8,128)S(1)} %get-tuple-element.23), channel_id=1, source_target_pairs={{0,1},{1,0},{2,3},{3,2},{4,5},{5,4},{6,7},{7,6},{8,9},{9,8},{10,11... | collective-permute-start | bytes 2359304 | tf_op jit(solution)/shard_map/ppermute | solution.py:52
  25.9 13.6 %collective-permute-start.1 = (f32[3,128,512]{2,1,0:T(8,128)S(1)}, f32[3,128,512]{2,1,0:T(8,128)S(1)}, u32[]{:S(2)}, u32[]{:S(2)}) collective-permute-start(f32[3,128,512]{2,1,0:T(8,128)S(1)} %get-tuple-element.24), channel_id=1, source_target_pairs={{1,2},{2,1},{3,4},{4,3},{5,6},{6,5},{9,10},{10,9},{11,12},{12,11},... | collective-permute-start | bytes 2359304 | tf_op jit(solution)/shard_map/ppermute | solution.py:52
  32.9 9.1 %collective-permute-start.8 = (f32[2,128,512]{2,1,0:T(8,128)S(1)}, f32[2,128,512]{2,1,0:T(8,128)S(1)}, u32[]{:S(2)}, u32[]{:S(2)}) collective-permute-start(f32[2,128,512]{2,1,0:T(8,128)S(1)} %get-tuple-element.34), channel_id=1, source_target_pairs={{0,1},{1,0},{2,3},{3,2},{4,5},{5,4},{6,7},{7,6},{8,9},{9,8},{10,11... | collective-permute-start | bytes 1572872 | tf_op jit(solution)/shard_map/ppermute | solution.py:52
  33.0 12.1 %collective-permute-start.9 = (f32[2,128,512]{2,1,0:T(8,128)S(1)}, f32[2,128,512]{2,1,0:T(8,128)S(1)}, u32[]{:S(2)}, u32[]{:S(2)}) collective-permute-start(f32[2,128,512]{2,1,0:T(8,128)S(1)} %get-tuple-element.35), channel_id=1, source_target_pairs={{1,2},{2,1},{3,4},{4,3},{5,6},{6,5},{9,10},{10,9},{11,12},{12,11},... | collective-permute-start | bytes 1572872 | tf_op jit(solution)/shard_map/ppermute | solution.py:52
  39.7 29.3 %copy-start = (f32[2,2,256,256]{3,2,1,0:T(8,128)S(1)}, f32[2,2,256,256]{3,2,1,0:T(8,128)}, u32[]{:S(2)}) copy-start(f32[2,2,256,256]{3,2,1,0:T(8,128)} %object_field.1) | copy-start | bytes 3145732
  39.7 10.6 %collective-permute-start.2 = (f32[3,256,128]{2,1,0:T(8,128)S(1)}, f32[3,256,128]{2,1,0:T(8,128)S(1)}, u32[]{:S(2)}, u32[]{:S(2)}) collective-permute-start(f32[3,256,128]{2,1,0:T(8,128)S(1)} %get-tuple-element.26), channel_id=1, source_target_pairs={{0,8},{8,0},{16,24},{24,16},{1,9},{9,1},{17,25},{25,17},{2,10},{10... | collective-permute-start | bytes 1179656 | tf_op jit(solution)/shard_map/ppermute | solution.py:52
  39.8 18.0 %collective-permute-start.3 = (f32[3,256,128]{2,1,0:T(8,128)S(1)}, f32[3,256,128]{2,1,0:T(8,128)S(1)}, u32[]{:S(2)}, u32[]{:S(2)}) collective-permute-start(f32[3,256,128]{2,1,0:T(8,128)S(1)} %get-tuple-element.27), channel_id=1, source_target_pairs={{8,16},{16,8},{9,17},{17,9},{10,18},{18,10},{11,19},{19,11},{12,20... | collective-permute-start | bytes 1179656 | tf_op jit(solution)/shard_map/ppermute | solution.py:52
  45.2 17.2 %collective-permute-start.10 = (f32[2,256,128]{2,1,0:T(8,128)S(1)}, f32[2,256,128]{2,1,0:T(8,128)S(1)}, u32[]{:S(2)}, u32[]{:S(2)}) collective-permute-start(f32[2,256,128]{2,1,0:T(8,128)S(1)} %get-tuple-element.37), channel_id=1, source_target_pairs={{0,8},{8,0},{16,24},{24,16},{1,9},{9,1},{17,25},{25,17},{2,10},{10... | collective-permute-start | bytes 786440 | tf_op jit(solution)/shard_map/ppermute | solution.py:52
  45.3 23.7 %collective-permute-start.11 = (f32[2,256,128]{2,1,0:T(8,128)S(1)}, f32[2,256,128]{2,1,0:T(8,128)S(1)}, u32[]{:S(2)}, u32[]{:S(2)}) collective-permute-start(f32[2,256,128]{2,1,0:T(8,128)S(1)} %get-tuple-element.38), channel_id=1, source_target_pairs={{8,16},{16,8},{9,17},{17,9},{10,18},{18,10},{11,19},{19,11},{12,20... | collective-permute-start | bytes 786440 | tf_op jit(solution)/shard_map/ppermute | solution.py:52

commit v2 on v1

v2 whole, which is shorter than its diff:
```python
import functools

import jax
import jax.numpy as jnp
import ml_dtypes
import numpy as np
from jax import lax
from jax.experimental import pallas as pl
from jax.experimental.pallas import tpu as pltpu
from jax.sharding import PartitionSpec as P

fresnel_rate = 200.0
ridge = 0.5
CHUNK = 32
F32 = jnp.float32
BF16 = jnp.bfloat16


def two_parts(table):
    high = table.astype(np.float32).astype(ml_dtypes.bfloat16)
    low = (table - high.astype(np.float64)).astype(ml_dtypes.bfloat16)
    return high, low


@functools.lru_cache(maxsize=None)
def tables(size):
    index = np.arange(size)
    inverse = np.exp(2j * np.pi * (np.outer(index, index) % size) / size) / np.sqrt(size)
    freq = ((index + size // 2) % size - size // 2) / size
    move = inverse @ np.diag(np.exp(1j * fresnel_rate * freq**2)) @ inverse.conj()
    out = []
    for matrix in (inverse, move):
        out.extend(two_parts(np.concatenate([matrix.real, matrix.imag], axis=1)))
    return tuple(out)


def swap_pairs(count, first):
    pairs = []
    for low in range(first, count - 1, 2):
        pairs += [(low, low + 1), (low + 1, low)]
    return pairs


def swapped(value, axis, first):
    return lax.ppermute(value, axis, swap_pairs(lax.axis_size(axis), first))


def dot(a, b):
    return jnp.dot(a, b, preferred_element_type=F32)


def split(value):
    high = value.astype(BF16)
    return high, (value - high.astype(F32)).astype(BF16)


def place(waves, corners, out_first, out_second, out_middle, odd, window):
    half = window // 2

    def rows(base, lower, store):
        for start in range(0, half, CHUNK):
            at = pl.multiple_of(base + start, CHUNK)
            row = lax.broadcasted_iota(jnp.int32, (CHUNK, window), 0) + at
            col = lax.broadcasted_iota(jnp.int32, (CHUNK, window), 1)
            masks = []
            for r, c in corners:
                inside = (row < r) == (lower == 1)
                masks.append((inside & (col >= c), inside & (col < c)))
            for plane in range(len(waves)):
                left = right = None
                for number, (in_left, in_right) in enumerate(masks):
                    value = waves[plane][number, pl.ds(at, CHUNK), :]
                    a = jnp.where(in_left, value, 0.0)
                    b = jnp.where(in_right, value, 0.0)
                    left = a if left is None else left + a
                    right = b if right is None else right + b
                store(plane, start, left, right)

    def writer(ref, offset):
        def store(plane, start, left, right):
            ref[plane, offset + start : offset + start + CHUNK, :window] = left
            ref[plane, offset + start : offset + start + CHUNK, window:] = right

        return store

    rows((1 - odd) * half, 1 - odd, writer(out_first, 0))
    rows(odd * half, odd, writer(out_second, 0))
    rows(half, 0, writer(out_middle, 0))
    rows(0, 1, writer(out_middle, half))


def from_right(rows_re, rows_im, high, low, passes):
    window = high.shape[0]
    sums = []
    for rows in (rows_re, rows_im):
        total = dot(rows[0], high[...]) + dot(rows[0], low[...])
        if passes == 3:
            total += dot(rows[1], high[...])
        sums.append(total)
    one, two = sums
    return one[:, :window] - two[:, window:], one[:, window:] + two[:, :window]


def from_left(high, low, inner_hi, inner_lo):
    window = high.shape[0]
    sums = []
    for part in range(2):
        cols = slice(part * window, (part + 1) * window)
        sums.append(dot(high[:, cols], inner_hi) + dot(low[:, cols], inner_hi) + dot(high[:, cols], inner_lo))
    one, two = sums
    return one[:, :window] - two[:, window:], one[:, window:] + two[:, :window]


def rolled(twice, corner, store, window):
    r, c = corner
    rest = lax.rem(window - r, 8)
    back = lax.rem(CHUNK + 8 - rest, CHUNK + 8)
    for start in range(0, window, CHUNK):
        value = twice[pl.ds(pl.multiple_of(window - r - rest + start, 8), CHUNK + 8), :]
        store(start, pltpu.roll(pltpu.roll(value, back, 0)[:CHUNK], c, 1))


def twofold(twice, start, value, window):
    rows = value.shape[0]
    twice[start : start + rows] = value
    twice[window + start : window + start + rows] = value
    if start == 0:
        twice[2 * window : 2 * window + 8] = value[:8]


def corners_of(pos, count):
    return [(pos[number, 0, 0], pos[number, 0, 1]) for number in range(count)]


def detect(pos, residual, wave, table_hi, table_lo, field, first, second, middle, twice, grads):
    window = residual.shape[-1]
    count = residual.shape[0]
    odd = lax.rem(lax.axis_index("gy"), 2)
    corners = corners_of(pos, count)
    for number, corner in enumerate(corners):
        line = from_right((residual[number, 0, 0],), (residual[number, 0, 1],), table_hi, table_lo, 2)
        high, low = split(jnp.concatenate(line, axis=1))
        field_re, field_im = from_left(table_hi, table_lo, high, low)
        field[number, 0] = field_re
        field[number, 1] = field_im
        for start in range(0, window, CHUNK):
            rows = slice(start, start + CHUNK)
            wave_re, wave_im = wave[number, 0, 0, rows].astype(F32), wave[number, 0, 1, rows].astype(F32)
            value_re, value_im = field[number, 0, rows], field[number, 1, rows]
            twofold(twice.at[number, 0], start, wave_re * value_re + wave_im * value_im, window)
            twofold(twice.at[number, 1], start, wave_re * value_im - wave_im * value_re, window)
        for part in range(2):

            def store(start, value):
                grads[part, number, start : start + CHUNK] = value

            rolled(twice.at[number, part], corner, store, window)
    place([grads.at[0], grads.at[1]], corners, first, second, middle, odd, window)
    for ref in (first, second):
        ref[0, window // 2 :] = notes_of(pos, count, 2 * window)


def roll_fields(pos, field, probe, field_out, probes, twice):
    window = probe.shape[-1]
    count = field.shape[0]
    for part in range(2):
        for start in range(0, window, CHUNK):
            twofold(twice.at[count, part], start, probe[part, start : start + CHUNK], window)
    for number, corner in enumerate(corners_of(pos, count)):
        for part in range(2):
            for start in range(0, window, CHUNK):
                twofold(twice.at[number, part], start, field[number, part, start : start + CHUNK], window)

            def to_field(start, value):
                field_out[number, part, start : start + CHUNK] = value

            rolled(twice.at[number, part], corner, to_field, window)

            def to_probes(start, value):
                probes[number, part, start : start + CHUNK] = value

            rolled(twice.at[count, part], corner, to_probes, window)


def notes_size(count):
    return -(-(1 + 2 * count) // 8) * 8


def notes_of(pos, count, width):
    size = notes_size(count)
    row = lax.broadcasted_iota(jnp.int32, (size, width), 0)
    notes = jnp.where(row == 0, 1, 0)
    for number in range(count):
        for part in range(2):
            notes = jnp.where(row == 1 + 2 * number + part, pos[number, 0, part], notes)
    return notes.astype(F32)


def widen(object_field, from_first, from_second, first, second_out, middle):
    half = from_first.shape[-1]
    odd_x = lax.rem(lax.axis_index("gx"), 2)
    odd_y = lax.rem(lax.axis_index("gy"), 2)
    at_first = pl.ds(pl.multiple_of((1 - odd_x) * 3 * half, half), half)
    at_second = pl.ds(pl.multiple_of(odd_x * 3 * half, half), half)
    for plane in range(middle.shape[0]):
        middle[plane, :, half : 3 * half] = object_field[1, plane]
        middle[plane, :, at_first] = from_first[plane]
        middle[plane, :, at_second] = from_second[plane]
        for ref, base in ((first, (1 - odd_y) * half), (second_out, odd_y * half)):
            ref[plane] = middle[plane, pl.ds(pl.multiple_of(base, half), half), :]


def propagate(
    pos, field, probes, middle_in, from_first, from_second, table_hi, table_lo,
    first, second, middle,
    chi_hi, chi_lo, grads,
):
    window = field.shape[-1]
    half = window // 2
    count = field.shape[0]
    odd = lax.rem(lax.axis_index("gy"), 2)
    corners = corners_of(pos, count)

    for start in range(0, window, CHUNK):
        rows = slice(start, start + CHUNK)
        row = lax.broadcasted_iota(jnp.int32, (CHUNK, window), 0) + start
        col = lax.broadcasted_iota(jnp.int32, (CHUNK, window), 1)
        upper, lower = [], []
        for part in range(2):
            if start < half:
                upper.append(jnp.where(odd == 1, from_first[part, rows], from_second[part, rows]))
                lower.append(middle_in[part, half + start : half + start + CHUNK])
            else:
                shifted = slice(start - half, start - half + CHUNK)
                upper.append(middle_in[part, shifted])
                lower.append(jnp.where(odd == 1, from_second[part, shifted], from_first[part, shifted]))
        for number, (r, c) in enumerate(corners):
            low_row, low_col = row < r, col < c
            patch = []
            for part in range(2):
                above = jnp.where(low_col, upper[part][:, window:], upper[part][:, :window])
                below = jnp.where(low_col, lower[part][:, window:], lower[part][:, :window])
                patch.append(jnp.where(low_row, below, above))
            field_re, field_im = field[number, 0, rows], field[number, 1, rows]
            high, low = split(patch[0] * field_re + patch[1] * field_im)
            chi_hi[number, 0, rows] = high
            chi_lo[number, 0, rows] = low
            high, low = split(patch[0] * field_im - patch[1] * field_re)
            chi_hi[number, 1, rows] = high
            chi_lo[number, 1, rows] = low

    for number in range(count):
        line = from_right(
            (chi_hi[number, 0], chi_lo[number, 0]), (chi_hi[number, 1], chi_lo[number, 1]), table_hi, table_lo, 3
        )
        high, low = split(jnp.concatenate(line, axis=1))
        back_re, back_im = from_left(table_hi, table_lo, high, low)
        probe_re, probe_im = probes[number, 0], probes[number, 1]
        grads[0, number] = probe_re * back_re + probe_im * back_im
        grads[1, number] = probe_re * back_im - probe_im * back_re
    place([grads.at[0], grads.at[1]], corners, first, second, middle, odd, window)


def illuminate(pos, probe, up, down, first, second, scale, twice, notes, sems):
    window = probe.shape[-1]
    half = window // 2
    count = pos.shape[0]
    size = notes_size(count)
    odd_x = lax.rem(lax.axis_index("gx"), 2)
    odd_y = lax.rem(lax.axis_index("gy"), 2)
    copies, at = [], 0
    for ref, start, rows in ((up, half, size), (down, half, size), (first, window, 3 * size), (second, window, 3 * size)):
        source = ref.at[0, pl.ds(start, rows), pl.ds(0, half)]
        copies.append(pltpu.make_async_copy(source, notes.at[pl.ds(at, rows), :], sems.at[len(copies)]))
        copies[-1].start()
        at += rows
    for start in range(0, window, CHUNK):
        rows = slice(start, start + CHUNK)
        twofold(twice, start, probe[0, rows] * probe[0, rows] + probe[1, rows] * probe[1, rows], window)
    for copy in copies:
        copy.wait()

    shifts = []
    for down in (-1, 0, 1):
        for along in (-1, 0, 1):
            if along == 0:
                base = (odd_y if down > 0 else 1 - odd_y) * size
            else:
                base = (2 + 3 * (odd_x if along > 0 else 1 - odd_x) + 1 + down) * size
            for number in range(count):
                if down == 0 and along == 0:
                    valid, r, c = 1, pos[number, 0, 0], pos[number, 0, 1]
                else:
                    valid, r, c = (
                        notes[base + row, 0].astype(jnp.int32) for row in (0, 1 + 2 * number, 2 + 2 * number)
                    )
                top = r - half + window * down
                left = c - half + window * along
                top = jnp.where(valid == 1, top, window)
                shifts.append((top, left, r, c))

    def rows_at(index, carry):
        start = index * CHUNK
        row = lax.broadcasted_iota(jnp.int32, (CHUNK, window), 0) + start
        col = lax.broadcasted_iota(jnp.int32, (CHUNK, window), 1)
        total = jnp.zeros((CHUNK, window), F32)
        for top, left, r, c in shifts:
            turn = lax.rem(2 * window - half - r, window)
            rest = lax.rem(turn, 8)
            value = twice[pl.ds(pl.multiple_of(turn - rest + start, 8), CHUNK + 8), :]
            value = pltpu.roll(value, lax.rem(CHUNK + 8 - rest, CHUNK + 8), 0)[:CHUNK]
            value = pltpu.roll(value, lax.rem(c + half, window), 1)
            inside = (row >= top) & (row < top + window) & (col >= left) & (col < left + window)
            total += jnp.where(inside, value, 0.0)
        scale[pl.ds(pl.multiple_of(start, CHUNK), CHUNK), :] = 1.0 / (total + ridge)
        return carry

    lax.fori_loop(0, window // CHUNK, rows_at, 0)


def narrow(pos, middle, from_first, from_second, first, second, centre):
    half = first.shape[-1]
    window = 2 * half
    odd_x = lax.rem(lax.axis_index("gx"), 2)
    odd_y = lax.rem(lax.axis_index("gy"), 2)
    for plane in range(middle.shape[0]):
        for start in range(0, half, CHUNK):
            rows = slice(start, start + CHUNK)
            for received, base in ((from_first, (1 - odd_y) * half), (from_second, odd_y * half)):
                at = pl.ds(pl.multiple_of(base + start, CHUNK), CHUNK)
                total = middle[plane, at, :] + received[plane, rows]
                left, right = total[:, :half], total[:, 3 * half :]
                centre[plane, at, :] = total[:, half : 3 * half]
                first[plane, at, :] = jnp.where(odd_x == 1, left, right)
                second[plane, at, :] = jnp.where(odd_x == 1, right, left)
    if first.shape[1] > window:
        size = from_first.shape[1] - half
        above = jnp.where(odd_y == 1, from_first[0, half:, :half], from_second[0, half:, :half])
        below = jnp.where(odd_y == 1, from_second[0, half:, :half], from_first[0, half:, :half])
        for ref in (first, second):
            ref[0, window : window + size] = above
            ref[0, window + size : window + 2 * size] = notes_of(pos, pos.shape[0], half)
            ref[0, window + 2 * size :] = below


def join(centre, from_first, from_second, out):
    window = centre.shape[-1]
    half = window // 2
    odd_x = lax.rem(lax.axis_index("gx"), 2)
    for plane in range(centre.shape[0]):
        for received, base in ((from_first, (1 - odd_x) * half), (from_second, odd_x * half)):
            at = pl.ds(pl.multiple_of(base, half), half)
            out[plane, :, at] = centre[plane, :, at] + received[plane, :window]


def update(object_field, scale, total2, centre1, first1, second1, out):
    window = centre1.shape[-1]
    half = window // 2
    odd_x = lax.rem(lax.axis_index("gx"), 2)
    for part in range(2):
        out[1, part] = object_field[1, part] - total2[part] * scale[...]
        for received, base in ((first1, (1 - odd_x) * half), (second1, odd_x * half)):
            at = pl.ds(pl.multiple_of(base, half), half)
            total = centre1[part, :, at] + received[part]
            out[0, part, :, at] = object_field[0, part, :, at] - total * scale[:, at]


VMEM = pl.BlockSpec(memory_space=pltpu.VMEM)
SMEM = pl.BlockSpec(memory_space=pltpu.SMEM)
HBM = pl.BlockSpec(memory_space=pltpu.HBM)


def call(body, outs, in_specs, args, scratch=(), micros=0.0, name=None):
    return pl.pallas_call(
        body,
        out_shape=[jax.ShapeDtypeStruct(shape, F32) for shape in outs],
        in_specs=in_specs,
        out_specs=[VMEM] * len(outs),
        scratch_shapes=list(scratch),
        compiler_params=pltpu.CompilerParams(vmem_limit_bytes=24 * 1024 * 1024),
        cost_estimate=pl.CostEstimate(flops=int(micros * 1e9), bytes_accessed=1, transcendentals=0),
        name=name,
    )(*args)


def shards(object_field, probe, positions, residual, saved_wave):
    window = probe.shape[-1]
    half = window // 2
    count = positions.shape[0]
    size = notes_size(count)
    wave_hi, wave_lo, move_hi, move_lo = (jnp.asarray(t) for t in tables(window))
    barrier = lax.optimization_barrier

    def twice(planes):
        return pltpu.VMEM((*planes, 2 * window + 8, window), F32)

    grads = pltpu.VMEM((2, count, window, window), F32)
    fields_shape = (count, 2, window, window)

    def pieces(planes, extra=0):
        return [(planes, half + extra, 2 * window), (planes, half + extra, 2 * window), (planes, window, 2 * window)]

    def strips(planes, extra=0):
        return [(planes, window + extra, half), (planes, window + extra, half), (planes, window, window)]

    odd_x = lax.rem(lax.axis_index("gx"), 2)
    left, right = object_field[1, :, :, :half], object_field[1, :, :, half:]
    first0 = jnp.where(odd_x == 1, left, right)
    second0 = jnp.where(odd_x == 1, right, left)
    halo_first = swapped(first0, "gx", 0)
    halo_second = swapped(second0, "gx", 1)

    field, up2, down2, middle2 = call(
        detect,
        [fields_shape] + pieces(2, size),
        [SMEM] + [VMEM] * 4,
        (positions, residual, saved_wave, wave_hi, wave_lo),
        [twice((count, 2)), grads],
        micros=12.0, name="detect",
    )
    from_up2 = swapped(up2, "gy", 0)
    from_down2 = swapped(down2, "gy", 1)

    halo_first, halo_second, field = barrier((halo_first, halo_second, field))
    fields, probes = call(
        roll_fields,
        [fields_shape] * 2,
        [SMEM] + [VMEM] * 2,
        (positions, field, probe),
        [twice((count + 1, 2))],
        micros=12.0, name="roll",
    )

    halo_first, halo_second, fields, probes, from_up2, from_down2 = barrier(
        (halo_first, halo_second, fields, probes, from_up2, from_down2)
    )
    up0, down0, wide0 = call(
        widen,
        pieces(2),
        [VMEM] * 3,
        (object_field, halo_first, halo_second),
        micros=0.2, name="widen",
    )
    from_up0 = swapped(up0, "gy", 0)
    from_down0 = swapped(down0, "gy", 1)

    first2, second2, centre2 = call(
        narrow,
        strips(2, 3 * size),
        [SMEM] + [VMEM] * 3,
        (positions, middle2, from_up2, from_down2),
        micros=0.2, name="narrow2",
    )
    from_up0, from_down0, first2, second2, centre2 = barrier((from_up0, from_down0, first2, second2, centre2))
    got_first2 = swapped(first2, "gx", 0)
    got_second2 = swapped(second2, "gx", 1)

    up1, down1, middle1 = call(
        propagate,
        pieces(2),
        [SMEM] + [VMEM] * 7,
        (positions, fields, probes, wide0, from_up0, from_down0, move_hi, move_lo),
        [pltpu.VMEM(fields_shape, BF16)] * 2 + [grads],
        micros=12.0, name="propagate",
    )
    from_up1 = swapped(up1, "gy", 0)
    from_down1 = swapped(down1, "gy", 1)
    (total2,) = call(
        join, [centre2.shape], [VMEM] * 3, (centre2, got_first2, got_second2), micros=12.0, name="join2"
    )
    middle1, total2 = barrier((middle1, total2))
    first1, second1, centre1 = call(
        narrow,
        strips(2),
        [SMEM] + [VMEM] * 3,
        (positions, middle1, from_up1, from_down1),
        micros=0.2, name="narrow1",
    )
    got_first1 = swapped(first1, "gx", 0)
    got_second1 = swapped(second1, "gx", 1)

    (scale,) = call(
        illuminate,
        [(window, window)],
        [SMEM] + [VMEM] * 5,
        (positions, probe, from_up2, from_down2, got_first2, got_second2),
        [twice(()), pltpu.SMEM((8 * size, half), F32), pltpu.SemaphoreType.DMA((4,))],
        micros=2.0, name="illuminate",
    )
    (new_object,) = call(
        update,
        [object_field.shape],
        [VMEM] * 6,
        (object_field, scale, total2, centre1, got_first1, got_second1),
        micros=1.0, name="update",
    )
    return new_object


def solution(mesh):
    placed = (
        P(None, None, "gy", "gx"),
        P(),
        P("gy", "gx", None),
        P("gy", "gx", None, None, None),
        P("gy", "gx", None, None, None),
    )
    return jax.shard_map(
        shards, mesh=mesh, in_specs=placed, out_specs=P(None, None, "gy", "gx"), check_vma=False
    )
```

time: 71.4 us -> 67.4 us (0.944); the launches traced: 70.2 us -> 67.1 us
  waiting for transfers between devices: 38.1 us -> 25.6 us
  Pallas kernels: 9.52 us -> 15.5 us
  starting transfers between devices: 19.9 us -> 22.7 us
  other arithmetic: 0.04 us -> 1.15 us
    ppermute x12, waiting for transfers between devices: 38.1 us -> 25.6 us  [swapped(): return lax.ppermute(value, axis, swap_pairs(lax.axis_size(axis), first))]
    pallas_call x6 -> x9, Pallas kernels: 9.52 us -> 15.5 us  [call(): pl.pallas_call(body, out_shape=[jax.ShapeDtypeStruct(shape, F32) for shap...]
    ppermute x12, starting transfers between devices: 19.9 us -> 22.7 us  [swapped(): return lax.ppermute(value, axis, swap_pairs(lax.axis_size(axis), first))]
    squeeze x1 -> x0, local copies, waits for them, and re-layouts: 1.23 us -> none  [shards(): second = object_field[1]]
    select_n x1, other arithmetic: 0.04 us -> 1.15 us  [shards(): second0 = jnp.where(odd_x == 1, right, left)]
    unnamed x26 -> x18, local copies, waits for them, and re-layouts: 1.09 us -> 1.93 us
  transfers between devices with their start and end apart: 12 -> 12, of which waited for: 8 -> 5; matrix products, arithmetic and copies ran while one was open for 0% -> 0% of each run, Pallas kernels for 12% -> 20%
where the time goes in v2:
time: 67.4 us; the launch traced here: 67.1 us
  waiting for transfers between devices  25.6 us (38%)
  starting transfers between devices  22.7 us (34%)
  Pallas kernels  15.5 us (23%)
  local copies, waits for them, and re-layouts  1.93 us (3%)
  other arithmetic  1.15 us (2%)
    ppermute x12, waiting for transfers between devices, swapped(): return lax.ppermute(value, axis, swap_pairs(lax.axis_size(axis), first))  25.6 us
    ppermute x12, starting transfers between devices, swapped(): return lax.ppermute(value, axis, swap_pairs(lax.axis_size(axis), first))  22.7 us
    pallas_call x9, Pallas kernels, call(): pl.pallas_call(body, out_shape=[jax.ShapeDtypeStruct(shape, F32) for shap...  15.5 us
    unnamed x18, local copies, waits for them, and re-layouts  1.93 us
  transfers between devices with their start and end apart: 12, of which 5 were waited for; matrix products, arithmetic and copies ran while one was open for 0% of the time, Pallas kernels for 20%

profile of v2, /device:TPU:11, one launch (start us, length us, event | category | flops | bytes accessed | tf_op | source)
XLA Modules:
  0.0 67.1 jit_solution(456657003279668939)
XLA Ops:
  0.0 0.0 copy-start.2
  0.0 0.0 copy-start.3
  0.0 1.2 %select_bitcast_fusion = (f32[2,256,128]{2,1,0:T(8,128)S(1)}, f32[2,256,128]{2,1,0:T(8,128)S(1)}) fusion(f32[2,2,256,256]{3,2,1,0:T(8,128)} %object_field.3, pred[]{:T(512)S(6)} %eq.4), kind=kLoop, calls=%fused_computation | loop fusion | flops 131072 | bytes 1048577 | tf_op jit(solution)/shard_map/jit(_where)/select_n | solution.py:409
  1.2 0.0 copy-start.1
  1.2 0.3 collective-permute-start
  1.5 0.0 copy-start.4
  1.5 4.2 %collective-permute-start.1 = (f32[2,256,128]{2,1,0:T(8,128)S(1)}, f32[2,256,128]{2,1,0:T(8,128)S(1)}, u32[]{:S(2)}, u32[]{:S(2)}) collective-permute-start(f32[2,256,128]{2,1,0:T(8,128)S(1)} %get-tuple-element.73), channel_id=1, source_target_pairs={{8,16},{16,8},{9,17},{17,9},{10,18},{18,10},{11,19},{19,11},{12,20... | collective-permute-start | bytes 786440 | tf_op jit(solution)/shard_map/ppermute | solution.py:45
  5.7 0.0 copy-done.2
  5.7 0.0 copy-done.3
  5.7 0.0 copy-done.1
  5.7 0.0 copy-start.7
  5.7 0.9 %copy-done.7 = bf16[256,512]{1,0:T(8,128)(2,1)S(1)} copy-done((bf16[256,512]{1,0:T(8,128)(2,1)S(1)}, bf16[256,512]{1,0:T(8,128)(2,1)}, u32[]{:S(2)}) %copy-start.7) | copy-done | bytes 262168
  6.7 0.0 copy-start.8
  6.7 0.9 %copy-done.8 = bf16[256,512]{1,0:T(8,128)(2,1)S(1)} copy-done((bf16[256,512]{1,0:T(8,128)(2,1)S(1)}, bf16[256,512]{1,0:T(8,128)(2,1)}, u32[]{:S(2)}) %copy-start.8) | copy-done | bytes 262168
  7.6 3.3 %detect.1 = (f32[2,2,256,256]{3,2,1,0:T(8,128)S(1)}, f32[2,136,512]{2,1,0:T(8,128)S(1)}, f32[2,136,512]{2,1,0:T(8,128)S(1)}, f32[2,256,512]{2,1,0:T(8,128)S(1)}) custom-call(s32[2,1,2]{2,1,0:T(1,128)S(1)} %copy-done.1, bf16[2,1,2,256,256]{4,3,2,1,0:T(8,128)(2,1)S(1)} %copy-done.2, bf16[2,1,2,256,256]{4,3,2,1,0:T(8,128)(2,1)S(1)} %copy-done.3, ...), custom_call_target="tpu_custom_call" | custom-call | flops 12000000000 | bytes 1 | tf_op jit(solution)/shard_map/detect/pallas_call | solution.py:374
  10.9 1.3 %collective-permute-start.2 = (f32[2,136,512]{2,1,0:T(8,128)S(1)}, f32[2,136,512]{2,1,0:T(8,128)S(1)}, u32[]{:S(2)}, u32[]{:S(2)}) collective-permute-start(f32[2,136,512]{2,1,0:T(8,128)S(1)} %get-tuple-element.45), channel_id=1, source_target_pairs={{0,1},{1,0},{2,3},{3,2},{4,5},{5,4},{6,7},{7,6},{8,9},{9,8},{10,11... | collective-permute-start | bytes 1671176 | tf_op jit(solution)/shard_map/ppermute | solution.py:45
  12.2 3.1 %collective-permute-start.3 = (f32[2,136,512]{2,1,0:T(8,128)S(1)}, f32[2,136,512]{2,1,0:T(8,128)S(1)}, u32[]{:S(2)}, u32[]{:S(2)}) collective-permute-start(f32[2,136,512]{2,1,0:T(8,128)S(1)} %get-tuple-element.46), channel_id=1, source_target_pairs={{1,2},{2,1},{3,4},{4,3},{5,6},{6,5},{9,10},{10,9},{11,12},{12,11},... | collective-permute-start | bytes 1671176 | tf_op jit(solution)/shard_map/ppermute | solution.py:45
  15.3 0.0 collective-permute-done.from_first
  15.3 0.0 collective-permute-done.1.from_second
  15.3 0.0 copy-done.4
  15.4 0.0 copy-start
  15.4 1.4 %roll.1 = (f32[2,2,256,256]{3,2,1,0:T(8,128)S(1)}, f32[2,2,256,256]{3,2,1,0:T(8,128)S(1)}) custom-call(s32[2,1,2]{2,1,0:T(1,128)S(1)} %copy-done.1, f32[2,2,256,256]{3,2,1,0:T(8,128)S(1)} %get-tuple-element.42.field, f32[2,256,256]{2,1,0:T(8,128)S(1)} %copy-done.4), custom_call_target="tpu_custom_call" | custom-call | flops 12000000000 | bytes 1 | tf_op jit(solution)/shard_map/roll/pallas_call | solution.py:374
  16.7 0.0 collective-permute-done.2.from_first.up
  16.7 6.3 %collective-permute-done.3.from_second.down = f32[2,136,512]{2,1,0:T(8,128)S(1)} collective-permute-done((f32[2,136,512]{2,1,0:T(8,128)S(1)}, f32[2,136,512]{2,1,0:T(8,128)S(1)}, u32[]{:S(2)}, u32[]{:S(2)}) %collective-permute-start.3) | collective-permute-done | bytes 557088 | tf_op jit(solution)/shard_map/ppermute | solution.py:45
  23.0 0.0 copy-done
  23.0 0.2 widen.1
  23.2 0.1 collective-permute-start.4
  23.3 3.6 %collective-permute-start.5 = (f32[2,128,512]{2,1,0:T(8,128)S(1)}, f32[2,128,512]{2,1,0:T(8,128)S(1)}, u32[]{:S(2)}, u32[]{:S(2)}) collective-permute-start(f32[2,128,512]{2,1,0:T(8,128)S(1)} %get-tuple-element.52), channel_id=1, source_target_pairs={{1,2},{2,1},{3,4},{4,3},{5,6},{6,5},{9,10},{10,9},{11,12},{12,11},... | collective-permute-start | bytes 1572872 | tf_op jit(solution)/shard_map/ppermute | solution.py:45
  26.9 0.0 copy-start.5
  26.9 0.0 copy-start.6
  26.9 0.7 narrow2.1
  27.6 0.0 collective-permute-done.4.from_first
  27.6 6.3 %collective-permute-done.5.from_second = f32[2,128,512]{2,1,0:T(8,128)S(1)} collective-permute-done((f32[2,128,512]{2,1,0:T(8,128)S(1)}, f32[2,128,512]{2,1,0:T(8,128)S(1)}, u32[]{:S(2)}, u32[]{:S(2)}) %collective-permute-start.5) | collective-permute-done | bytes 524320 | tf_op jit(solution)/shard_map/ppermute | solution.py:45
  33.9 0.0 collective-permute-start.6
  33.9 2.1 %collective-permute-start.7 = (f32[2,280,128]{2,1,0:T(8,128)S(1)}, f32[2,280,128]{2,1,0:T(8,128)S(1)}, u32[]{:S(2)}, u32[]{:S(2)}) collective-permute-start(f32[2,280,128]{2,1,0:T(8,128)S(1)} %get-tuple-element.58), channel_id=1, source_target_pairs={{8,16},{16,8},{9,17},{17,9},{10,18},{18,10},{11,19},{19,11},{12,20... | collective-permute-start | bytes 860168 | tf_op jit(solution)/shard_map/ppermute | solution.py:45
  36.0 0.0 copy-done.5
  36.0 0.0 copy-done.6
  36.0 3.5 %propagate.1 = (f32[2,128,512]{2,1,0:T(8,128)S(1)}, f32[2,128,512]{2,1,0:T(8,128)S(1)}, f32[2,256,512]{2,1,0:T(8,128)S(1)}) custom-call(s32[2,1,2]{2,1,0:T(1,128)S(1)} %copy-done.1, f32[2,2,256,256]{3,2,1,0:T(8,128)S(1)} %get-tuple-element.59.field, f32[2,2,256,256]{3,2,1,0:T(8,128)S(1)} %get-tuple-element.60.probes, ...), custom_call_target="tpu_custom_call" | custom-call | flops 12000000000 | bytes 1 | tf_op jit(solution)/shard_map/propagate/pallas_call | solution.py:374
  39.5 0.7 %collective-permute-start.8 = (f32[2,128,512]{2,1,0:T(8,128)S(1)}, f32[2,128,512]{2,1,0:T(8,128)S(1)}, u32[]{:S(2)}, u32[]{:S(2)}) collective-permute-start(f32[2,128,512]{2,1,0:T(8,128)S(1)} %get-tuple-element.68), channel_id=1, source_target_pairs={{0,1},{1,0},{2,3},{3,2},{4,5},{5,4},{6,7},{7,6},{8,9},{9,8},{10,11... | collective-permute-start | bytes 1572872 | tf_op jit(solution)/shard_map/ppermute | solution.py:45
  40.3 3.1 %collective-permute-start.9 = (f32[2,128,512]{2,1,0:T(8,128)S(1)}, f32[2,128,512]{2,1,0:T(8,128)S(1)}, u32[]{:S(2)}, u32[]{:S(2)}) collective-permute-start(f32[2,128,512]{2,1,0:T(8,128)S(1)} %get-tuple-element.69), channel_id=1, source_target_pairs={{1,2},{2,1},{3,4},{4,3},{5,6},{6,5},{9,10},{10,9},{11,12},{12,11},... | collective-permute-start | bytes 1572872 | tf_op jit(solution)/shard_map/ppermute | solution.py:45
  43.4 0.0 collective-permute-done.6.first.from_first
  43.4 3.7 %collective-permute-done.7.second.from_second = f32[2,280,128]{2,1,0:T(8,128)S(1)} collective-permute-done((f32[2,280,128]{2,1,0:T(8,128)S(1)}, f32[2,280,128]{2,1,0:T(8,128)S(1)}, u32[]{:S(2)}, u32[]{:S(2)}) %collective-permute-start.7) | collective-permute-done | bytes 286752 | tf_op jit(solution)/shard_map/ppermute | solution.py:45
  47.1 0.1 join2.1.total2
  47.2 0.0 collective-permute-done.8.from_first
  47.2 3.5 %collective-permute-done.9.from_second = f32[2,128,512]{2,1,0:T(8,128)S(1)} collective-permute-done((f32[2,128,512]{2,1,0:T(8,128)S(1)}, f32[2,128,512]{2,1,0:T(8,128)S(1)}, u32[]{:S(2)}, u32[]{:S(2)}) %collective-permute-start.9) | collective-permute-done | bytes 524320 | tf_op jit(solution)/shard_map/ppermute | solution.py:45
  50.7 0.7 narrow1.1
  51.4 0.1 collective-permute-start.10
  51.5 4.1 %collective-permute-start.11 = (f32[2,256,128]{2,1,0:T(8,128)S(1)}, f32[2,256,128]{2,1,0:T(8,128)S(1)}, u32[]{:S(2)}, u32[]{:S(2)}) collective-permute-start(f32[2,256,128]{2,1,0:T(8,128)S(1)} %get-tuple-element.72), channel_id=1, source_target_pairs={{8,16},{16,8},{9,17},{17,9},{10,18},{18,10},{11,19},{19,11},{12,20... | collective-permute-start | bytes 786440 | tf_op jit(solution)/shard_map/ppermute | solution.py:45
  55.6 4.6 %illuminate.1.scale = f32[256,256]{1,0:T(8,128)S(1)} custom-call(s32[2,1,2]{2,1,0:T(1,128)S(1)} %copy-done.1, f32[2,256,256]{2,1,0:T(8,128)S(1)} %copy-done.4, f32[2,136,512]{2,1,0:T(8,128)S(1)} %collective-permute-done.2.from_first.up, f32[2,136,512]{2,1,0:T(8,128)S(1)} %collective-permute-done.3.from_second.down, ...), custom_call_target="tpu_custom_call" | custom-call | flops 2000000000 | bytes 1 | tf_op jit(solution)/shard_map/illuminate/pallas_call | solution.py:374
  60.2 0.0 collective-permute-done.10.first1
  60.2 5.7 %collective-permute-done.11.second1 = f32[2,256,128]{2,1,0:T(8,128)S(1)} collective-permute-done((f32[2,256,128]{2,1,0:T(8,128)S(1)}, f32[2,256,128]{2,1,0:T(8,128)S(1)}, u32[]{:S(2)}, u32[]{:S(2)}) %collective-permute-start.11) | collective-permute-done | bytes 262176 | tf_op jit(solution)/shard_map/ppermute | solution.py:45
  65.9 1.2 %update.1 = f32[2,2,256,256]{3,2,1,0:T(8,128)} custom-call(f32[2,2,256,256]{3,2,1,0:T(8,128)S(1)} %copy-done, f32[256,256]{1,0:T(8,128)S(1)} %illuminate.1.scale, f32[2,256,256]{2,1,0:T(8,128)S(1)} %join2.1.total2, f32[2,256,256]{2,1,0:T(8,128)S(1)} %get-tuple-element.70.centre1, f32[2,256,128]{2,1,0:T(8,128)S(1)} %collective-permute-done.10.first1, ...), custom_call_target="tpu_custom_call" | custom-call | flops 1000000000 | bytes 1 | tf_op jit(solution)/shard_map/update/pallas_call | solution.py:374
Async XLA Ops:
  0.0 5.7 %copy-start.2 = (bf16[2,1,2,256,256]{4,3,2,1,0:T(8,128)(2,1)S(1)}, bf16[2,1,2,256,256]{4,3,2,1,0:T(8,128)(2,1)}, u32[]{:S(2)}) copy-start(bf16[2,1,2,256,256]{4,3,2,1,0:T(8,128)(2,1)} %residual.1) | copy-start | bytes 1572868
  0.0 5.7 %copy-start.3 = (bf16[2,1,2,256,256]{4,3,2,1,0:T(8,128)(2,1)S(1)}, bf16[2,1,2,256,256]{4,3,2,1,0:T(8,128)(2,1)}, u32[]{:S(2)}) copy-start(bf16[2,1,2,256,256]{4,3,2,1,0:T(8,128)(2,1)} %wave.1) | copy-start | bytes 1572868
  1.2 4.6 %copy-start.1 = (s32[2,1,2]{2,1,0:T(1,128)S(1)}, s32[2,1,2]{2,1,0:T(1,128)}, u32[]{:S(2)}) copy-start(s32[2,1,2]{2,1,0:T(1,128)} %pos.11) | copy-start | bytes 52
  1.2 14.1 %collective-permute-start = (f32[2,256,128]{2,1,0:T(8,128)S(1)}, f32[2,256,128]{2,1,0:T(8,128)S(1)}, u32[]{:S(2)}, u32[]{:S(2)}) collective-permute-start(f32[2,256,128]{2,1,0:T(8,128)S(1)} %get-tuple-element.74), channel_id=1, source_target_pairs={{0,8},{8,0},{16,24},{24,16},{1,9},{9,1},{17,25},{25,17},{2,10},{10... | collective-permute-start | bytes 786440 | tf_op jit(solution)/shard_map/ppermute | solution.py:45
  1.5 13.8 %copy-start.4 = (f32[2,256,256]{2,1,0:T(8,128)S(1)}, f32[2,256,256]{2,1,0:T(8,128)}, u32[]{:S(2)}) copy-start(f32[2,256,256]{2,1,0:T(8,128)} %probe.3) | copy-start | bytes 1572868
  1.5 13.8 %collective-permute-start.1 = (f32[2,256,128]{2,1,0:T(8,128)S(1)}, f32[2,256,128]{2,1,0:T(8,128)S(1)}, u32[]{:S(2)}, u32[]{:S(2)}) collective-permute-start(f32[2,256,128]{2,1,0:T(8,128)S(1)} %get-tuple-element.73), channel_id=1, source_target_pairs={{8,16},{16,8},{9,17},{17,9},{10,18},{18,10},{11,19},{19,11},{12,20... | collective-permute-start | bytes 786440 | tf_op jit(solution)/shard_map/ppermute | solution.py:45
  5.7 1.0 %copy-start.7 = (bf16[256,512]{1,0:T(8,128)(2,1)S(1)}, bf16[256,512]{1,0:T(8,128)(2,1)}, u32[]{:S(2)}) copy-start(bf16[256,512]{1,0:T(8,128)(2,1)} %constant.19.clone.table_hi) | copy-start | bytes 786436
  6.7 0.9 %copy-start.8 = (bf16[256,512]{1,0:T(8,128)(2,1)S(1)}, bf16[256,512]{1,0:T(8,128)(2,1)}, u32[]{:S(2)}) copy-start(bf16[256,512]{1,0:T(8,128)(2,1)} %constant.20.clone.table_lo) | copy-start | bytes 786436
  10.9 5.8 %collective-permute-start.2 = (f32[2,136,512]{2,1,0:T(8,128)S(1)}, f32[2,136,512]{2,1,0:T(8,128)S(1)}, u32[]{:S(2)}, u32[]{:S(2)}) collective-permute-start(f32[2,136,512]{2,1,0:T(8,128)S(1)} %get-tuple-element.45), channel_id=1, source_target_pairs={{0,1},{1,0},{2,3},{3,2},{4,5},{5,4},{6,7},{7,6},{8,9},{9,8},{10,11... | collective-permute-start | bytes 1671176 | tf_op jit(solution)/shard_map/ppermute | solution.py:45
  12.2 10.8 %collective-permute-start.3 = (f32[2,136,512]{2,1,0:T(8,128)S(1)}, f32[2,136,512]{2,1,0:T(8,128)S(1)}, u32[]{:S(2)}, u32[]{:S(2)}) collective-permute-start(f32[2,136,512]{2,1,0:T(8,128)S(1)} %get-tuple-element.46), channel_id=1, source_target_pairs={{1,2},{2,1},{3,4},{4,3},{5,6},{6,5},{9,10},{10,9},{11,12},{12,11},... | collective-permute-start | bytes 1671176 | tf_op jit(solution)/shard_map/ppermute | solution.py:45
  15.4 7.7 %copy-start = (f32[2,2,256,256]{3,2,1,0:T(8,128)S(1)}, f32[2,2,256,256]{3,2,1,0:T(8,128)}, u32[]{:S(2)}) copy-start(f32[2,2,256,256]{3,2,1,0:T(8,128)} %object_field.3) | copy-start | bytes 3145732
  23.2 4.4 %collective-permute-start.4 = (f32[2,128,512]{2,1,0:T(8,128)S(1)}, f32[2,128,512]{2,1,0:T(8,128)S(1)}, u32[]{:S(2)}, u32[]{:S(2)}) collective-permute-start(f32[2,128,512]{2,1,0:T(8,128)S(1)} %get-tuple-element.51), channel_id=1, source_target_pairs={{0,1},{1,0},{2,3},{3,2},{4,5},{5,4},{6,7},{7,6},{8,9},{9,8},{10,11... | collective-permute-start | bytes 1572872 | tf_op jit(solution)/shard_map/ppermute | solution.py:45
  23.3 10.6 %collective-permute-start.5 = (f32[2,128,512]{2,1,0:T(8,128)S(1)}, f32[2,128,512]{2,1,0:T(8,128)S(1)}, u32[]{:S(2)}, u32[]{:S(2)}) collective-permute-start(f32[2,128,512]{2,1,0:T(8,128)S(1)} %get-tuple-element.52), channel_id=1, source_target_pairs={{1,2},{2,1},{3,4},{4,3},{5,6},{6,5},{9,10},{10,9},{11,12},{12,11},... | collective-permute-start | bytes 1572872 | tf_op jit(solution)/shard_map/ppermute | solution.py:45
  26.9 9.1 %copy-start.5 = (bf16[256,512]{1,0:T(8,128)(2,1)S(1)}, bf16[256,512]{1,0:T(8,128)(2,1)}, u32[]{:S(2)}) copy-start(bf16[256,512]{1,0:T(8,128)(2,1)} %constant.21.clone.table_hi) | copy-start | bytes 786436
  26.9 9.1 %copy-start.6 = (bf16[256,512]{1,0:T(8,128)(2,1)S(1)}, bf16[256,512]{1,0:T(8,128)(2,1)}, u32[]{:S(2)}) copy-start(bf16[256,512]{1,0:T(8,128)(2,1)} %constant.22.clone.table_lo) | copy-start | bytes 786436
  33.9 9.5 %collective-permute-start.6 = (f32[2,280,128]{2,1,0:T(8,128)S(1)}, f32[2,280,128]{2,1,0:T(8,128)S(1)}, u32[]{:S(2)}, u32[]{:S(2)}) collective-permute-start(f32[2,280,128]{2,1,0:T(8,128)S(1)} %get-tuple-element.57), channel_id=1, source_target_pairs={{0,8},{8,0},{16,24},{24,16},{1,9},{9,1},{17,25},{25,17},{2,10},{10... | collective-permute-start | bytes 860168 | tf_op jit(solution)/shard_map/ppermute | solution.py:45
  33.9 13.2 %collective-permute-start.7 = (f32[2,280,128]{2,1,0:T(8,128)S(1)}, f32[2,280,128]{2,1,0:T(8,128)S(1)}, u32[]{:S(2)}, u32[]{:S(2)}) collective-permute-start(f32[2,280,128]{2,1,0:T(8,128)S(1)} %get-tuple-element.58), channel_id=1, source_target_pairs={{8,16},{16,8},{9,17},{17,9},{10,18},{18,10},{11,19},{19,11},{12,20... | collective-permute-start | bytes 860168 | tf_op jit(solution)/shard_map/ppermute | solution.py:45
  39.5 7.7 %collective-permute-start.8 = (f32[2,128,512]{2,1,0:T(8,128)S(1)}, f32[2,128,512]{2,1,0:T(8,128)S(1)}, u32[]{:S(2)}, u32[]{:S(2)}) collective-permute-start(f32[2,128,512]{2,1,0:T(8,128)S(1)} %get-tuple-element.68), channel_id=1, source_target_pairs={{0,1},{1,0},{2,3},{3,2},{4,5},{5,4},{6,7},{7,6},{8,9},{9,8},{10,11... | collective-permute-start | bytes 1572872 | tf_op jit(solution)/shard_map/ppermute | solution.py:45
  40.3 10.5 %collective-permute-start.9 = (f32[2,128,512]{2,1,0:T(8,128)S(1)}, f32[2,128,512]{2,1,0:T(8,128)S(1)}, u32[]{:S(2)}, u32[]{:S(2)}) collective-permute-start(f32[2,128,512]{2,1,0:T(8,128)S(1)} %get-tuple-element.69), channel_id=1, source_target_pairs={{1,2},{2,1},{3,4},{4,3},{5,6},{6,5},{9,10},{10,9},{11,12},{12,11},... | collective-permute-start | bytes 1572872 | tf_op jit(solution)/shard_map/ppermute | solution.py:45
  51.4 8.8 %collective-permute-start.10 = (f32[2,256,128]{2,1,0:T(8,128)S(1)}, f32[2,256,128]{2,1,0:T(8,128)S(1)}, u32[]{:S(2)}, u32[]{:S(2)}) collective-permute-start(f32[2,256,128]{2,1,0:T(8,128)S(1)} %get-tuple-element.71), channel_id=1, source_target_pairs={{0,8},{8,0},{16,24},{24,16},{1,9},{9,1},{17,25},{25,17},{2,10},{10... | collective-permute-start | bytes 786440 | tf_op jit(solution)/shard_map/ppermute | solution.py:45
  51.5 14.4 %collective-permute-start.11 = (f32[2,256,128]{2,1,0:T(8,128)S(1)}, f32[2,256,128]{2,1,0:T(8,128)S(1)}, u32[]{:S(2)}, u32[]{:S(2)}) collective-permute-start(f32[2,256,128]{2,1,0:T(8,128)S(1)} %get-tuple-element.72), channel_id=1, source_target_pairs={{8,16},{16,8},{9,17},{17,9},{10,18},{18,10},{11,19},{19,11},{12,20... | collective-permute-start | bytes 786440 | tf_op jit(solution)/shard_map/ppermute | solution.py:45

commit v3 on v2

--- a/solution.py
+++ b/solution.py
@@ -31,7 +31,7 @@
     out = []
     for matrix in (inverse, move):
         out.extend(two_parts(np.concatenate([matrix.real, matrix.imag], axis=1)))
-    return tuple(out)
+    return np.stack(out)
 
 
 def swap_pairs(count, first):
@@ -78,8 +78,15 @@
 
     def writer(ref, offset):
         def store(plane, start, left, right):
-            ref[plane, offset + start : offset + start + CHUNK, :window] = left
-            ref[plane, offset + start : offset + start + CHUNK, window:] = right
+            at = slice(offset + start, offset + start + CHUNK)
+            if isinstance(ref, tuple):
+                ref[0][plane, at, :half] = left[:, :half]
+                ref[0][plane, at, half:] = right[:, half:]
+                ref[1][plane, at, :half] = left[:, half:]
+                ref[1][plane, at, half:] = right[:, :half]
+            else:
+                ref[plane, at, :window] = left
+                ref[plane, at, window:] = right
 
         return store
 
@@ -128,16 +135,25 @@
         twice[2 * window : 2 * window + 8] = value[:8]
 
 
-def corners_of(pos, count):
-    return [(pos[number, 0, 0], pos[number, 0, 1]) for number in range(count)]
-
-
-def detect(pos, residual, wave, table_hi, table_lo, field, first, second, middle, twice, grads):
+def corners_of(pos):
+    return [(pos[number, 0, 0], pos[number, 0, 1]) for number in range(pos.shape[0])]
+
+
+def fetched(pos_any, pos, sem):
+    copy = pltpu.make_async_copy(pos_any, pos, sem)
+    copy.start()
+    return copy
+
+
+def detect(
+    pos_any, residual, wave, table, field, first, second, middle, notes, marks, twice, grads, pos, sem
+):
     window = residual.shape[-1]
     count = residual.shape[0]
     odd = lax.rem(lax.axis_index("gy"), 2)
-    corners = corners_of(pos, count)
-    for number, corner in enumerate(corners):
+    arrival = fetched(pos_any, pos, sem)
+    table_hi, table_lo = table.at[0], table.at[1]
+    for number in range(count):
         line = from_right((residual[number, 0, 0],), (residual[number, 0, 1],), table_hi, table_lo, 2)
         high, low = split(jnp.concatenate(line, axis=1))
         field_re, field_im = from_left(table_hi, table_lo, high, low)
@@ -149,27 +165,34 @@
             value_re, value_im = field[number, 0, rows], field[number, 1, rows]
             twofold(twice.at[number, 0], start, wave_re * value_re + wave_im * value_im, window)
             twofold(twice.at[number, 1], start, wave_re * value_im - wave_im * value_re, window)
+    arrival.wait()
+    corners = corners_of(pos)
+    for number, corner in enumerate(corners):
         for part in range(2):
 
             def store(start, value):
                 grads[part, number, start : start + CHUNK] = value
 
             rolled(twice.at[number, part], corner, store, window)
+            marks[2 * number + part] = jnp.full(marks.shape[1:], corner[part], jnp.int32)
     place([grads.at[0], grads.at[1]], corners, first, second, middle, odd, window)
     for ref in (first, second):
         ref[0, window // 2 :] = notes_of(pos, count, 2 * window)
-
-
-def roll_fields(pos, field, probe, field_out, probes, twice):
+    notes[...] = notes_of(pos, count, window // 2)
+
+
+def roll_fields(pos_any, field, probe, field_out, probes, twice, pos, sem):
     window = probe.shape[-1]
     count = field.shape[0]
+    arrival = fetched(pos_any, pos, sem)
     for part in range(2):
         for start in range(0, window, CHUNK):
             twofold(twice.at[count, part], start, probe[part, start : start + CHUNK], window)
-    for number, corner in enumerate(corners_of(pos, count)):
+            for number in range(count):
+                twofold(twice.at[number, part], start, field[number, part, start : start + CHUNK], window)
+    arrival.wait()
+    for number, corner in enumerate(corners_of(pos)):
         for part in range(2):
-            for start in range(0, window, CHUNK):
-                twofold(twice.at[number, part], start, field[number, part, start : start + CHUNK], window)
 
             def to_field(start, value):
                 field_out[number, part, start : start + CHUNK] = value
@@ -196,30 +219,56 @@
     return notes.astype(F32)
 
 
-def widen(object_field, from_first, from_second, first, second_out, middle):
+def sides(odd, one, two):
+    return jnp.where(odd == 1, one, two), jnp.where(odd == 1, two, one)
+
+
+def edges(object_field, first, second, own_first, own_second):
+    window = object_field.shape[-1]
+    half = window // 2
+    odd_x = lax.rem(lax.axis_index("gx"), 2)
+    odd_y = lax.rem(lax.axis_index("gy"), 2)
+    for ref, odd in ((first, 1 - odd_x), (second, odd_x)):
+        ref[...] = object_field[1, :, :, pl.ds(pl.multiple_of(odd * half, half), half)]
+    for ref, odd in ((own_first, 1 - odd_y), (own_second, odd_y)):
+        ref[...] = object_field[1, :, pl.ds(pl.multiple_of(odd * half, half), half), :]
+
+
+def relay(from_first, from_second, first, second):
     half = from_first.shape[-1]
     odd_x = lax.rem(lax.axis_index("gx"), 2)
     odd_y = lax.rem(lax.axis_index("gy"), 2)
-    at_first = pl.ds(pl.multiple_of((1 - odd_x) * 3 * half, half), half)
-    at_second = pl.ds(pl.multiple_of(odd_x * 3 * half, half), half)
-    for plane in range(middle.shape[0]):
-        middle[plane, :, half : 3 * half] = object_field[1, plane]
-        middle[plane, :, at_first] = from_first[plane]
-        middle[plane, :, at_second] = from_second[plane]
-        for ref, base in ((first, (1 - odd_y) * half), (second_out, odd_y * half)):
-            ref[plane] = middle[plane, pl.ds(pl.multiple_of(base, half), half), :]
+    at_first = pl.ds(pl.multiple_of((1 - odd_x) * half, half), half)
+    at_second = pl.ds(pl.multiple_of(odd_x * half, half), half)
+    for ref, base in ((first, (1 - odd_y) * half), (second, odd_y * half)):
+        rows = pl.ds(pl.multiple_of(base, half), half)
+        for plane in range(ref.shape[0]):
+            ref[plane, :, at_first] = from_first[plane, rows]
+            ref[plane, :, at_second] = from_second[plane, rows]
 
 
 def propagate(
-    pos, field, probes, middle_in, from_first, from_second, table_hi, table_lo,
-    first, second, middle,
+    marks, field, probes, object_field, halo_first, halo_second,
+    own_first, own_second, corner_first, corner_second, table,
+    outer_first, outer_second, inner_first, inner_second, middle,
     chi_hi, chi_lo, grads,
 ):
     window = field.shape[-1]
     half = window // 2
     count = field.shape[0]
+    odd_x = lax.rem(lax.axis_index("gx"), 2)
     odd = lax.rem(lax.axis_index("gy"), 2)
-    corners = corners_of(pos, count)
+    corners = [(marks[2 * number, :1], marks[2 * number + 1, :1]) for number in range(count)]
+    table_hi, table_lo = table.at[2], table.at[3]
+
+    def wide(part, rows):
+        left, right = sides(odd_x, halo_first[part, rows], halo_second[part, rows])
+        return jnp.concatenate([left, object_field[1, part, rows], right], axis=1)
+
+    def beyond(part, rows, below):
+        own = sides(odd, own_first[part, rows], own_second[part, rows])[below]
+        corner = sides(odd, corner_first[part, rows], corner_second[part, rows])[below]
+        return jnp.concatenate([corner[:, :half], own, corner[:, half:]], axis=1)
 
     for start in range(0, window, CHUNK):
         rows = slice(start, start + CHUNK)
@@ -228,12 +277,12 @@
         upper, lower = [], []
         for part in range(2):
             if start < half:
-                upper.append(jnp.where(odd == 1, from_first[part, rows], from_second[part, rows]))
-                lower.append(middle_in[part, half + start : half + start + CHUNK])
+                upper.append(beyond(part, rows, 0))
+                lower.append(wide(part, slice(half + start, half + start + CHUNK)))
             else:
                 shifted = slice(start - half, start - half + CHUNK)
-                upper.append(middle_in[part, shifted])
-                lower.append(jnp.where(odd == 1, from_second[part, shifted], from_first[part, shifted]))
+                upper.append(wide(part, shifted))
+                lower.append(beyond(part, shifted, 1))
         for number, (r, c) in enumerate(corners):
             low_row, low_col = row < r, col < c
             patch = []
@@ -258,7 +307,9 @@
         probe_re, probe_im = probes[number, 0], probes[number, 1]
         grads[0, number] = probe_re * back_re + probe_im * back_im
         grads[1, number] = probe_re * back_im - probe_im * back_re
-    place([grads.at[0], grads.at[1]], corners, first, second, middle, odd, window)
+    place(
+        [grads.at[0], grads.at[1]], corners, (outer_first, inner_first), (outer_second, inner_second), middle, odd, window
+    )
 
 
 def illuminate(pos, probe, up, down, first, second, scale, twice, notes, sems):
@@ -318,7 +369,7 @@
     lax.fori_loop(0, window // CHUNK, rows_at, 0)
 
 
-def narrow(pos, middle, from_first, from_second, first, second, centre):
+def narrow(notes, middle, from_first, from_second, first, second, centre):
     half = first.shape[-1]
     window = 2 * half
     odd_x = lax.rem(lax.axis_index("gx"), 2)
@@ -329,18 +380,26 @@
             for received, base in ((from_first, (1 - odd_y) * half), (from_second, odd_y * half)):
                 at = pl.ds(pl.multiple_of(base + start, CHUNK), CHUNK)
                 total = middle[plane, at, :] + received[plane, rows]
-                left, right = total[:, :half], total[:, 3 * half :]
                 centre[plane, at, :] = total[:, half : 3 * half]
-                first[plane, at, :] = jnp.where(odd_x == 1, left, right)
-                second[plane, at, :] = jnp.where(odd_x == 1, right, left)
-    if first.shape[1] > window:
-        size = from_first.shape[1] - half
-        above = jnp.where(odd_y == 1, from_first[0, half:, :half], from_second[0, half:, :half])
-        below = jnp.where(odd_y == 1, from_second[0, half:, :half], from_first[0, half:, :half])
-        for ref in (first, second):
-            ref[0, window : window + size] = above
-            ref[0, window + size : window + 2 * size] = notes_of(pos, pos.shape[0], half)
-            ref[0, window + 2 * size :] = below
+                second[plane, at, :], first[plane, at, :] = sides(odd_x, total[:, 3 * half :], total[:, :half])
+    size = notes.shape[0]
+    above, below = sides(odd_y, from_first[0, half:, :half], from_second[0, half:, :half])
+    for ref in (first, second):
+        ref[0, window : window + size] = above
+        ref[0, window + size : window + 2 * size] = notes[...]
+        ref[0, window + 2 * size :] = below
+
+
+def narrow_outer(middle, from_first, from_second, first, second):
+    half = first.shape[-1]
+    odd_x = lax.rem(lax.axis_index("gx"), 2)
+    odd_y = lax.rem(lax.axis_index("gy"), 2)
+    for plane in range(middle.shape[0]):
+        for received, base in ((from_first, (1 - odd_y) * half), (from_second, odd_y * half)):
+            at = pl.ds(pl.multiple_of(base, half), half)
+            left = middle[plane, at, :half] + received[plane, :, :half]
+            right = middle[plane, at, 3 * half :] + received[plane, :, half:]
+            second[plane, at, :], first[plane, at, :] = sides(odd_x, right, left)
 
 
 def join(centre, from_first, from_second, out):
@@ -353,27 +412,29 @@
             out[plane, :, at] = centre[plane, :, at] + received[plane, :window]
 
 
-def update(object_field, scale, total2, centre1, first1, second1, out):
-    window = centre1.shape[-1]
-    half = window // 2
-    odd_x = lax.rem(lax.axis_index("gx"), 2)
+def update(first1, second1, object_field, scale, total2, middle1, inner_first, inner_second, out):
+    window = scale.shape[-1]
+    half = window // 2
+    odd_x = lax.rem(lax.axis_index("gx"), 2)
+    odd_y = lax.rem(lax.axis_index("gy"), 2)
     for part in range(2):
         out[1, part] = object_field[1, part] - total2[part] * scale[...]
-        for received, base in ((first1, (1 - odd_x) * half), (second1, odd_x * half)):
-            at = pl.ds(pl.multiple_of(base, half), half)
-            total = centre1[part, :, at] + received[part]
-            out[0, part, :, at] = object_field[0, part, :, at] - total * scale[:, at]
+        for received, base in ((inner_first, (1 - odd_y) * half), (inner_second, odd_y * half)):
+            rows = pl.ds(pl.multiple_of(base, half), half)
+            outer = jnp.concatenate(sides(odd_x, first1[part, rows], second1[part, rows]), axis=1)
+            total = middle1[part, rows, half : 3 * half] + received[part] + outer
+            out[0, part, rows] = object_field[0, part, rows] - total * scale[rows]
 
 
 VMEM = pl.BlockSpec(memory_space=pltpu.VMEM)
 SMEM = pl.BlockSpec(memory_space=pltpu.SMEM)
-HBM = pl.BlockSpec(memory_space=pltpu.HBM)
+ANY = pl.BlockSpec(memory_space=pl.ANY)
 
 
 def call(body, outs, in_specs, args, scratch=(), micros=0.0, name=None):
     return pl.pallas_call(
         body,
-        out_shape=[jax.ShapeDtypeStruct(shape, F32) for shape in outs],
+        out_shape=[x if hasattr(x, "dtype") else jax.ShapeDtypeStruct(x, F32) for x in outs],
         in_specs=in_specs,
         out_specs=[VMEM] * len(outs),
         scratch_shapes=list(scratch),
@@ -388,110 +449,104 @@
     half = window // 2
     count = positions.shape[0]
     size = notes_size(count)
-    wave_hi, wave_lo, move_hi, move_lo = (jnp.asarray(t) for t in tables(window))
+    table = jnp.asarray(tables(window))
     barrier = lax.optimization_barrier
 
-    def twice(planes):
+    def twice(*planes):
         return pltpu.VMEM((*planes, 2 * window + 8, window), F32)
 
     grads = pltpu.VMEM((2, count, window, window), F32)
+    pos_scratch = [pltpu.SMEM(positions.shape, jnp.int32), pltpu.SemaphoreType.DMA]
     fields_shape = (count, 2, window, window)
-
-    def pieces(planes, extra=0):
-        return [(planes, half + extra, 2 * window), (planes, half + extra, 2 * window), (planes, window, 2 * window)]
-
-    def strips(planes, extra=0):
-        return [(planes, window + extra, half), (planes, window + extra, half), (planes, window, window)]
-
-    odd_x = lax.rem(lax.axis_index("gx"), 2)
-    left, right = object_field[1, :, :, :half], object_field[1, :, :, half:]
-    first0 = jnp.where(odd_x == 1, left, right)
-    second0 = jnp.where(odd_x == 1, right, left)
-    halo_first = swapped(first0, "gx", 0)
-    halo_second = swapped(second0, "gx", 1)
-
-    field, up2, down2, middle2 = call(
+    wide_shape = (2, window, 2 * window)
+    square, strip = (2, half, window), (2, window, half)
+
+    edge_first, edge_second, rows_first, rows_second = call(
+        edges, [strip] * 2 + [square] * 2, [VMEM], (object_field,), micros=0.2, name="edges"
+    )
+    halo_first = swapped(edge_first, "gx", 0)
+    halo_second = swapped(edge_second, "gx", 1)
+
+    field, up2, down2, middle2, notes, marks = call(
         detect,
-        [fields_shape] + pieces(2, size),
-        [SMEM] + [VMEM] * 4,
-        (positions, residual, saved_wave, wave_hi, wave_lo),
-        [twice((count, 2)), grads],
+        [fields_shape]
+        + [(2, half + size, 2 * window)] * 2
+        + [wide_shape, (size, half), jax.ShapeDtypeStruct((2 * count, 8, window), jnp.int32)],
+        [ANY] + [VMEM] * 3,
+        (positions, residual, saved_wave, table),
+        [twice(count, 2), grads] + pos_scratch,
         micros=12.0, name="detect",
     )
+    up2, down2, rows_first, rows_second = barrier((up2, down2, rows_first, rows_second))
     from_up2 = swapped(up2, "gy", 0)
     from_down2 = swapped(down2, "gy", 1)
-
-    halo_first, halo_second, field = barrier((halo_first, halo_second, field))
+    own_first = swapped(rows_first, "gy", 0)
+    own_second = swapped(rows_second, "gy", 1)
+
     fields, probes = call(
         roll_fields,
         [fields_shape] * 2,
-        [SMEM] + [VMEM] * 2,
+        [ANY] + [VMEM] * 2,
         (positions, field, probe),
-        [twice((count + 1, 2))],
-        micros=12.0, name="roll",
-    )
-
-    halo_first, halo_second, fields, probes, from_up2, from_down2 = barrier(
-        (halo_first, halo_second, fields, probes, from_up2, from_down2)
-    )
-    up0, down0, wide0 = call(
-        widen,
-        pieces(2),
-        [VMEM] * 3,
-        (object_field, halo_first, halo_second),
-        micros=0.2, name="widen",
-    )
-    from_up0 = swapped(up0, "gy", 0)
-    from_down0 = swapped(down0, "gy", 1)
-
+        [twice(count + 1, 2)] + pos_scratch,
+        micros=0.1, name="roll",
+    )
+    corner0_first, corner0_second = call(
+        relay, [square] * 2, [VMEM] * 2, (halo_first, halo_second), micros=12.0, name="widen"
+    )
+    from_corner0_first = swapped(corner0_first, "gy", 0)
+    from_corner0_second = swapped(corner0_second, "gy", 1)
+
+    from_up2, from_down2, own_first, own_second, fields, probes = barrier(
+        (from_up2, from_down2, own_first, own_second, fields, probes)
+    )
     first2, second2, centre2 = call(
         narrow,
-        strips(2, 3 * size),
-        [SMEM] + [VMEM] * 3,
-        (positions, middle2, from_up2, from_down2),
+        [(2, window + 3 * size, half)] * 2 + [fields_shape[1:]],
+        [VMEM] * 4,
+        (notes, middle2, from_up2, from_down2),
         micros=0.2, name="narrow2",
     )
-    from_up0, from_down0, first2, second2, centre2 = barrier((from_up0, from_down0, first2, second2, centre2))
+    from_corner0_first, from_corner0_second, first2, second2, centre2 = barrier(
+        (from_corner0_first, from_corner0_second, first2, second2, centre2)
+    )
     got_first2 = swapped(first2, "gx", 0)
     got_second2 = swapped(second2, "gx", 1)
 
-    up1, down1, middle1 = call(
+    outer_first, outer_second, inner_first, inner_second, middle1 = call(
         propagate,
-        pieces(2),
-        [SMEM] + [VMEM] * 7,
-        (positions, fields, probes, wide0, from_up0, from_down0, move_hi, move_lo),
+        [square] * 4 + [wide_shape],
+        [VMEM] * 11,
+        (marks, fields, probes, object_field, halo_first, halo_second, own_first, own_second)
+        + (from_corner0_first, from_corner0_second, table),
         [pltpu.VMEM(fields_shape, BF16)] * 2 + [grads],
-        micros=12.0, name="propagate",
-    )
-    from_up1 = swapped(up1, "gy", 0)
-    from_down1 = swapped(down1, "gy", 1)
-    (total2,) = call(
-        join, [centre2.shape], [VMEM] * 3, (centre2, got_first2, got_second2), micros=12.0, name="join2"
-    )
-    middle1, total2 = barrier((middle1, total2))
-    first1, second1, centre1 = call(
-        narrow,
-        strips(2),
-        [SMEM] + [VMEM] * 3,
-        (positions, middle1, from_up1, from_down1),
-        micros=0.2, name="narrow1",
-    )
+        micros=0.1, name="propagate",
+    )
+    from_outer_first = swapped(outer_first, "gy", 0)
+    from_outer_second = swapped(outer_second, "gy", 1)
+    (total2,) = call(join, [centre2.shape], [VMEM] * 3, (centre2, got_first2, got_second2), micros=12.0, name="join2")
+    first1, second1 = call(
+        narrow_outer, [strip] * 2, [VMEM] * 3, (middle1, from_outer_first, from_outer_second), micros=0.2, name="narrow1"
+    )
+    first1, second1, inner_first, inner_second = barrier((first1, second1, inner_first, inner_second))
     got_first1 = swapped(first1, "gx", 0)
     got_second1 = swapped(second1, "gx", 1)
+    from_inner_first = swapped(inner_first, "gy", 0)
+    from_inner_second = swapped(inner_second, "gy", 1)
 
     (scale,) = call(
         illuminate,
         [(window, window)],
         [SMEM] + [VMEM] * 5,
         (positions, probe, from_up2, from_down2, got_first2, got_second2),
-        [twice(()), pltpu.SMEM((8 * size, half), F32), pltpu.SemaphoreType.DMA((4,))],
-        micros=2.0, name="illuminate",
+        [twice(), pltpu.SMEM((8 * size, half), F32), pltpu.SemaphoreType.DMA((4,))],
+        micros=12.0, name="illuminate",
     )
     (new_object,) = call(
         update,
         [object_field.shape],
-        [VMEM] * 6,
-        (object_field, scale, total2, centre1, got_first1, got_second1),
+        [VMEM] * 8,
+        (got_first1, got_second1, object_field, scale, total2, middle1, from_inner_first, from_inner_second),
         micros=1.0, name="update",
     )
     return new_object

time: 67.4 us -> 58.3 us (0.86)
  waiting for transfers between devices: 25.6 us -> 12.5 us
  starting transfers between devices: 22.7 us -> 28.5 us
  Pallas kernels: 15.5 us -> 13.2 us
  local copies, waits for them, and re-layouts: 1.93 us -> 3.32 us
  other arithmetic: 1.15 us -> 0 us
    ppermute x12 -> x16, waiting for transfers between devices: 25.6 us -> 12.5 us  [swapped(): return lax.ppermute(value, axis, swap_pairs(lax.axis_size(axis), first))]
    ppermute x12 -> x16, starting transfers between devices: 22.7 us -> 28.5 us  [swapped(): return lax.ppermute(value, axis, swap_pairs(lax.axis_size(axis), first))]
    pallas_call x9 -> x10, Pallas kernels: 15.5 us -> 13.2 us  [call(): pl.pallas_call(body, out_shape=[x if hasattr(x, 'dtype') else jax.ShapeDt...]
    unnamed x18 -> x14, local copies, waits for them, and re-layouts: 1.93 us -> 3.32 us
    select_n x1 -> x0, other arithmetic: 1.15 us -> none  [shards(): second0 = jnp.where(odd_x == 1, right, left)]
  transfers between devices with their start and end apart: 12 -> 16, of which waited for: 5 -> 4; matrix products, arithmetic and copies ran while one was open for 0% -> 0% of each run, Pallas kernels for 20% -> 21%
where the time goes in v3:
time: 58.3 us; the launch traced here: 57.9 us
  starting transfers between devices  28.5 us (49%)
  Pallas kernels  13.2 us (23%)
  waiting for transfers between devices  12.5 us (21%)
  local copies, waits for them, and re-layouts  3.32 us (6%)
    ppermute x16, starting transfers between devices, swapped(): return lax.ppermute(value, axis, swap_pairs(lax.axis_size(axis), first))  28.5 us
    pallas_call x10, Pallas kernels, call(): pl.pallas_call(body, out_shape=[x if hasattr(x, 'dtype') else jax.ShapeDt...  13.2 us
    ppermute x16, waiting for transfers between devices, swapped(): return lax.ppermute(value, axis, swap_pairs(lax.axis_size(axis), first))  12.5 us
    unnamed x14, local copies, waits for them, and re-layouts  3.32 us
  transfers between devices with their start and end apart: 16, of which 4 were waited for; matrix products, arithmetic and copies ran while one was open for 0% of the time, Pallas kernels for 21%

profile of v3, /device:TPU:11, one launch (start us, length us, event | category | flops | bytes accessed | tf_op | source)
XLA Modules:
  0.0 57.9 jit_solution(8839035310755374222)
XLA Ops:
  0.0 0.0 copy-start
  0.0 1.2 %copy-done = f32[2,2,256,256]{3,2,1,0:T(8,128)S(1)} copy-done((f32[2,2,256,256]{3,2,1,0:T(8,128)S(1)}, f32[2,2,256,256]{3,2,1,0:T(8,128)}, u32[]{:S(2)}) %copy-start) | copy-done | bytes 1048600
  1.2 0.0 copy-start.2
  1.2 0.1 edges.1
  1.3 0.0 copy-start.4
  1.3 0.3 collective-permute-start.4
  1.6 4.1 %collective-permute-start.5 = (f32[2,256,128]{2,1,0:T(8,128)S(1)}, f32[2,256,128]{2,1,0:T(8,128)S(1)}, u32[]{:S(2)}, u32[]{:S(2)}) collective-permute-start(f32[2,256,128]{2,1,0:T(8,128)S(1)} %get-tuple-element.63), channel_id=1, source_target_pairs={{8,16},{16,8},{9,17},{17,9},{10,18},{18,10},{11,19},{19,11},{12,20... | collective-permute-start | bytes 786440 | tf_op jit(solution)/shard_map/ppermute | solution.py:45
  5.7 0.0 copy-done.2
  5.7 0.0 copy-done.4
  5.7 0.0 copy-start.5
  5.7 1.0 %copy-done.5 = bf16[2,1,2,256,256]{4,3,2,1,0:T(8,128)(2,1)S(1)} copy-done((bf16[2,1,2,256,256]{4,3,2,1,0:T(8,128)(2,1)S(1)}, bf16[2,1,2,256,256]{4,3,2,1,0:T(8,128)(2,1)}, u32[]{:S(2)}) %copy-start.5) | copy-done | bytes 524312
  6.8 0.0 copy-start.6
  6.8 1.0 %copy-done.6 = bf16[2,1,2,256,256]{4,3,2,1,0:T(8,128)(2,1)S(1)} copy-done((bf16[2,1,2,256,256]{4,3,2,1,0:T(8,128)(2,1)S(1)}, bf16[2,1,2,256,256]{4,3,2,1,0:T(8,128)(2,1)}, u32[]{:S(2)}) %copy-start.6) | copy-done | bytes 524312
  7.8 2.9 %detect.1 = (f32[2,2,256,256]{3,2,1,0:T(8,128)S(1)}, f32[2,136,512]{2,1,0:T(8,128)S(1)}, f32[2,136,512]{2,1,0:T(8,128)S(1)}, f32[2,256,512]{2,1,0:T(8,128)S(1)},...) custom-call(s32[2,1,2]{2,1,0:T(1,128)S(1)} %copy-done.4, bf16[2,1,2,256,256]{4,3,2,1,0:T(8,128)(2,1)S(1)} %copy-done.5, ...), custom_call_target="tpu_custom_call" | custom-call | flops 12000000000 | bytes 1 | tf_op jit(solution)/shard_map/detect/pallas_call | solution.py:435
  10.7 0.0 copy-start.3
  10.7 1.3 %collective-permute-start = (f32[2,136,512]{2,1,0:T(8,128)S(1)}, f32[2,136,512]{2,1,0:T(8,128)S(1)}, u32[]{:S(2)}, u32[]{:S(2)}) collective-permute-start(f32[2,136,512]{2,1,0:T(8,128)S(1)} %get-tuple-element.53), channel_id=1, source_target_pairs={{0,1},{1,0},{2,3},{3,2},{4,5},{5,4},{6,7},{7,6},{8,9},{9,8},{10,11... | collective-permute-start | bytes 1671176 | tf_op jit(solution)/shard_map/ppermute | solution.py:45
  12.0 3.2 %collective-permute-start.1 = (f32[2,136,512]{2,1,0:T(8,128)S(1)}, f32[2,136,512]{2,1,0:T(8,128)S(1)}, u32[]{:S(2)}, u32[]{:S(2)}) collective-permute-start(f32[2,136,512]{2,1,0:T(8,128)S(1)} %get-tuple-element.54), channel_id=1, source_target_pairs={{1,2},{2,1},{3,4},{4,3},{5,6},{6,5},{9,10},{10,9},{11,12},{12,11},... | collective-permute-start | bytes 1671176 | tf_op jit(solution)/shard_map/ppermute | solution.py:45
  15.3 0.1 collective-permute-start.2
  15.3 0.0 collective-permute-done.4.from_first.halo_first
  15.4 3.6 %collective-permute-start.3 = (f32[2,128,256]{2,1,0:T(8,128)S(1)}, f32[2,128,256]{2,1,0:T(8,128)S(1)}, u32[]{:S(2)}, u32[]{:S(2)}) collective-permute-start(f32[2,128,256]{2,1,0:T(8,128)S(1)} %get-tuple-element.56), channel_id=1, source_target_pairs={{1,2},{2,1},{3,4},{4,3},{5,6},{6,5},{9,10},{10,9},{11,12},{12,11},... | collective-permute-start | bytes 786440 | tf_op jit(solution)/shard_map/ppermute | solution.py:45
  18.9 0.0 collective-permute-done.5.from_second.halo_second
  18.9 0.1 widen.1
  19.0 0.1 collective-permute-start.6
  19.1 0.0 collective-permute-done.2.own_first
  19.1 2.3 %collective-permute-start.7 = (f32[2,128,256]{2,1,0:T(8,128)S(1)}, f32[2,128,256]{2,1,0:T(8,128)S(1)}, u32[]{:S(2)}, u32[]{:S(2)}) collective-permute-start(f32[2,128,256]{2,1,0:T(8,128)S(1)} %get-tuple-element.67), channel_id=1, source_target_pairs={{1,2},{2,1},{3,4},{4,3},{5,6},{6,5},{9,10},{10,9},{11,12},{12,11},... | collective-permute-start | bytes 786440 | tf_op jit(solution)/shard_map/ppermute | solution.py:45
  21.4 0.0 copy-done.3
  21.4 1.2 %roll.1 = (f32[2,2,256,256]{3,2,1,0:T(8,128)S(1)}, f32[2,2,256,256]{3,2,1,0:T(8,128)S(1)}) custom-call(s32[2,1,2]{2,1,0:T(1,128)S(1)} %copy-done.4, f32[2,2,256,256]{3,2,1,0:T(8,128)S(1)} %get-tuple-element.57.field, f32[2,256,256]{2,1,0:T(8,128)S(1)} %copy-done.3), custom_call_target="tpu_custom_call" | custom-call | flops 100000000 | bytes 1 | tf_op jit(solution)/shard_map/roll/pallas_call | solution.py:435
  22.6 3.3 %collective-permute-done.3.own_second = f32[2,128,256]{2,1,0:T(8,128)S(1)} collective-permute-done((f32[2,128,256]{2,1,0:T(8,128)S(1)}, f32[2,128,256]{2,1,0:T(8,128)S(1)}, u32[]{:S(2)}, u32[]{:S(2)}) %collective-permute-start.3) | collective-permute-done | bytes 262176 | tf_op jit(solution)/shard_map/ppermute | solution.py:45
  26.0 0.0 collective-permute-done.from_first.up
  26.0 0.0 collective-permute-done.1.from_second.down
  26.0 0.0 copy-start.1
  26.0 0.1 narrow2.1
  26.1 0.0 collective-permute-done.6.corner_first
  26.1 2.3 %collective-permute-done.7.corner_second = f32[2,128,256]{2,1,0:T(8,128)S(1)} collective-permute-done((f32[2,128,256]{2,1,0:T(8,128)S(1)}, f32[2,128,256]{2,1,0:T(8,128)S(1)}, u32[]{:S(2)}, u32[]{:S(2)}) %collective-permute-start.7) | collective-permute-done | bytes 262176 | tf_op jit(solution)/shard_map/ppermute | solution.py:45
  28.5 0.0 collective-permute-start.12
  28.5 2.1 %collective-permute-start.13 = (f32[2,280,128]{2,1,0:T(8,128)S(1)}, f32[2,280,128]{2,1,0:T(8,128)S(1)}, u32[]{:S(2)}, u32[]{:S(2)}) collective-permute-start(f32[2,280,128]{2,1,0:T(8,128)S(1)} %get-tuple-element.87), channel_id=1, source_target_pairs={{8,16},{16,8},{9,17},{17,9},{10,18},{18,10},{11,19},{19,11},{12,20... | collective-permute-start | bytes 860168 | tf_op jit(solution)/shard_map/ppermute | solution.py:45
  30.6 0.0 copy-done.1
  30.6 2.9 %propagate.1 = (f32[2,128,256]{2,1,0:T(8,128)S(1)}, f32[2,128,256]{2,1,0:T(8,128)S(1)}, f32[2,128,256]{2,1,0:T(8,128)S(1)}, f32[2,128,256]{2,1,0:T(8,128)S(1)}, f32[2,256,512]{2,1,0:T(8,128)S(1)}) custom-call(s32[4,8,256]{2,1,0:T(8,128)S(1)} %get-tuple-element.48.marks, f32[2,2,256,256]{3,2,1,0:T(8,128)S(1)} %get-tuple-element.60.field, ...), custom_call_target="tpu_custom_call" | custom-call | flops 100000000 | bytes 1 | tf_op jit(solution)/shard_map/propagate/pallas_call | solution.py:435
  33.5 0.5 collective-permute-start.8
  34.0 3.2 %collective-permute-start.9 = (f32[2,128,256]{2,1,0:T(8,128)S(1)}, f32[2,128,256]{2,1,0:T(8,128)S(1)}, u32[]{:S(2)}, u32[]{:S(2)}) collective-permute-start(f32[2,128,256]{2,1,0:T(8,128)S(1)} %get-tuple-element.79), channel_id=1, source_target_pairs={{1,2},{2,1},{3,4},{4,3},{5,6},{6,5},{9,10},{10,9},{11,12},{12,11},... | collective-permute-start | bytes 786440 | tf_op jit(solution)/shard_map/ppermute | solution.py:45
  37.2 0.0 collective-permute-done.8.from_first
  37.2 4.8 %collective-permute-done.9.from_second = f32[2,128,256]{2,1,0:T(8,128)S(1)} collective-permute-done((f32[2,128,256]{2,1,0:T(8,128)S(1)}, f32[2,128,256]{2,1,0:T(8,128)S(1)}, u32[]{:S(2)}, u32[]{:S(2)}) %collective-permute-start.9) | collective-permute-done | bytes 262176 | tf_op jit(solution)/shard_map/ppermute | solution.py:45
  42.0 0.1 narrow1.1
  42.1 0.1 collective-permute-start.10
  42.1 4.1 %collective-permute-start.11 = (f32[2,256,128]{2,1,0:T(8,128)S(1)}, f32[2,256,128]{2,1,0:T(8,128)S(1)}, u32[]{:S(2)}, u32[]{:S(2)}) collective-permute-start(f32[2,256,128]{2,1,0:T(8,128)S(1)} %get-tuple-element.85), channel_id=1, source_target_pairs={{8,16},{16,8},{9,17},{17,9},{10,18},{18,10},{11,19},{19,11},{12,20... | collective-permute-start | bytes 786440 | tf_op jit(solution)/shard_map/ppermute | solution.py:45
  46.2 0.1 collective-permute-start.14
  46.4 0.0 collective-permute-done.12.first.from_first
  46.4 3.5 %collective-permute-start.15 = (f32[2,128,256]{2,1,0:T(8,128)S(1)}, f32[2,128,256]{2,1,0:T(8,128)S(1)}, u32[]{:S(2)}, u32[]{:S(2)}) collective-permute-start(f32[2,128,256]{2,1,0:T(8,128)S(1)} %get-tuple-element.90), channel_id=1, source_target_pairs={{1,2},{2,1},{3,4},{4,3},{5,6},{6,5},{9,10},{10,9},{11,12},{12,11},... | collective-permute-start | bytes 786440 | tf_op jit(solution)/shard_map/ppermute | solution.py:45
  49.9 0.0 collective-permute-done.13.second.from_second
  49.9 4.6 %illuminate.1.scale = f32[256,256]{1,0:T(8,128)S(1)} custom-call(s32[2,1,2]{2,1,0:T(1,128)S(1)} %copy-done.4, f32[2,256,256]{2,1,0:T(8,128)S(1)} %copy-done.3, f32[2,136,512]{2,1,0:T(8,128)S(1)} %collective-permute-done.from_first.up, f32[2,136,512]{2,1,0:T(8,128)S(1)} %collective-permute-done.1.from_second.down, ...), custom_call_target="tpu_custom_call" | custom-call | flops 12000000000 | bytes 1 | tf_op jit(solution)/shard_map/illuminate/pallas_call | solution.py:435
  54.6 0.1 join2.1.total2
  54.7 0.0 collective-permute-done.10.first1
  54.7 2.0 %collective-permute-done.11.second1 = f32[2,256,128]{2,1,0:T(8,128)S(1)} collective-permute-done((f32[2,256,128]{2,1,0:T(8,128)S(1)}, f32[2,256,128]{2,1,0:T(8,128)S(1)}, u32[]{:S(2)}, u32[]{:S(2)}) %collective-permute-start.11) | collective-permute-done | bytes 262176 | tf_op jit(solution)/shard_map/ppermute | solution.py:45
  56.7 0.0 collective-permute-done.14.inner_first
  56.7 0.0 collective-permute-done.15.inner_second
  56.7 1.2 %update.1 = f32[2,2,256,256]{3,2,1,0:T(8,128)} custom-call(f32[2,256,128]{2,1,0:T(8,128)S(1)} %collective-permute-done.10.first1, f32[2,256,128]{2,1,0:T(8,128)S(1)} %collective-permute-done.11.second1, f32[2,2,256,256]{3,2,1,0:T(8,128)S(1)} %copy-done.1, f32[256,256]{1,0:T(8,128)S(1)} %illuminate.1.scale, f32[2,256,256]{2,1,0:T(8,128)S(1)} %join2.1.total2, ...), custom_call_target="tpu_custom_call" | custom-call | flops 1000000000 | bytes 1 | tf_op jit(solution)/shard_map/update/pallas_call | solution.py:435
Async XLA Ops:
  0.0 1.2 %copy-start = (f32[2,2,256,256]{3,2,1,0:T(8,128)S(1)}, f32[2,2,256,256]{3,2,1,0:T(8,128)}, u32[]{:S(2)}) copy-start(f32[2,2,256,256]{3,2,1,0:T(8,128)} %object_field.5) | copy-start | bytes 3145732
  1.2 4.5 %copy-start.2 = (bf16[4,256,512]{2,1,0:T(8,128)(2,1)S(1)}, bf16[4,256,512]{2,1,0:T(8,128)(2,1)}, u32[]{:S(2)}) copy-start(bf16[4,256,512]{2,1,0:T(8,128)(2,1)} %constant.2.clone.table) | copy-start | bytes 3145732
  1.3 4.4 %copy-start.4 = (s32[2,1,2]{2,1,0:T(1,128)S(1)}, s32[2,1,2]{2,1,0:T(1,128)}, u32[]{:S(2)}) copy-start(s32[2,1,2]{2,1,0:T(1,128)} %pos.1) | copy-start | bytes 52
  1.3 14.0 %collective-permute-start.4 = (f32[2,256,128]{2,1,0:T(8,128)S(1)}, f32[2,256,128]{2,1,0:T(8,128)S(1)}, u32[]{:S(2)}, u32[]{:S(2)}) collective-permute-start(f32[2,256,128]{2,1,0:T(8,128)S(1)} %get-tuple-element.62), channel_id=1, source_target_pairs={{0,8},{8,0},{16,24},{24,16},{1,9},{9,1},{17,25},{25,17},{2,10},{10... | collective-permute-start | bytes 786440 | tf_op jit(solution)/shard_map/ppermute | solution.py:45
  1.6 17.3 %collective-permute-start.5 = (f32[2,256,128]{2,1,0:T(8,128)S(1)}, f32[2,256,128]{2,1,0:T(8,128)S(1)}, u32[]{:S(2)}, u32[]{:S(2)}) collective-permute-start(f32[2,256,128]{2,1,0:T(8,128)S(1)} %get-tuple-element.63), channel_id=1, source_target_pairs={{8,16},{16,8},{9,17},{17,9},{10,18},{18,10},{11,19},{19,11},{12,20... | collective-permute-start | bytes 786440 | tf_op jit(solution)/shard_map/ppermute | solution.py:45
  5.7 1.0 %copy-start.5 = (bf16[2,1,2,256,256]{4,3,2,1,0:T(8,128)(2,1)S(1)}, bf16[2,1,2,256,256]{4,3,2,1,0:T(8,128)(2,1)}, u32[]{:S(2)}) copy-start(bf16[2,1,2,256,256]{4,3,2,1,0:T(8,128)(2,1)} %residual.1) | copy-start | bytes 1572868
  6.8 1.0 %copy-start.6 = (bf16[2,1,2,256,256]{4,3,2,1,0:T(8,128)(2,1)S(1)}, bf16[2,1,2,256,256]{4,3,2,1,0:T(8,128)(2,1)}, u32[]{:S(2)}) copy-start(bf16[2,1,2,256,256]{4,3,2,1,0:T(8,128)(2,1)} %wave.1) | copy-start | bytes 1572868
  10.7 10.7 %copy-start.3 = (f32[2,256,256]{2,1,0:T(8,128)S(1)}, f32[2,256,256]{2,1,0:T(8,128)}, u32[]{:S(2)}) copy-start(f32[2,256,256]{2,1,0:T(8,128)} %probe.3) | copy-start | bytes 1572868
  10.7 15.2 %collective-permute-start = (f32[2,136,512]{2,1,0:T(8,128)S(1)}, f32[2,136,512]{2,1,0:T(8,128)S(1)}, u32[]{:S(2)}, u32[]{:S(2)}) collective-permute-start(f32[2,136,512]{2,1,0:T(8,128)S(1)} %get-tuple-element.53), channel_id=1, source_target_pairs={{0,1},{1,0},{2,3},{3,2},{4,5},{5,4},{6,7},{7,6},{8,9},{9,8},{10,11... | collective-permute-start | bytes 1671176 | tf_op jit(solution)/shard_map/ppermute | solution.py:45
  12.0 13.9 %collective-permute-start.1 = (f32[2,136,512]{2,1,0:T(8,128)S(1)}, f32[2,136,512]{2,1,0:T(8,128)S(1)}, u32[]{:S(2)}, u32[]{:S(2)}) collective-permute-start(f32[2,136,512]{2,1,0:T(8,128)S(1)} %get-tuple-element.54), channel_id=1, source_target_pairs={{1,2},{2,1},{3,4},{4,3},{5,6},{6,5},{9,10},{10,9},{11,12},{12,11},... | collective-permute-start | bytes 1671176 | tf_op jit(solution)/shard_map/ppermute | solution.py:45
  15.3 3.8 %collective-permute-start.2 = (f32[2,128,256]{2,1,0:T(8,128)S(1)}, f32[2,128,256]{2,1,0:T(8,128)S(1)}, u32[]{:S(2)}, u32[]{:S(2)}) collective-permute-start(f32[2,128,256]{2,1,0:T(8,128)S(1)} %get-tuple-element.55), channel_id=1, source_target_pairs={{0,1},{1,0},{2,3},{3,2},{4,5},{5,4},{6,7},{7,6},{8,9},{9,8},{10,11... | collective-permute-start | bytes 786440 | tf_op jit(solution)/shard_map/ppermute | solution.py:45
  15.4 10.6 %collective-permute-start.3 = (f32[2,128,256]{2,1,0:T(8,128)S(1)}, f32[2,128,256]{2,1,0:T(8,128)S(1)}, u32[]{:S(2)}, u32[]{:S(2)}) collective-permute-start(f32[2,128,256]{2,1,0:T(8,128)S(1)} %get-tuple-element.56), channel_id=1, source_target_pairs={{1,2},{2,1},{3,4},{4,3},{5,6},{6,5},{9,10},{10,9},{11,12},{12,11},... | collective-permute-start | bytes 786440 | tf_op jit(solution)/shard_map/ppermute | solution.py:45
  19.0 7.1 %collective-permute-start.6 = (f32[2,128,256]{2,1,0:T(8,128)S(1)}, f32[2,128,256]{2,1,0:T(8,128)S(1)}, u32[]{:S(2)}, u32[]{:S(2)}) collective-permute-start(f32[2,128,256]{2,1,0:T(8,128)S(1)} %get-tuple-element.66), channel_id=1, source_target_pairs={{0,1},{1,0},{2,3},{3,2},{4,5},{5,4},{6,7},{7,6},{8,9},{9,8},{10,11... | collective-permute-start | bytes 786440 | tf_op jit(solution)/shard_map/ppermute | solution.py:45
  19.1 9.4 %collective-permute-start.7 = (f32[2,128,256]{2,1,0:T(8,128)S(1)}, f32[2,128,256]{2,1,0:T(8,128)S(1)}, u32[]{:S(2)}, u32[]{:S(2)}) collective-permute-start(f32[2,128,256]{2,1,0:T(8,128)S(1)} %get-tuple-element.67), channel_id=1, source_target_pairs={{1,2},{2,1},{3,4},{4,3},{5,6},{6,5},{9,10},{10,9},{11,12},{12,11},... | collective-permute-start | bytes 786440 | tf_op jit(solution)/shard_map/ppermute | solution.py:45
  26.0 4.6 %copy-start.1 = (f32[2,2,256,256]{3,2,1,0:T(8,128)S(1)}, f32[2,2,256,256]{3,2,1,0:T(8,128)}, u32[]{:S(2)}) copy-start(f32[2,2,256,256]{3,2,1,0:T(8,128)} %object_field.5) | copy-start | bytes 3145732
  28.5 17.9 %collective-permute-start.12 = (f32[2,280,128]{2,1,0:T(8,128)S(1)}, f32[2,280,128]{2,1,0:T(8,128)S(1)}, u32[]{:S(2)}, u32[]{:S(2)}) collective-permute-start(f32[2,280,128]{2,1,0:T(8,128)S(1)} %get-tuple-element.86), channel_id=1, source_target_pairs={{0,8},{8,0},{16,24},{24,16},{1,9},{9,1},{17,25},{25,17},{2,10},{10... | collective-permute-start | bytes 860168 | tf_op jit(solution)/shard_map/ppermute | solution.py:45
  28.5 21.4 %collective-permute-start.13 = (f32[2,280,128]{2,1,0:T(8,128)S(1)}, f32[2,280,128]{2,1,0:T(8,128)S(1)}, u32[]{:S(2)}, u32[]{:S(2)}) collective-permute-start(f32[2,280,128]{2,1,0:T(8,128)S(1)} %get-tuple-element.87), channel_id=1, source_target_pairs={{8,16},{16,8},{9,17},{17,9},{10,18},{18,10},{11,19},{19,11},{12,20... | collective-permute-start | bytes 860168 | tf_op jit(solution)/shard_map/ppermute | solution.py:45
  33.5 3.7 %collective-permute-start.8 = (f32[2,128,256]{2,1,0:T(8,128)S(1)}, f32[2,128,256]{2,1,0:T(8,128)S(1)}, u32[]{:S(2)}, u32[]{:S(2)}) collective-permute-start(f32[2,128,256]{2,1,0:T(8,128)S(1)} %get-tuple-element.78), channel_id=1, source_target_pairs={{0,1},{1,0},{2,3},{3,2},{4,5},{5,4},{6,7},{7,6},{8,9},{9,8},{10,11... | collective-permute-start | bytes 786440 | tf_op jit(solution)/shard_map/ppermute | solution.py:45
  34.0 8.0 %collective-permute-start.9 = (f32[2,128,256]{2,1,0:T(8,128)S(1)}, f32[2,128,256]{2,1,0:T(8,128)S(1)}, u32[]{:S(2)}, u32[]{:S(2)}) collective-permute-start(f32[2,128,256]{2,1,0:T(8,128)S(1)} %get-tuple-element.79), channel_id=1, source_target_pairs={{1,2},{2,1},{3,4},{4,3},{5,6},{6,5},{9,10},{10,9},{11,12},{12,11},... | collective-permute-start | bytes 786440 | tf_op jit(solution)/shard_map/ppermute | solution.py:45
  42.1 12.6 %collective-permute-start.10 = (f32[2,256,128]{2,1,0:T(8,128)S(1)}, f32[2,256,128]{2,1,0:T(8,128)S(1)}, u32[]{:S(2)}, u32[]{:S(2)}) collective-permute-start(f32[2,256,128]{2,1,0:T(8,128)S(1)} %get-tuple-element.84), channel_id=1, source_target_pairs={{0,8},{8,0},{16,24},{24,16},{1,9},{9,1},{17,25},{25,17},{2,10},{10... | collective-permute-start | bytes 786440 | tf_op jit(solution)/shard_map/ppermute | solution.py:45
  42.1 14.6 %collective-permute-start.11 = (f32[2,256,128]{2,1,0:T(8,128)S(1)}, f32[2,256,128]{2,1,0:T(8,128)S(1)}, u32[]{:S(2)}, u32[]{:S(2)}) collective-permute-start(f32[2,256,128]{2,1,0:T(8,128)S(1)} %get-tuple-element.85), channel_id=1, source_target_pairs={{8,16},{16,8},{9,17},{17,9},{10,18},{18,10},{11,19},{19,11},{12,20... | collective-permute-start | bytes 786440 | tf_op jit(solution)/shard_map/ppermute | solution.py:45
  46.2 10.5 %collective-permute-start.14 = (f32[2,128,256]{2,1,0:T(8,128)S(1)}, f32[2,128,256]{2,1,0:T(8,128)S(1)}, u32[]{:S(2)}, u32[]{:S(2)}) collective-permute-start(f32[2,128,256]{2,1,0:T(8,128)S(1)} %get-tuple-element.89), channel_id=1, source_target_pairs={{0,1},{1,0},{2,3},{3,2},{4,5},{5,4},{6,7},{7,6},{8,9},{9,8},{10,11... | collective-permute-start | bytes 786440 | tf_op jit(solution)/shard_map/ppermute | solution.py:45
  46.4 10.3 %collective-permute-start.15 = (f32[2,128,256]{2,1,0:T(8,128)S(1)}, f32[2,128,256]{2,1,0:T(8,128)S(1)}, u32[]{:S(2)}, u32[]{:S(2)}) collective-permute-start(f32[2,128,256]{2,1,0:T(8,128)S(1)} %get-tuple-element.90), channel_id=1, source_target_pairs={{1,2},{2,1},{3,4},{4,3},{5,6},{6,5},{9,10},{10,9},{11,12},{12,11},... | collective-permute-start | bytes 786440 | tf_op jit(solution)/shard_map/ppermute | solution.py:45

commit v4 on v3

--- a/solution.py
+++ b/solution.py
@@ -146,7 +146,9 @@
 
 
 def detect(
-    pos_any, residual, wave, table, field, first, second, middle, notes, marks, twice, grads, pos, sem
+    pos_any, residual, wave, table,
+    field, first, second, middle, notes, marks,
+    twice, grads, pos, sem,
 ):
     window = residual.shape[-1]
     count = residual.shape[0]
@@ -223,33 +225,30 @@
     return jnp.where(odd == 1, one, two), jnp.where(odd == 1, two, one)
 
 
-def edges(object_field, first, second, own_first, own_second):
-    window = object_field.shape[-1]
-    half = window // 2
-    odd_x = lax.rem(lax.axis_index("gx"), 2)
-    odd_y = lax.rem(lax.axis_index("gy"), 2)
+def edges(object_field, first, second):
+    half = object_field.shape[-1] // 2
+    odd_x = lax.rem(lax.axis_index("gx"), 2)
     for ref, odd in ((first, 1 - odd_x), (second, odd_x)):
         ref[...] = object_field[1, :, :, pl.ds(pl.multiple_of(odd * half, half), half)]
-    for ref, odd in ((own_first, 1 - odd_y), (own_second, odd_y)):
-        ref[...] = object_field[1, :, pl.ds(pl.multiple_of(odd * half, half), half), :]
-
-
-def relay(from_first, from_second, first, second):
+
+
+def relay(object_field, from_first, from_second, first, second):
     half = from_first.shape[-1]
     odd_x = lax.rem(lax.axis_index("gx"), 2)
     odd_y = lax.rem(lax.axis_index("gy"), 2)
-    at_first = pl.ds(pl.multiple_of((1 - odd_x) * half, half), half)
-    at_second = pl.ds(pl.multiple_of(odd_x * half, half), half)
+    at_first = pl.ds(pl.multiple_of((1 - odd_x) * 3 * half, half), half)
+    at_second = pl.ds(pl.multiple_of(odd_x * 3 * half, half), half)
     for ref, base in ((first, (1 - odd_y) * half), (second, odd_y * half)):
         rows = pl.ds(pl.multiple_of(base, half), half)
         for plane in range(ref.shape[0]):
+            ref[plane, :, half : 3 * half] = object_field[1, plane, rows]
             ref[plane, :, at_first] = from_first[plane, rows]
             ref[plane, :, at_second] = from_second[plane, rows]
 
 
 def propagate(
     marks, field, probes, object_field, halo_first, halo_second,
-    own_first, own_second, corner_first, corner_second, table,
+    rows_first, rows_second, table,
     outer_first, outer_second, inner_first, inner_second, middle,
     chi_hi, chi_lo, grads,
 ):
@@ -266,9 +265,7 @@
         return jnp.concatenate([left, object_field[1, part, rows], right], axis=1)
 
     def beyond(part, rows, below):
-        own = sides(odd, own_first[part, rows], own_second[part, rows])[below]
-        corner = sides(odd, corner_first[part, rows], corner_second[part, rows])[below]
-        return jnp.concatenate([corner[:, :half], own, corner[:, half:]], axis=1)
+        return sides(odd, rows_first[part, rows], rows_second[part, rows])[below]
 
     for start in range(0, window, CHUNK):
         rows = slice(start, start + CHUNK)
@@ -402,23 +399,23 @@
             second[plane, at, :], first[plane, at, :] = sides(odd_x, right, left)
 
 
-def join(centre, from_first, from_second, out):
+def join(centre, received, out, low):
     window = centre.shape[-1]
     half = window // 2
     odd_x = lax.rem(lax.axis_index("gx"), 2)
-    for plane in range(centre.shape[0]):
-        for received, base in ((from_first, (1 - odd_x) * half), (from_second, odd_x * half)):
-            at = pl.ds(pl.multiple_of(base, half), half)
-            out[plane, :, at] = centre[plane, :, at] + received[plane, :window]
-
-
-def update(first1, second1, object_field, scale, total2, middle1, inner_first, inner_second, out):
+    base = (odd_x if low else 1 - odd_x) * half
+    at = pl.ds(pl.multiple_of(base, half), half)
+    out[...] = centre[:, :, at] + received[:, :window]
+
+
+def update(first1, second1, object_field, scale, total2_first, total2_second, middle1, inner_first, inner_second, out):
     window = scale.shape[-1]
     half = window // 2
     odd_x = lax.rem(lax.axis_index("gx"), 2)
     odd_y = lax.rem(lax.axis_index("gy"), 2)
     for part in range(2):
-        out[1, part] = object_field[1, part] - total2[part] * scale[...]
+        total = jnp.concatenate(sides(odd_x, total2_first[part], total2_second[part]), axis=1)
+        out[1, part] = object_field[1, part] - total * scale[...]
         for received, base in ((inner_first, (1 - odd_y) * half), (inner_second, odd_y * half)):
             rows = pl.ds(pl.multiple_of(base, half), half)
             outer = jnp.concatenate(sides(odd_x, first1[part, rows], second1[part, rows]), axis=1)
@@ -461,8 +458,8 @@
     wide_shape = (2, window, 2 * window)
     square, strip = (2, half, window), (2, window, half)
 
-    edge_first, edge_second, rows_first, rows_second = call(
-        edges, [strip] * 2 + [square] * 2, [VMEM], (object_field,), micros=0.2, name="edges"
+    edge_first, edge_second = call(
+        edges, [strip] * 2, [VMEM], (object_field,), micros=12.0, name="edges"
     )
     halo_first = swapped(edge_first, "gx", 0)
     halo_second = swapped(edge_second, "gx", 1)
@@ -477,11 +474,8 @@
         [twice(count, 2), grads] + pos_scratch,
         micros=12.0, name="detect",
     )
-    up2, down2, rows_first, rows_second = barrier((up2, down2, rows_first, rows_second))
     from_up2 = swapped(up2, "gy", 0)
     from_down2 = swapped(down2, "gy", 1)
-    own_first = swapped(rows_first, "gy", 0)
-    own_second = swapped(rows_second, "gy", 1)
 
     fields, probes = call(
         roll_fields,
@@ -491,15 +485,17 @@
         [twice(count + 1, 2)] + pos_scratch,
         micros=0.1, name="roll",
     )
-    corner0_first, corner0_second = call(
-        relay, [square] * 2, [VMEM] * 2, (halo_first, halo_second), micros=12.0, name="widen"
-    )
-    from_corner0_first = swapped(corner0_first, "gy", 0)
-    from_corner0_second = swapped(corner0_second, "gy", 1)
-
-    from_up2, from_down2, own_first, own_second, fields, probes = barrier(
-        (from_up2, from_down2, own_first, own_second, fields, probes)
-    )
+    rows_first, rows_second = call(
+        relay,
+        [(2, half, 2 * window)] * 2,
+        [VMEM] * 3,
+        (object_field, halo_first, halo_second),
+        micros=12.0, name="widen",
+    )
+    from_rows_first = swapped(rows_first, "gy", 0)
+    from_rows_second = swapped(rows_second, "gy", 1)
+
+    from_up2, from_down2, fields, probes = barrier((from_up2, from_down2, fields, probes))
     first2, second2, centre2 = call(
         narrow,
         [(2, window + 3 * size, half)] * 2 + [fields_shape[1:]],
@@ -507,33 +503,35 @@
         (notes, middle2, from_up2, from_down2),
         micros=0.2, name="narrow2",
     )
-    from_corner0_first, from_corner0_second, first2, second2, centre2 = barrier(
-        (from_corner0_first, from_corner0_second, first2, second2, centre2)
-    )
+    from_rows_first, from_rows_second, centre2 = barrier((from_rows_first, from_rows_second, centre2))
     got_first2 = swapped(first2, "gx", 0)
     got_second2 = swapped(second2, "gx", 1)
 
     outer_first, outer_second, inner_first, inner_second, middle1 = call(
         propagate,
         [square] * 4 + [wide_shape],
-        [VMEM] * 11,
-        (marks, fields, probes, object_field, halo_first, halo_second, own_first, own_second)
-        + (from_corner0_first, from_corner0_second, table),
+        [VMEM] * 9,
+        (marks, fields, probes, object_field, halo_first, halo_second, from_rows_first, from_rows_second, table),
         [pltpu.VMEM(fields_shape, BF16)] * 2 + [grads],
         micros=0.1, name="propagate",
     )
     from_outer_first = swapped(outer_first, "gy", 0)
     from_outer_second = swapped(outer_second, "gy", 1)
-    (total2,) = call(join, [centre2.shape], [VMEM] * 3, (centre2, got_first2, got_second2), micros=12.0, name="join2")
+    (total2_first,) = call(
+        functools.partial(join, low=False), [strip], [VMEM] * 2, (centre2, got_first2), micros=1.0, name="join2"
+    )
+    middle1, total2_first = barrier((middle1, total2_first))
     first1, second1 = call(
         narrow_outer, [strip] * 2, [VMEM] * 3, (middle1, from_outer_first, from_outer_second), micros=0.2, name="narrow1"
     )
-    first1, second1, inner_first, inner_second = barrier((first1, second1, inner_first, inner_second))
     got_first1 = swapped(first1, "gx", 0)
     got_second1 = swapped(second1, "gx", 1)
     from_inner_first = swapped(inner_first, "gy", 0)
     from_inner_second = swapped(inner_second, "gy", 1)
 
+    from_inner_first, from_inner_second, got_first2, got_second2 = barrier(
+        (from_inner_first, from_inner_second, got_first2, got_second2)
+    )
     (scale,) = call(
         illuminate,
         [(window, window)],
@@ -542,11 +540,15 @@
         [twice(), pltpu.SMEM((8 * size, half), F32), pltpu.SemaphoreType.DMA((4,))],
         micros=12.0, name="illuminate",
     )
+    (total2_second,) = call(
+        functools.partial(join, low=True), [strip], [VMEM] * 2, (centre2, got_second2), micros=0.1, name="join3"
+    )
     (new_object,) = call(
         update,
         [object_field.shape],
-        [VMEM] * 8,
-        (got_first1, got_second1, object_field, scale, total2, middle1, from_inner_first, from_inner_second),
+        [VMEM] * 9,
+        (got_first1, got_second1, object_field, scale, total2_first, total2_second)
+        + (middle1, from_inner_first, from_inner_second),
         micros=1.0, name="update",
     )
     return new_object

time: 58.3 us -> 53.7 us (0.921)
  the two profiles are of different devices: /device:TPU:11 before, /device:TPU:20 now
where the time goes in v4:
time: 53.7 us; the launch traced here: 53.4 us
  starting transfers between devices  24.6 us (46%)
  waiting for transfers between devices  13.9 us (26%)
  Pallas kernels  13.4 us (25%)
  local copies, waits for them, and re-layouts  1.25 us (2%)
    ppermute x14, starting transfers between devices, swapped(): return lax.ppermute(value, axis, swap_pairs(lax.axis_size(axis), first))  24.6 us
    ppermute x14, waiting for transfers between devices, swapped(): return lax.ppermute(value, axis, swap_pairs(lax.axis_size(axis), first))  13.9 us
    pallas_call x11, Pallas kernels, call(): pl.pallas_call(body, out_shape=[x if hasattr(x, 'dtype') else jax.ShapeDt...  13.4 us
    unnamed x14, local copies, waits for them, and re-layouts  1.25 us
  transfers between devices with their start and end apart: 14, of which 5 were waited for; matrix products, arithmetic and copies ran while one was open for 0% of the time, Pallas kernels for 23%

profile of v4, /device:TPU:20, one launch (start us, length us, event | category | flops | bytes accessed | tf_op | source)
XLA Modules:
  0.0 53.4 jit_solution(5345450391498322296)
XLA Ops:
  0.0 0.0 copy-start
  0.0 1.2 %copy-done = f32[2,2,256,256]{3,2,1,0:T(8,128)S(1)} copy-done((f32[2,2,256,256]{3,2,1,0:T(8,128)S(1)}, f32[2,2,256,256]{3,2,1,0:T(8,128)}, u32[]{:S(2)}) %copy-start) | copy-done | bytes 1048600
  1.2 0.0 copy-start.2
  1.2 0.0 copy-start.5
  1.2 0.0 copy-start.6
  1.3 0.0 copy-start.4
  1.3 1.6 %collective-permute-start.2 = (f32[2,256,128]{2,1,0:T(8,128)S(1)}, f32[2,256,128]{2,1,0:T(8,128)S(1)}, u32[]{:S(2)}, u32[]{:S(2)}) collective-permute-start(f32[2,256,128]{2,1,0:T(8,128)S(1)} %get-tuple-element.48), channel_id=1, source_target_pairs={{0,8},{8,0},{16,24},{24,16},{1,9},{9,1},{17,25},{25,17},{2,10},{10... | collective-permute-start | bytes 786440 | tf_op jit(solution)/shard_map/ppermute | solution.py:45
  2.8 0.0 copy-start.1
  2.8 2.5 %collective-permute-start.3 = (f32[2,256,128]{2,1,0:T(8,128)S(1)}, f32[2,256,128]{2,1,0:T(8,128)S(1)}, u32[]{:S(2)}, u32[]{:S(2)}) collective-permute-start(f32[2,256,128]{2,1,0:T(8,128)S(1)} %get-tuple-element.49), channel_id=1, source_target_pairs={{8,16},{16,8},{9,17},{17,9},{10,18},{18,10},{11,19},{19,11},{12,20... | collective-permute-start | bytes 786440 | tf_op jit(solution)/shard_map/ppermute | solution.py:45
  5.4 0.0 copy-done.2
  5.4 0.0 copy-done.5
  5.4 0.0 copy-done.6
  5.4 0.0 copy-done.4
  5.4 2.9 %detect.1 = (f32[2,2,256,256]{3,2,1,0:T(8,128)S(1)}, f32[2,136,512]{2,1,0:T(8,128)S(1)}, f32[2,136,512]{2,1,0:T(8,128)S(1)}, f32[2,256,512]{2,1,0:T(8,128)S(1)},...) custom-call(s32[2,1,2]{2,1,0:T(1,128)S(1)} %copy-done.4, bf16[2,1,2,256,256]{4,3,2,1,0:T(8,128)(2,1)S(1)} %copy-done.5, ...), custom_call_target="tpu_custom_call" | custom-call | flops 12000000000 | bytes 1 | tf_op jit(solution)/shard_map/detect/pallas_call | solution.py:432
  8.3 0.1 collective-permute-start
  8.4 0.0 copy-start.3
  8.4 2.6 %collective-permute-start.1 = (f32[2,136,512]{2,1,0:T(8,128)S(1)}, f32[2,136,512]{2,1,0:T(8,128)S(1)}, u32[]{:S(2)}, u32[]{:S(2)}) collective-permute-start(f32[2,136,512]{2,1,0:T(8,128)S(1)} %get-tuple-element.42), channel_id=1, source_target_pairs={{1,2},{2,1},{3,4},{4,3},{5,6},{6,5},{9,10},{10,9},{11,12},{12,11},... | collective-permute-start | bytes 1671176 | tf_op jit(solution)/shard_map/ppermute | solution.py:45
  11.0 0.0 collective-permute-done.2.from_first.halo_first
  11.0 4.0 %collective-permute-done.3.from_second.halo_second = f32[2,256,128]{2,1,0:T(8,128)S(1)} collective-permute-done((f32[2,256,128]{2,1,0:T(8,128)S(1)}, f32[2,256,128]{2,1,0:T(8,128)S(1)}, u32[]{:S(2)}, u32[]{:S(2)}) %collective-permute-start.3) | collective-permute-done | bytes 262176 | tf_op jit(solution)/shard_map/ppermute | solution.py:45
  15.0 0.0 copy-done.1
  15.0 0.1 widen.1
  15.1 0.1 collective-permute-start.4
  15.2 2.4 %collective-permute-start.5 = (f32[2,128,512]{2,1,0:T(8,128)S(1)}, f32[2,128,512]{2,1,0:T(8,128)S(1)}, u32[]{:S(2)}, u32[]{:S(2)}) collective-permute-start(f32[2,128,512]{2,1,0:T(8,128)S(1)} %get-tuple-element.51), channel_id=1, source_target_pairs={{1,2},{2,1},{3,4},{4,3},{5,6},{6,5},{9,10},{10,9},{11,12},{12,11},... | collective-permute-start | bytes 1572872 | tf_op jit(solution)/shard_map/ppermute | solution.py:45
  17.6 0.0 copy-done.3
  17.6 1.2 %roll.1 = (f32[2,2,256,256]{3,2,1,0:T(8,128)S(1)}, f32[2,2,256,256]{3,2,1,0:T(8,128)S(1)}) custom-call(s32[2,1,2]{2,1,0:T(1,128)S(1)} %copy-done.4, f32[2,2,256,256]{3,2,1,0:T(8,128)S(1)} %get-tuple-element.43.field, f32[2,256,256]{2,1,0:T(8,128)S(1)} %copy-done.3), custom_call_target="tpu_custom_call" | custom-call | flops 100000000 | bytes 1 | tf_op jit(solution)/shard_map/roll/pallas_call | solution.py:432
  18.8 0.0 collective-permute-done.from_first.up
  18.8 0.5 collective-permute-done.1.from_second.down
  19.4 0.1 narrow2.1
  19.5 0.1 collective-permute-start.6
  19.6 4.4 %collective-permute-start.13 = (f32[2,280,128]{2,1,0:T(8,128)S(1)}, f32[2,280,128]{2,1,0:T(8,128)S(1)}, u32[]{:S(2)}, u32[]{:S(2)}) collective-permute-start(f32[2,280,128]{2,1,0:T(8,128)S(1)} %get-tuple-element.69), channel_id=1, source_target_pairs={{8,16},{16,8},{9,17},{17,9},{10,18},{18,10},{11,19},{19,11},{12,20... | collective-permute-start | bytes 860168 | tf_op jit(solution)/shard_map/ppermute | solution.py:45
  23.9 0.0 collective-permute-done.4.rows_first
  24.0 1.7 %collective-permute-done.5.rows_second = f32[2,128,512]{2,1,0:T(8,128)S(1)} collective-permute-done((f32[2,128,512]{2,1,0:T(8,128)S(1)}, f32[2,128,512]{2,1,0:T(8,128)S(1)}, u32[]{:S(2)}, u32[]{:S(2)}) %collective-permute-start.5) | collective-permute-done | bytes 524320 | tf_op jit(solution)/shard_map/ppermute | solution.py:45
  25.7 2.9 %propagate.1 = (f32[2,128,256]{2,1,0:T(8,128)S(1)}, f32[2,128,256]{2,1,0:T(8,128)S(1)}, f32[2,128,256]{2,1,0:T(8,128)S(1)}, f32[2,128,256]{2,1,0:T(8,128)S(1)}, f32[2,256,512]{2,1,0:T(8,128)S(1)}) custom-call(s32[4,8,256]{2,1,0:T(8,128)S(1)} %get-tuple-element.40.marks, f32[2,2,256,256]{3,2,1,0:T(8,128)S(1)} %get-tuple-element.46.field, ...), custom_call_target="tpu_custom_call" | custom-call | flops 100000000 | bytes 1 | tf_op jit(solution)/shard_map/propagate/pallas_call | solution.py:432
  28.6 0.8 %collective-permute-start.7 = (f32[2,128,256]{2,1,0:T(8,128)S(1)}, f32[2,128,256]{2,1,0:T(8,128)S(1)}, u32[]{:S(2)}, u32[]{:S(2)}) collective-permute-start(f32[2,128,256]{2,1,0:T(8,128)S(1)} %get-tuple-element.63), channel_id=1, source_target_pairs={{0,1},{1,0},{2,3},{3,2},{4,5},{5,4},{6,7},{7,6},{8,9},{9,8},{10,11... | collective-permute-start | bytes 786440 | tf_op jit(solution)/shard_map/ppermute | solution.py:45
  29.4 2.0 %collective-permute-start.8 = (f32[2,128,256]{2,1,0:T(8,128)S(1)}, f32[2,128,256]{2,1,0:T(8,128)S(1)}, u32[]{:S(2)}, u32[]{:S(2)}) collective-permute-start(f32[2,128,256]{2,1,0:T(8,128)S(1)} %get-tuple-element.64), channel_id=1, source_target_pairs={{1,2},{2,1},{3,4},{4,3},{5,6},{6,5},{9,10},{10,9},{11,12},{12,11},... | collective-permute-start | bytes 786440 | tf_op jit(solution)/shard_map/ppermute | solution.py:45
  31.4 0.9 %collective-permute-start.11 = (f32[2,128,256]{2,1,0:T(8,128)S(1)}, f32[2,128,256]{2,1,0:T(8,128)S(1)}, u32[]{:S(2)}, u32[]{:S(2)}) collective-permute-start(f32[2,128,256]{2,1,0:T(8,128)S(1)} %get-tuple-element.67), channel_id=1, source_target_pairs={{0,1},{1,0},{2,3},{3,2},{4,5},{5,4},{6,7},{7,6},{8,9},{9,8},{10,11... | collective-permute-start | bytes 786440 | tf_op jit(solution)/shard_map/ppermute | solution.py:45
  32.4 0.0 collective-permute-done.6.received.first
  32.4 2.7 %collective-permute-start.12 = (f32[2,128,256]{2,1,0:T(8,128)S(1)}, f32[2,128,256]{2,1,0:T(8,128)S(1)}, u32[]{:S(2)}, u32[]{:S(2)}) collective-permute-start(f32[2,128,256]{2,1,0:T(8,128)S(1)} %get-tuple-element.68), channel_id=1, source_target_pairs={{1,2},{2,1},{3,4},{4,3},{5,6},{6,5},{9,10},{10,9},{11,12},{12,11},... | collective-permute-start | bytes 786440 | tf_op jit(solution)/shard_map/ppermute | solution.py:45
  35.2 0.0 collective-permute-done.7.from_first
  35.2 2.0 %collective-permute-done.8.from_second = f32[2,128,256]{2,1,0:T(8,128)S(1)} collective-permute-done((f32[2,128,256]{2,1,0:T(8,128)S(1)}, f32[2,128,256]{2,1,0:T(8,128)S(1)}, u32[]{:S(2)}, u32[]{:S(2)}) %collective-permute-start.8) | collective-permute-done | bytes 262176 | tf_op jit(solution)/shard_map/ppermute | solution.py:45
  37.1 0.1 narrow1.1
  37.2 0.1 collective-permute-start.9
  37.3 4.4 %collective-permute-start.10 = (f32[2,256,128]{2,1,0:T(8,128)S(1)}, f32[2,256,128]{2,1,0:T(8,128)S(1)}, u32[]{:S(2)}, u32[]{:S(2)}) collective-permute-start(f32[2,256,128]{2,1,0:T(8,128)S(1)} %get-tuple-element.66), channel_id=1, source_target_pairs={{8,16},{16,8},{9,17},{17,9},{10,18},{18,10},{11,19},{19,11},{12,20... | collective-permute-start | bytes 786440 | tf_op jit(solution)/shard_map/ppermute | solution.py:45
  41.6 0.0 collective-permute-done.13.second.received
  41.6 0.0 collective-permute-done.11.inner_first
  41.6 0.0 collective-permute-done.12.inner_second
  41.7 4.6 %illuminate.1.scale = f32[256,256]{1,0:T(8,128)S(1)} custom-call(s32[2,1,2]{2,1,0:T(1,128)S(1)} %copy-done.4, f32[2,256,256]{2,1,0:T(8,128)S(1)} %copy-done.3, f32[2,136,512]{2,1,0:T(8,128)S(1)} %collective-permute-done.from_first.up, f32[2,136,512]{2,1,0:T(8,128)S(1)} %collective-permute-done.1.from_second.down, ...), custom_call_target="tpu_custom_call" | custom-call | flops 12000000000 | bytes 1 | tf_op jit(solution)/shard_map/illuminate/pallas_call | solution.py:432
  46.4 0.0 collective-permute-done.9.first1
  46.4 5.7 %collective-permute-done.10.second1 = f32[2,256,128]{2,1,0:T(8,128)S(1)} collective-permute-done((f32[2,256,128]{2,1,0:T(8,128)S(1)}, f32[2,256,128]{2,1,0:T(8,128)S(1)}, u32[]{:S(2)}, u32[]{:S(2)}) %collective-permute-start.10) | collective-permute-done | bytes 262176 | tf_op jit(solution)/shard_map/ppermute | solution.py:45
  52.1 1.3 %update.1 = f32[2,2,256,256]{3,2,1,0:T(8,128)} custom-call(f32[2,256,128]{2,1,0:T(8,128)S(1)} %collective-permute-done.9.first1, f32[2,256,128]{2,1,0:T(8,128)S(1)} %collective-permute-done.10.second1, f32[2,2,256,256]{3,2,1,0:T(8,128)S(1)} %copy-done.1, f32[256,256]{1,0:T(8,128)S(1)} %illuminate.1.scale, f32[2,256,128]{2,1,0:T(8,128)S(1)} %join2.1.total2_first, ...), custom_call_target="tpu_custom_call" | custom-call | flops 1000000000 | bytes 1 | tf_op jit(solution)/shard_map/update/pallas_call | solution.py:432
  (3 shorter events, 0.1 us)
Async XLA Ops:
  0.0 1.2 %copy-start = (f32[2,2,256,256]{3,2,1,0:T(8,128)S(1)}, f32[2,2,256,256]{3,2,1,0:T(8,128)}, u32[]{:S(2)}) copy-start(f32[2,2,256,256]{3,2,1,0:T(8,128)} %object_field.7) | copy-start | bytes 3145732
  1.2 4.1 %copy-start.2 = (bf16[4,256,512]{2,1,0:T(8,128)(2,1)S(1)}, bf16[4,256,512]{2,1,0:T(8,128)(2,1)}, u32[]{:S(2)}) copy-start(bf16[4,256,512]{2,1,0:T(8,128)(2,1)} %constant.2.clone.table) | copy-start | bytes 3145732
  1.2 4.1 %copy-start.5 = (bf16[2,1,2,256,256]{4,3,2,1,0:T(8,128)(2,1)S(1)}, bf16[2,1,2,256,256]{4,3,2,1,0:T(8,128)(2,1)}, u32[]{:S(2)}) copy-start(bf16[2,1,2,256,256]{4,3,2,1,0:T(8,128)(2,1)} %residual.1) | copy-start | bytes 1572868
  1.2 4.1 %copy-start.6 = (bf16[2,1,2,256,256]{4,3,2,1,0:T(8,128)(2,1)S(1)}, bf16[2,1,2,256,256]{4,3,2,1,0:T(8,128)(2,1)}, u32[]{:S(2)}) copy-start(bf16[2,1,2,256,256]{4,3,2,1,0:T(8,128)(2,1)} %wave.1) | copy-start | bytes 1572868
  1.3 4.1 %copy-start.4 = (s32[2,1,2]{2,1,0:T(1,128)S(1)}, s32[2,1,2]{2,1,0:T(1,128)}, u32[]{:S(2)}) copy-start(s32[2,1,2]{2,1,0:T(1,128)} %pos.1) | copy-start | bytes 52
  1.3 9.7 %collective-permute-start.2 = (f32[2,256,128]{2,1,0:T(8,128)S(1)}, f32[2,256,128]{2,1,0:T(8,128)S(1)}, u32[]{:S(2)}, u32[]{:S(2)}) collective-permute-start(f32[2,256,128]{2,1,0:T(8,128)S(1)} %get-tuple-element.48), channel_id=1, source_target_pairs={{0,8},{8,0},{16,24},{24,16},{1,9},{9,1},{17,25},{25,17},{2,10},{10... | collective-permute-start | bytes 786440 | tf_op jit(solution)/shard_map/ppermute | solution.py:45
  2.8 12.1 %copy-start.1 = (f32[2,2,256,256]{3,2,1,0:T(8,128)S(1)}, f32[2,2,256,256]{3,2,1,0:T(8,128)}, u32[]{:S(2)}) copy-start(f32[2,2,256,256]{3,2,1,0:T(8,128)} %object_field.7) | copy-start | bytes 3145732
  2.8 12.1 %collective-permute-start.3 = (f32[2,256,128]{2,1,0:T(8,128)S(1)}, f32[2,256,128]{2,1,0:T(8,128)S(1)}, u32[]{:S(2)}, u32[]{:S(2)}) collective-permute-start(f32[2,256,128]{2,1,0:T(8,128)S(1)} %get-tuple-element.49), channel_id=1, source_target_pairs={{8,16},{16,8},{9,17},{17,9},{10,18},{18,10},{11,19},{19,11},{12,20... | collective-permute-start | bytes 786440 | tf_op jit(solution)/shard_map/ppermute | solution.py:45
  8.3 10.6 %collective-permute-start = (f32[2,136,512]{2,1,0:T(8,128)S(1)}, f32[2,136,512]{2,1,0:T(8,128)S(1)}, u32[]{:S(2)}, u32[]{:S(2)}) collective-permute-start(f32[2,136,512]{2,1,0:T(8,128)S(1)} %get-tuple-element.41), channel_id=1, source_target_pairs={{0,1},{1,0},{2,3},{3,2},{4,5},{5,4},{6,7},{7,6},{8,9},{9,8},{10,11... | collective-permute-start | bytes 1671176 | tf_op jit(solution)/shard_map/ppermute | solution.py:45
  8.4 9.2 %copy-start.3 = (f32[2,256,256]{2,1,0:T(8,128)S(1)}, f32[2,256,256]{2,1,0:T(8,128)}, u32[]{:S(2)}) copy-start(f32[2,256,256]{2,1,0:T(8,128)} %probe.3) | copy-start | bytes 1572868
  8.4 11.0 %collective-permute-start.1 = (f32[2,136,512]{2,1,0:T(8,128)S(1)}, f32[2,136,512]{2,1,0:T(8,128)S(1)}, u32[]{:S(2)}, u32[]{:S(2)}) collective-permute-start(f32[2,136,512]{2,1,0:T(8,128)S(1)} %get-tuple-element.42), channel_id=1, source_target_pairs={{1,2},{2,1},{3,4},{4,3},{5,6},{6,5},{9,10},{10,9},{11,12},{12,11},... | collective-permute-start | bytes 1671176 | tf_op jit(solution)/shard_map/ppermute | solution.py:45
  15.1 8.9 %collective-permute-start.4 = (f32[2,128,512]{2,1,0:T(8,128)S(1)}, f32[2,128,512]{2,1,0:T(8,128)S(1)}, u32[]{:S(2)}, u32[]{:S(2)}) collective-permute-start(f32[2,128,512]{2,1,0:T(8,128)S(1)} %get-tuple-element.50), channel_id=1, source_target_pairs={{0,1},{1,0},{2,3},{3,2},{4,5},{5,4},{6,7},{7,6},{8,9},{9,8},{10,11... | collective-permute-start | bytes 1572872 | tf_op jit(solution)/shard_map/ppermute | solution.py:45
  15.2 10.5 %collective-permute-start.5 = (f32[2,128,512]{2,1,0:T(8,128)S(1)}, f32[2,128,512]{2,1,0:T(8,128)S(1)}, u32[]{:S(2)}, u32[]{:S(2)}) collective-permute-start(f32[2,128,512]{2,1,0:T(8,128)S(1)} %get-tuple-element.51), channel_id=1, source_target_pairs={{1,2},{2,1},{3,4},{4,3},{5,6},{6,5},{9,10},{10,9},{11,12},{12,11},... | collective-permute-start | bytes 1572872 | tf_op jit(solution)/shard_map/ppermute | solution.py:45
  19.5 12.9 %collective-permute-start.6 = (f32[2,280,128]{2,1,0:T(8,128)S(1)}, f32[2,280,128]{2,1,0:T(8,128)S(1)}, u32[]{:S(2)}, u32[]{:S(2)}) collective-permute-start(f32[2,280,128]{2,1,0:T(8,128)S(1)} %get-tuple-element.61), channel_id=1, source_target_pairs={{0,8},{8,0},{16,24},{24,16},{1,9},{9,1},{17,25},{25,17},{2,10},{10... | collective-permute-start | bytes 860168 | tf_op jit(solution)/shard_map/ppermute | solution.py:45
  19.6 22.1 %collective-permute-start.13 = (f32[2,280,128]{2,1,0:T(8,128)S(1)}, f32[2,280,128]{2,1,0:T(8,128)S(1)}, u32[]{:S(2)}, u32[]{:S(2)}) collective-permute-start(f32[2,280,128]{2,1,0:T(8,128)S(1)} %get-tuple-element.69), channel_id=1, source_target_pairs={{8,16},{16,8},{9,17},{17,9},{10,18},{18,10},{11,19},{19,11},{12,20... | collective-permute-start | bytes 860168 | tf_op jit(solution)/shard_map/ppermute | solution.py:45
  28.6 6.6 %collective-permute-start.7 = (f32[2,128,256]{2,1,0:T(8,128)S(1)}, f32[2,128,256]{2,1,0:T(8,128)S(1)}, u32[]{:S(2)}, u32[]{:S(2)}) collective-permute-start(f32[2,128,256]{2,1,0:T(8,128)S(1)} %get-tuple-element.63), channel_id=1, source_target_pairs={{0,1},{1,0},{2,3},{3,2},{4,5},{5,4},{6,7},{7,6},{8,9},{9,8},{10,11... | collective-permute-start | bytes 786440 | tf_op jit(solution)/shard_map/ppermute | solution.py:45
  29.4 7.7 %collective-permute-start.8 = (f32[2,128,256]{2,1,0:T(8,128)S(1)}, f32[2,128,256]{2,1,0:T(8,128)S(1)}, u32[]{:S(2)}, u32[]{:S(2)}) collective-permute-start(f32[2,128,256]{2,1,0:T(8,128)S(1)} %get-tuple-element.64), channel_id=1, source_target_pairs={{1,2},{2,1},{3,4},{4,3},{5,6},{6,5},{9,10},{10,9},{11,12},{12,11},... | collective-permute-start | bytes 786440 | tf_op jit(solution)/shard_map/ppermute | solution.py:45
  31.4 10.2 %collective-permute-start.11 = (f32[2,128,256]{2,1,0:T(8,128)S(1)}, f32[2,128,256]{2,1,0:T(8,128)S(1)}, u32[]{:S(2)}, u32[]{:S(2)}) collective-permute-start(f32[2,128,256]{2,1,0:T(8,128)S(1)} %get-tuple-element.67), channel_id=1, source_target_pairs={{0,1},{1,0},{2,3},{3,2},{4,5},{5,4},{6,7},{7,6},{8,9},{9,8},{10,11... | collective-permute-start | bytes 786440 | tf_op jit(solution)/shard_map/ppermute | solution.py:45
  32.4 9.3 %collective-permute-start.12 = (f32[2,128,256]{2,1,0:T(8,128)S(1)}, f32[2,128,256]{2,1,0:T(8,128)S(1)}, u32[]{:S(2)}, u32[]{:S(2)}) collective-permute-start(f32[2,128,256]{2,1,0:T(8,128)S(1)} %get-tuple-element.68), channel_id=1, source_target_pairs={{1,2},{2,1},{3,4},{4,3},{5,6},{6,5},{9,10},{10,9},{11,12},{12,11},... | collective-permute-start | bytes 786440 | tf_op jit(solution)/shard_map/ppermute | solution.py:45
  37.2 9.2 %collective-permute-start.9 = (f32[2,256,128]{2,1,0:T(8,128)S(1)}, f32[2,256,128]{2,1,0:T(8,128)S(1)}, u32[]{:S(2)}, u32[]{:S(2)}) collective-permute-start(f32[2,256,128]{2,1,0:T(8,128)S(1)} %get-tuple-element.65), channel_id=1, source_target_pairs={{0,8},{8,0},{16,24},{24,16},{1,9},{9,1},{17,25},{25,17},{2,10},{10... | collective-permute-start | bytes 786440 | tf_op jit(solution)/shard_map/ppermute | solution.py:45
  37.3 14.8 %collective-permute-start.10 = (f32[2,256,128]{2,1,0:T(8,128)S(1)}, f32[2,256,128]{2,1,0:T(8,128)S(1)}, u32[]{:S(2)}, u32[]{:S(2)}) collective-permute-start(f32[2,256,128]{2,1,0:T(8,128)S(1)} %get-tuple-element.66), channel_id=1, source_target_pairs={{8,16},{16,8},{9,17},{17,9},{10,18},{18,10},{11,19},{19,11},{12,20... | collective-permute-start | bytes 786440 | tf_op jit(solution)/shard_map/ppermute | solution.py:45

commit v5 on v4

--- a/solution.py
+++ b/solution.py
@@ -146,8 +146,8 @@
 
 
 def detect(
-    pos_any, residual, wave, table,
-    field, first, second, middle, notes, marks,
+    pos_any, residual, wave, table, object_field,
+    field, first, second, inner_first, inner_second, middle, notes, marks,
     twice, grads, pos, sem,
 ):
     window = residual.shape[-1]
@@ -177,9 +177,12 @@
 
             rolled(twice.at[number, part], corner, store, window)
             marks[2 * number + part] = jnp.full(marks.shape[1:], corner[part], jnp.int32)
-    place([grads.at[0], grads.at[1]], corners, first, second, middle, odd, window)
-    for ref in (first, second):
-        ref[0, window // 2 :] = notes_of(pos, count, 2 * window)
+    place([grads.at[0], grads.at[1]], corners, (first, inner_first), (second, inner_second), middle, odd, window)
+    half = window // 2
+    for ref, base in ((first, (1 - odd) * half), (second, odd * half)):
+        ref[0, half:] = notes_of(pos, count, window)
+        for part in range(2):
+            ref[2 + part, :half] = object_field[1, part, pl.ds(pl.multiple_of(base, half), half), :]
     notes[...] = notes_of(pos, count, window // 2)
 
 
@@ -232,23 +235,22 @@
         ref[...] = object_field[1, :, :, pl.ds(pl.multiple_of(odd * half, half), half)]
 
 
-def relay(object_field, from_first, from_second, first, second):
+def relay(from_first, from_second, first, second):
     half = from_first.shape[-1]
     odd_x = lax.rem(lax.axis_index("gx"), 2)
     odd_y = lax.rem(lax.axis_index("gy"), 2)
-    at_first = pl.ds(pl.multiple_of((1 - odd_x) * 3 * half, half), half)
-    at_second = pl.ds(pl.multiple_of(odd_x * 3 * half, half), half)
+    at_first = pl.ds(pl.multiple_of((1 - odd_x) * half, half), half)
+    at_second = pl.ds(pl.multiple_of(odd_x * half, half), half)
     for ref, base in ((first, (1 - odd_y) * half), (second, odd_y * half)):
         rows = pl.ds(pl.multiple_of(base, half), half)
         for plane in range(ref.shape[0]):
-            ref[plane, :, half : 3 * half] = object_field[1, plane, rows]
             ref[plane, :, at_first] = from_first[plane, rows]
             ref[plane, :, at_second] = from_second[plane, rows]
 
 
 def propagate(
     marks, field, probes, object_field, halo_first, halo_second,
-    rows_first, rows_second, table,
+    own_second, own_first, corner_second, corner_first, table, inner2_first, inner2_second,
     outer_first, outer_second, inner_first, inner_second, middle,
     chi_hi, chi_lo, grads,
 ):
@@ -259,13 +261,17 @@
     odd = lax.rem(lax.axis_index("gy"), 2)
     corners = [(marks[2 * number, :1], marks[2 * number + 1, :1]) for number in range(count)]
     table_hi, table_lo = table.at[2], table.at[3]
+    inner_first[2:] = inner2_first[...]
+    inner_second[2:] = inner2_second[...]
 
     def wide(part, rows):
         left, right = sides(odd_x, halo_first[part, rows], halo_second[part, rows])
         return jnp.concatenate([left, object_field[1, part, rows], right], axis=1)
 
     def beyond(part, rows, below):
-        return sides(odd, rows_first[part, rows], rows_second[part, rows])[below]
+        own = sides(odd, own_first[2 + part, rows], own_second[2 + part, rows])[below]
+        corner = sides(odd, corner_first[part, rows], corner_second[part, rows])[below]
+        return jnp.concatenate([corner[:, :half], own, corner[:, half:]], axis=1)
 
     for start in range(0, window, CHUNK):
         rows = slice(start, start + CHUNK)
@@ -366,19 +372,14 @@
     lax.fori_loop(0, window // CHUNK, rows_at, 0)
 
 
-def narrow(notes, middle, from_first, from_second, first, second, centre):
+def narrow_noted(notes, middle, from_second, from_first, first, second):
     half = first.shape[-1]
     window = 2 * half
-    odd_x = lax.rem(lax.axis_index("gx"), 2)
     odd_y = lax.rem(lax.axis_index("gy"), 2)
-    for plane in range(middle.shape[0]):
-        for start in range(0, half, CHUNK):
-            rows = slice(start, start + CHUNK)
-            for received, base in ((from_first, (1 - odd_y) * half), (from_second, odd_y * half)):
-                at = pl.ds(pl.multiple_of(base + start, CHUNK), CHUNK)
-                total = middle[plane, at, :] + received[plane, rows]
-                centre[plane, at, :] = total[:, half : 3 * half]
-                second[plane, at, :], first[plane, at, :] = sides(odd_x, total[:, 3 * half :], total[:, :half])
+    columns = pl.ds(0, window)
+    narrow_outer(
+        middle, from_second.at[:2, :half], from_first.at[:2, :half], first.at[:, columns], second.at[:, columns]
+    )
     size = notes.shape[0]
     above, below = sides(odd_y, from_first[0, half:, :half], from_second[0, half:, :half])
     for ref in (first, second):
@@ -387,7 +388,7 @@
         ref[0, window + 2 * size :] = below
 
 
-def narrow_outer(middle, from_first, from_second, first, second):
+def narrow_outer(middle, from_second, from_first, first, second):
     half = first.shape[-1]
     odd_x = lax.rem(lax.axis_index("gx"), 2)
     odd_y = lax.rem(lax.axis_index("gy"), 2)
@@ -399,28 +400,53 @@
             second[plane, at, :], first[plane, at, :] = sides(odd_x, right, left)
 
 
-def join(centre, received, out, low):
-    window = centre.shape[-1]
+def join(middle, received, out, low):
+    window = middle.shape[1]
     half = window // 2
     odd_x = lax.rem(lax.axis_index("gx"), 2)
     base = (odd_x if low else 1 - odd_x) * half
-    at = pl.ds(pl.multiple_of(base, half), half)
-    out[...] = centre[:, :, at] + received[:, :window]
-
-
-def update(first1, second1, object_field, scale, total2_first, total2_second, middle1, inner_first, inner_second, out):
+    at = pl.ds(pl.multiple_of(half + base, half), half)
+    out[...] = middle[:, :, at] + received[:, :window]
+
+
+def written(value, out, number, sem):
+    copy = pltpu.make_async_copy(value, out.at[number], sem)
+    copy.start()
+    return copy
+
+
+def update_second(
+    object_field, scale, total2_first, total2_second, inner_second, inner_first, out, value, sem
+):
+    half = scale.shape[-1] // 2
+    odd_x = lax.rem(lax.axis_index("gx"), 2)
+    odd_y = lax.rem(lax.axis_index("gy"), 2)
+    for part in range(2):
+        for received, base in ((inner_first, (1 - odd_y) * half), (inner_second, odd_y * half)):
+            rows = pl.ds(pl.multiple_of(base, half), half)
+            outer = jnp.concatenate(sides(odd_x, total2_first[part, rows], total2_second[part, rows]), axis=1)
+            value[part, rows] = object_field[1, part, rows] - (outer + received[2 + part]) * scale[rows]
+    written(value, out, 1, sem).wait()
+
+
+def update_first(
+    begun, first1, second1, object_field, scale, middle1, inner_second, inner_first, out, value, sems
+):
+    del begun
     window = scale.shape[-1]
     half = window // 2
     odd_x = lax.rem(lax.axis_index("gx"), 2)
     odd_y = lax.rem(lax.axis_index("gy"), 2)
+    copies = []
     for part in range(2):
-        total = jnp.concatenate(sides(odd_x, total2_first[part], total2_second[part]), axis=1)
-        out[1, part] = object_field[1, part] - total * scale[...]
         for received, base in ((inner_first, (1 - odd_y) * half), (inner_second, odd_y * half)):
             rows = pl.ds(pl.multiple_of(base, half), half)
             outer = jnp.concatenate(sides(odd_x, first1[part, rows], second1[part, rows]), axis=1)
             total = middle1[part, rows, half : 3 * half] + received[part] + outer
-            out[0, part, rows] = object_field[0, part, rows] - total * scale[rows]
+            value[part, rows] = object_field[0, part, rows] - total * scale[rows]
+        copies.append(written(value.at[part], out.at[0], part, sems.at[part]))
+    for copy in copies:
+        copy.wait()
 
 
 VMEM = pl.BlockSpec(memory_space=pltpu.VMEM)
@@ -428,12 +454,13 @@
 ANY = pl.BlockSpec(memory_space=pl.ANY)
 
 
-def call(body, outs, in_specs, args, scratch=(), micros=0.0, name=None):
+def call(body, outs, in_specs, args, scratch=(), out_specs=None, aliases=None, micros=0.0, name=None):
     return pl.pallas_call(
         body,
         out_shape=[x if hasattr(x, "dtype") else jax.ShapeDtypeStruct(x, F32) for x in outs],
         in_specs=in_specs,
-        out_specs=[VMEM] * len(outs),
+        out_specs=out_specs or [VMEM] * len(outs),
+        input_output_aliases=aliases or {},
         scratch_shapes=list(scratch),
         compiler_params=pltpu.CompilerParams(vmem_limit_bytes=24 * 1024 * 1024),
         cost_estimate=pl.CostEstimate(flops=int(micros * 1e9), bytes_accessed=1, transcendentals=0),
@@ -464,18 +491,18 @@
     halo_first = swapped(edge_first, "gx", 0)
     halo_second = swapped(edge_second, "gx", 1)
 
-    field, up2, down2, middle2, notes, marks = call(
+    field, up2, down2, inner2_first, inner2_second, middle2, notes, marks = call(
         detect,
         [fields_shape]
-        + [(2, half + size, 2 * window)] * 2
-        + [wide_shape, (size, half), jax.ShapeDtypeStruct((2 * count, 8, window), jnp.int32)],
-        [ANY] + [VMEM] * 3,
-        (positions, residual, saved_wave, table),
+        + [(4, half + size, window)] * 2
+        + [square, square, wide_shape, (size, half), jax.ShapeDtypeStruct((2 * count, 8, window), jnp.int32)],
+        [ANY] + [VMEM] * 4,
+        (positions, residual, saved_wave, table, object_field),
         [twice(count, 2), grads] + pos_scratch,
         micros=12.0, name="detect",
     )
+    from_down2 = swapped(down2, "gy", 1)
     from_up2 = swapped(up2, "gy", 0)
-    from_down2 = swapped(down2, "gy", 1)
 
     fields, probes = call(
         roll_fields,
@@ -487,51 +514,49 @@
     )
     rows_first, rows_second = call(
         relay,
-        [(2, half, 2 * window)] * 2,
-        [VMEM] * 3,
-        (object_field, halo_first, halo_second),
+        [square] * 2,
+        [VMEM] * 2,
+        (halo_first, halo_second),
         micros=12.0, name="widen",
     )
+    from_rows_second = swapped(rows_second, "gy", 1)
     from_rows_first = swapped(rows_first, "gy", 0)
-    from_rows_second = swapped(rows_second, "gy", 1)
-
-    from_up2, from_down2, fields, probes = barrier((from_up2, from_down2, fields, probes))
-    first2, second2, centre2 = call(
-        narrow,
-        [(2, window + 3 * size, half)] * 2 + [fields_shape[1:]],
+
+    from_down2, from_up2, fields, probes = barrier((from_down2, from_up2, fields, probes))
+    first2, second2 = call(
+        narrow_noted,
+        [(2, window + 3 * size, half)] * 2,
         [VMEM] * 4,
-        (notes, middle2, from_up2, from_down2),
+        (notes, middle2, from_down2, from_up2),
         micros=0.2, name="narrow2",
     )
-    from_rows_first, from_rows_second, centre2 = barrier((from_rows_first, from_rows_second, centre2))
+    from_rows_second, from_rows_first, marks, _ = barrier((from_rows_second, from_rows_first, marks, first2))
     got_first2 = swapped(first2, "gx", 0)
     got_second2 = swapped(second2, "gx", 1)
 
     outer_first, outer_second, inner_first, inner_second, middle1 = call(
         propagate,
-        [square] * 4 + [wide_shape],
-        [VMEM] * 9,
-        (marks, fields, probes, object_field, halo_first, halo_second, from_rows_first, from_rows_second, table),
+        [square] * 2 + [(4, half, window)] * 2 + [wide_shape],
+        [VMEM] * 13,
+        (marks, fields, probes, object_field, halo_first, halo_second, from_down2, from_up2)
+        + (from_rows_second, from_rows_first, table, inner2_first, inner2_second),
         [pltpu.VMEM(fields_shape, BF16)] * 2 + [grads],
         micros=0.1, name="propagate",
     )
+    from_outer_second = swapped(outer_second, "gy", 1)
     from_outer_first = swapped(outer_first, "gy", 0)
-    from_outer_second = swapped(outer_second, "gy", 1)
-    (total2_first,) = call(
-        functools.partial(join, low=False), [strip], [VMEM] * 2, (centre2, got_first2), micros=1.0, name="join2"
-    )
-    middle1, total2_first = barrier((middle1, total2_first))
+    (total2_second,) = call(
+        functools.partial(join, low=True), [strip], [VMEM] * 2, (middle2, got_second2), micros=1.0, name="join3"
+    )
+    middle1, total2_second = barrier((middle1, total2_second))
     first1, second1 = call(
-        narrow_outer, [strip] * 2, [VMEM] * 3, (middle1, from_outer_first, from_outer_second), micros=0.2, name="narrow1"
+        narrow_outer, [strip] * 2, [VMEM] * 3, (middle1, from_outer_second, from_outer_first), micros=0.2, name="narrow1"
     )
     got_first1 = swapped(first1, "gx", 0)
     got_second1 = swapped(second1, "gx", 1)
     from_inner_first = swapped(inner_first, "gy", 0)
     from_inner_second = swapped(inner_second, "gy", 1)
 
-    from_inner_first, from_inner_second, got_first2, got_second2 = barrier(
-        (from_inner_first, from_inner_second, got_first2, got_second2)
-    )
     (scale,) = call(
         illuminate,
         [(window, window)],
@@ -540,16 +565,25 @@
         [twice(), pltpu.SMEM((8 * size, half), F32), pltpu.SemaphoreType.DMA((4,))],
         micros=12.0, name="illuminate",
     )
-    (total2_second,) = call(
-        functools.partial(join, low=True), [strip], [VMEM] * 2, (centre2, got_second2), micros=0.1, name="join3"
+    (total2_first,) = call(
+        functools.partial(join, low=False), [strip], [VMEM] * 2, (middle2, got_first2), micros=0.5, name="join2"
+    )
+    value = pltpu.VMEM(fields_shape[1:], F32)
+    (begun,) = call(
+        update_second,
+        [object_field.shape],
+        [VMEM] * 6,
+        (object_field, scale, total2_first, total2_second, from_inner_second, from_inner_first),
+        [value, pltpu.SemaphoreType.DMA],
+        out_specs=[ANY], micros=0.1, name="update2",
     )
     (new_object,) = call(
-        update,
+        update_first,
         [object_field.shape],
-        [VMEM] * 9,
-        (got_first1, got_second1, object_field, scale, total2_first, total2_second)
-        + (middle1, from_inner_first, from_inner_second),
-        micros=1.0, name="update",
+        [ANY] + [VMEM] * 7,
+        (begun, got_first1, got_second1, object_field, scale, middle1, from_inner_second, from_inner_first),
+        [value, pltpu.SemaphoreType.DMA((2,))],
+        out_specs=[ANY], aliases={0: 0}, micros=1.0, name="update",
     )
     return new_object
 

time: 53.7 us -> 52.2 us (0.972)
  the two profiles are of different devices: /device:TPU:20 before, /device:TPU:11 now
where the time goes in v5:
time: 52.2 us; the launch traced here: 51.5 us
  starting transfers between devices  28.6 us (55%)
  Pallas kernels  14.3 us (27%)
  waiting for transfers between devices  6.93 us (13%)
  local copies, waits for them, and re-layouts  1.25 us (2%)
    ppermute x14, starting transfers between devices, swapped(): return lax.ppermute(value, axis, swap_pairs(lax.axis_size(axis), first))  28.6 us
    pallas_call x12, Pallas kernels, call(): pl.pallas_call(body, out_shape=[x if hasattr(x, 'dtype') else jax.ShapeDt...  14.3 us
    ppermute x14, waiting for transfers between devices, swapped(): return lax.ppermute(value, axis, swap_pairs(lax.axis_size(axis), first))  6.93 us
    unnamed x14, local copies, waits for them, and re-layouts  1.25 us
  transfers between devices with their start and end apart: 14, of which 4 were waited for; matrix products, arithmetic and copies ran while one was open for 0% of the time, Pallas kernels for 26%

profile of v5, /device:TPU:11, one launch (start us, length us, event | category | flops | bytes accessed | tf_op | source)
XLA Modules:
  0.0 51.5 jit_solution(3198020750620241992)
XLA Ops:
  0.0 0.0 copy-start
  0.0 1.2 %copy-done = f32[2,2,256,256]{3,2,1,0:T(8,128)S(1)} copy-done((f32[2,2,256,256]{3,2,1,0:T(8,128)S(1)}, f32[2,2,256,256]{3,2,1,0:T(8,128)}, u32[]{:S(2)}) %copy-start) | copy-done | bytes 1048600
  1.2 0.0 copy-start.1
  1.2 0.0 copy-start.2
  1.2 0.0 copy-start.5
  1.2 0.0 copy-start.6
  1.2 0.1 edges.1
  1.3 0.0 copy-start.4
  1.3 0.3 collective-permute-start.4
  1.6 4.1 %collective-permute-start.5 = (f32[2,256,128]{2,1,0:T(8,128)S(1)}, f32[2,256,128]{2,1,0:T(8,128)S(1)}, u32[]{:S(2)}, u32[]{:S(2)}) collective-permute-start(f32[2,256,128]{2,1,0:T(8,128)S(1)} %get-tuple-element.49), channel_id=1, source_target_pairs={{8,16},{16,8},{9,17},{17,9},{10,18},{18,10},{11,19},{19,11},{12,20... | collective-permute-start | bytes 786440 | tf_op jit(solution)/shard_map/ppermute | solution.py:45
  5.7 0.0 copy-done.1
  5.7 0.0 copy-done.2
  5.7 0.0 copy-done.5
  5.7 0.0 copy-done.6
  5.7 0.0 copy-done.4
  5.7 3.2 %detect.1 = (f32[2,2,256,256]{3,2,1,0:T(8,128)S(1)}, f32[4,136,256]{2,1,0:T(8,128)S(1)}, f32[4,136,256]{2,1,0:T(8,128)S(1)}, f32[2,128,256]{2,1,0:T(8,128)S(1)},...) custom-call(s32[2,1,2]{2,1,0:T(1,128)S(1)} %copy-done.4, ...), custom_call_target="tpu_custom_call" | custom-call | flops 12000000000 | bytes 1 | tf_op jit(solution)/shard_map/detect/pallas_call | solution.py:458
  9.0 4.3 %collective-permute-start = (f32[4,136,256]{2,1,0:T(8,128)S(1)}, f32[4,136,256]{2,1,0:T(8,128)S(1)}, u32[]{:S(2)}, u32[]{:S(2)}) collective-permute-start(f32[4,136,256]{2,1,0:T(8,128)S(1)} %get-tuple-element.37), channel_id=1, source_target_pairs={{1,2},{2,1},{3,4},{4,3},{5,6},{6,5},{9,10},{10,9},{11,12},{12,11},... | collective-permute-start | bytes 1671176 | tf_op jit(solution)/shard_map/ppermute | solution.py:45
  13.3 0.0 copy-start.3
  13.3 0.1 collective-permute-start.1
  13.4 0.0 collective-permute-done.4.from_first.halo_first
  13.4 1.7 %collective-permute-done.5.from_second.halo_second = f32[2,256,128]{2,1,0:T(8,128)S(1)} collective-permute-done((f32[2,256,128]{2,1,0:T(8,128)S(1)}, f32[2,256,128]{2,1,0:T(8,128)S(1)}, u32[]{:S(2)}, u32[]{:S(2)}) %collective-permute-start.5) | collective-permute-done | bytes 262176 | tf_op jit(solution)/shard_map/ppermute | solution.py:45
  15.2 4.6 %collective-permute-start.6 = (f32[2,128,256]{2,1,0:T(8,128)S(1)}, f32[2,128,256]{2,1,0:T(8,128)S(1)}, u32[]{:S(2)}, u32[]{:S(2)}) collective-permute-start(f32[2,128,256]{2,1,0:T(8,128)S(1)} %get-tuple-element.50), channel_id=1, source_target_pairs={{1,2},{2,1},{3,4},{4,3},{5,6},{6,5},{9,10},{10,9},{11,12},{12,11},... | collective-permute-start | bytes 786440 | tf_op jit(solution)/shard_map/ppermute | solution.py:45
  19.8 0.1 collective-permute-start.7
  19.9 0.0 copy-done.3
  19.9 1.2 %roll.1 = (f32[2,2,256,256]{3,2,1,0:T(8,128)S(1)}, f32[2,2,256,256]{3,2,1,0:T(8,128)S(1)}) custom-call(s32[2,1,2]{2,1,0:T(1,128)S(1)} %copy-done.4, f32[2,2,256,256]{3,2,1,0:T(8,128)S(1)} %get-tuple-element.39.field, f32[2,256,256]{2,1,0:T(8,128)S(1)} %copy-done.3), custom_call_target="tpu_custom_call" | custom-call | flops 100000000 | bytes 1 | tf_op jit(solution)/shard_map/roll/pallas_call | solution.py:458
  21.1 0.0 collective-permute-done.from_second.down.own_second
  21.1 0.0 collective-permute-done.1.from_first.up.own_first
  21.1 0.1 narrow2.1
  21.2 2.1 %collective-permute-start.3 = (f32[2,280,128]{2,1,0:T(8,128)S(1)}, f32[2,280,128]{2,1,0:T(8,128)S(1)}, u32[]{:S(2)}, u32[]{:S(2)}) collective-permute-start(f32[2,280,128]{2,1,0:T(8,128)S(1)} %get-tuple-element.47), channel_id=1, source_target_pairs={{8,16},{16,8},{9,17},{17,9},{10,18},{18,10},{11,19},{19,11},{12,20... | collective-permute-start | bytes 860168 | tf_op jit(solution)/shard_map/ppermute | solution.py:45
  23.3 0.1 collective-permute-start.2
  23.4 0.6 %collective-permute-done.6.corner_second = f32[2,128,256]{2,1,0:T(8,128)S(1)} collective-permute-done((f32[2,128,256]{2,1,0:T(8,128)S(1)}, f32[2,128,256]{2,1,0:T(8,128)S(1)}, u32[]{:S(2)}, u32[]{:S(2)}) %collective-permute-start.6) | collective-permute-done | bytes 262176 | tf_op jit(solution)/shard_map/ppermute | solution.py:45
  24.0 0.0 collective-permute-done.7.corner_first
  24.0 3.1 %propagate.1 = (f32[2,128,256]{2,1,0:T(8,128)S(1)}, f32[2,128,256]{2,1,0:T(8,128)S(1)}, f32[4,128,256]{2,1,0:T(8,128)S(1)}, f32[4,128,256]{2,1,0:T(8,128)S(1)}, f32[2,256,512]{2,1,0:T(8,128)S(1)}) custom-call(s32[4,8,256]{2,1,0:T(8,128)S(1)} %get-tuple-element.53.marks, f32[2,2,256,256]{3,2,1,0:T(8,128)S(1)} %get-tuple-element.54.field, ...), custom_call_target="tpu_custom_call" | custom-call | flops 100000000 | bytes 1 | tf_op jit(solution)/shard_map/propagate/pallas_call | solution.py:458
  27.1 3.5 %collective-permute-start.10 = (f32[2,128,256]{2,1,0:T(8,128)S(1)}, f32[2,128,256]{2,1,0:T(8,128)S(1)}, u32[]{:S(2)}, u32[]{:S(2)}) collective-permute-start(f32[2,128,256]{2,1,0:T(8,128)S(1)} %get-tuple-element.65), channel_id=1, source_target_pairs={{1,2},{2,1},{3,4},{4,3},{5,6},{6,5},{9,10},{10,9},{11,12},{12,11},... | collective-permute-start | bytes 786440 | tf_op jit(solution)/shard_map/ppermute | solution.py:45
  30.6 0.1 collective-permute-start.11
  30.7 3.6 %collective-permute-start.8 = (f32[4,128,256]{2,1,0:T(8,128)S(1)}, f32[4,128,256]{2,1,0:T(8,128)S(1)}, u32[]{:S(2)}, u32[]{:S(2)}) collective-permute-start(f32[4,128,256]{2,1,0:T(8,128)S(1)} %get-tuple-element.62), channel_id=1, source_target_pairs={{1,2},{2,1},{3,4},{4,3},{5,6},{6,5},{9,10},{10,9},{11,12},{12,11},... | collective-permute-start | bytes 1572872 | tf_op jit(solution)/shard_map/ppermute | solution.py:45
  34.3 0.0 collective-permute-done.3.second.received
  34.3 0.1 collective-permute-start.9
  34.4 0.1 join3.1.total2_second
  34.4 0.4 collective-permute-done.10.from_second
  34.8 0.0 collective-permute-done.11.from_first
  34.8 0.1 narrow1.1
  34.9 1.7 %collective-permute-start.12 = (f32[2,256,128]{2,1,0:T(8,128)S(1)}, f32[2,256,128]{2,1,0:T(8,128)S(1)}, u32[]{:S(2)}, u32[]{:S(2)}) collective-permute-start(f32[2,256,128]{2,1,0:T(8,128)S(1)} %get-tuple-element.67), channel_id=1, source_target_pairs={{0,8},{8,0},{16,24},{24,16},{1,9},{9,1},{17,25},{25,17},{2,10},{10... | collective-permute-start | bytes 786440 | tf_op jit(solution)/shard_map/ppermute | solution.py:45
  36.6 4.1 %collective-permute-start.13 = (f32[2,256,128]{2,1,0:T(8,128)S(1)}, f32[2,256,128]{2,1,0:T(8,128)S(1)}, u32[]{:S(2)}, u32[]{:S(2)}) collective-permute-start(f32[2,256,128]{2,1,0:T(8,128)S(1)} %get-tuple-element.68), channel_id=1, source_target_pairs={{8,16},{16,8},{9,17},{17,9},{10,18},{18,10},{11,19},{19,11},{12,20... | collective-permute-start | bytes 786440 | tf_op jit(solution)/shard_map/ppermute | solution.py:45
  40.7 0.0 collective-permute-done.2.first.received
  40.7 4.6 %illuminate.1.scale = f32[256,256]{1,0:T(8,128)S(1)} custom-call(s32[2,1,2]{2,1,0:T(1,128)S(1)} %copy-done.4, f32[2,256,256]{2,1,0:T(8,128)S(1)} %copy-done.3, f32[4,136,256]{2,1,0:T(8,128)S(1)} %collective-permute-done.1.from_first.up.own_first, f32[4,136,256]{2,1,0:T(8,128)S(1)} %collective-permute-done.from_second.down.own_second, ...), custom_call_target="tpu_custom_call" | custom-call | flops 12000000000 | bytes 1 | tf_op jit(solution)/shard_map/illuminate/pallas_call | solution.py:458
  45.3 0.1 join2.1.total2_first
  45.4 0.0 collective-permute-done.8.inner_second
  45.4 0.0 collective-permute-done.9.inner_first
  45.4 1.0 %update2.1.begun = f32[2,2,256,256]{3,2,1,0:T(8,128)} custom-call(f32[2,2,256,256]{3,2,1,0:T(8,128)S(1)} %copy-done.1, f32[256,256]{1,0:T(8,128)S(1)} %illuminate.1.scale, f32[2,256,128]{2,1,0:T(8,128)S(1)} %join2.1.total2_first, f32[2,256,128]{2,1,0:T(8,128)S(1)} %join3.1.total2_second, f32[4,128,256]{2,1,0:T(8,128)S(1)} %collective-permute-done.8.inner_second, ...), custom_call_target="tpu_custom_call" | custom-call | flops 100000000 | bytes 1 | tf_op jit(solution)/shard_map/update2/pallas_call | solution.py:458
  46.4 0.0 collective-permute-done.12.first1
  46.4 4.2 %collective-permute-done.13.second1 = f32[2,256,128]{2,1,0:T(8,128)S(1)} collective-permute-done((f32[2,256,128]{2,1,0:T(8,128)S(1)}, f32[2,256,128]{2,1,0:T(8,128)S(1)}, u32[]{:S(2)}, u32[]{:S(2)}) %collective-permute-start.13) | collective-permute-done | bytes 262176 | tf_op jit(solution)/shard_map/ppermute | solution.py:45
  50.6 0.9 %update.1 = f32[2,2,256,256]{3,2,1,0:T(8,128)} custom-call(f32[2,2,256,256]{3,2,1,0:T(8,128)} %update2.1.begun, f32[2,256,128]{2,1,0:T(8,128)S(1)} %collective-permute-done.12.first1, f32[2,256,128]{2,1,0:T(8,128)S(1)} %collective-permute-done.13.second1, f32[2,2,256,256]{3,2,1,0:T(8,128)S(1)} %copy-done.1, ...), custom_call_target="tpu_custom_call", output_to_operand_aliasing={{}: (0, {})} | custom-call | flops 1000000000 | bytes 1 | tf_op jit(solution)/shard_map/update/pallas_call | solution.py:458
  (1 shorter events, 0.0 us)
Async XLA Ops:
  0.0 1.2 %copy-start = (f32[2,2,256,256]{3,2,1,0:T(8,128)S(1)}, f32[2,2,256,256]{3,2,1,0:T(8,128)}, u32[]{:S(2)}) copy-start(f32[2,2,256,256]{3,2,1,0:T(8,128)} %object_field.9) | copy-start | bytes 3145732
  1.2 4.5 %copy-start.1 = (f32[2,2,256,256]{3,2,1,0:T(8,128)S(1)}, f32[2,2,256,256]{3,2,1,0:T(8,128)}, u32[]{:S(2)}) copy-start(f32[2,2,256,256]{3,2,1,0:T(8,128)} %object_field.9) | copy-start | bytes 3145732
  1.2 4.5 %copy-start.2 = (bf16[4,256,512]{2,1,0:T(8,128)(2,1)S(1)}, bf16[4,256,512]{2,1,0:T(8,128)(2,1)}, u32[]{:S(2)}) copy-start(bf16[4,256,512]{2,1,0:T(8,128)(2,1)} %constant.2.clone.table) | copy-start | bytes 3145732
  1.2 4.5 %copy-start.5 = (bf16[2,1,2,256,256]{4,3,2,1,0:T(8,128)(2,1)S(1)}, bf16[2,1,2,256,256]{4,3,2,1,0:T(8,128)(2,1)}, u32[]{:S(2)}) copy-start(bf16[2,1,2,256,256]{4,3,2,1,0:T(8,128)(2,1)} %residual.1) | copy-start | bytes 1572868
  1.2 4.5 %copy-start.6 = (bf16[2,1,2,256,256]{4,3,2,1,0:T(8,128)(2,1)S(1)}, bf16[2,1,2,256,256]{4,3,2,1,0:T(8,128)(2,1)}, u32[]{:S(2)}) copy-start(bf16[2,1,2,256,256]{4,3,2,1,0:T(8,128)(2,1)} %wave.1) | copy-start | bytes 1572868
  1.3 4.4 %copy-start.4 = (s32[2,1,2]{2,1,0:T(1,128)S(1)}, s32[2,1,2]{2,1,0:T(1,128)}, u32[]{:S(2)}) copy-start(s32[2,1,2]{2,1,0:T(1,128)} %pos.1) | copy-start | bytes 52
  1.3 12.1 %collective-permute-start.4 = (f32[2,256,128]{2,1,0:T(8,128)S(1)}, f32[2,256,128]{2,1,0:T(8,128)S(1)}, u32[]{:S(2)}, u32[]{:S(2)}) collective-permute-start(f32[2,256,128]{2,1,0:T(8,128)S(1)} %get-tuple-element.48), channel_id=1, source_target_pairs={{0,8},{8,0},{16,24},{24,16},{1,9},{9,1},{17,25},{25,17},{2,10},{10... | collective-permute-start | bytes 786440 | tf_op jit(solution)/shard_map/ppermute | solution.py:45
  1.6 13.5 %collective-permute-start.5 = (f32[2,256,128]{2,1,0:T(8,128)S(1)}, f32[2,256,128]{2,1,0:T(8,128)S(1)}, u32[]{:S(2)}, u32[]{:S(2)}) collective-permute-start(f32[2,256,128]{2,1,0:T(8,128)S(1)} %get-tuple-element.49), channel_id=1, source_target_pairs={{8,16},{16,8},{9,17},{17,9},{10,18},{18,10},{11,19},{19,11},{12,20... | collective-permute-start | bytes 786440 | tf_op jit(solution)/shard_map/ppermute | solution.py:45
  9.0 12.2 %collective-permute-start = (f32[4,136,256]{2,1,0:T(8,128)S(1)}, f32[4,136,256]{2,1,0:T(8,128)S(1)}, u32[]{:S(2)}, u32[]{:S(2)}) collective-permute-start(f32[4,136,256]{2,1,0:T(8,128)S(1)} %get-tuple-element.37), channel_id=1, source_target_pairs={{1,2},{2,1},{3,4},{4,3},{5,6},{6,5},{9,10},{10,9},{11,12},{12,11},... | collective-permute-start | bytes 1671176 | tf_op jit(solution)/shard_map/ppermute | solution.py:45
  13.3 6.6 %copy-start.3 = (f32[2,256,256]{2,1,0:T(8,128)S(1)}, f32[2,256,256]{2,1,0:T(8,128)}, u32[]{:S(2)}) copy-start(f32[2,256,256]{2,1,0:T(8,128)} %probe.3) | copy-start | bytes 1572868
  13.3 7.8 %collective-permute-start.1 = (f32[4,136,256]{2,1,0:T(8,128)S(1)}, f32[4,136,256]{2,1,0:T(8,128)S(1)}, u32[]{:S(2)}, u32[]{:S(2)}) collective-permute-start(f32[4,136,256]{2,1,0:T(8,128)S(1)} %get-tuple-element.38), channel_id=1, source_target_pairs={{0,1},{1,0},{2,3},{3,2},{4,5},{5,4},{6,7},{7,6},{8,9},{9,8},{10,11... | collective-permute-start | bytes 1671176 | tf_op jit(solution)/shard_map/ppermute | solution.py:45
  15.2 8.8 %collective-permute-start.6 = (f32[2,128,256]{2,1,0:T(8,128)S(1)}, f32[2,128,256]{2,1,0:T(8,128)S(1)}, u32[]{:S(2)}, u32[]{:S(2)}) collective-permute-start(f32[2,128,256]{2,1,0:T(8,128)S(1)} %get-tuple-element.50), channel_id=1, source_target_pairs={{1,2},{2,1},{3,4},{4,3},{5,6},{6,5},{9,10},{10,9},{11,12},{12,11},... | collective-permute-start | bytes 786440 | tf_op jit(solution)/shard_map/ppermute | solution.py:45
  19.8 4.2 %collective-permute-start.7 = (f32[2,128,256]{2,1,0:T(8,128)S(1)}, f32[2,128,256]{2,1,0:T(8,128)S(1)}, u32[]{:S(2)}, u32[]{:S(2)}) collective-permute-start(f32[2,128,256]{2,1,0:T(8,128)S(1)} %get-tuple-element.51), channel_id=1, source_target_pairs={{0,1},{1,0},{2,3},{3,2},{4,5},{5,4},{6,7},{7,6},{8,9},{9,8},{10,11... | collective-permute-start | bytes 786440 | tf_op jit(solution)/shard_map/ppermute | solution.py:45
  21.2 13.1 %collective-permute-start.3 = (f32[2,280,128]{2,1,0:T(8,128)S(1)}, f32[2,280,128]{2,1,0:T(8,128)S(1)}, u32[]{:S(2)}, u32[]{:S(2)}) collective-permute-start(f32[2,280,128]{2,1,0:T(8,128)S(1)} %get-tuple-element.47), channel_id=1, source_target_pairs={{8,16},{16,8},{9,17},{17,9},{10,18},{18,10},{11,19},{19,11},{12,20... | collective-permute-start | bytes 860168 | tf_op jit(solution)/shard_map/ppermute | solution.py:45
  23.3 17.3 %collective-permute-start.2 = (f32[2,280,128]{2,1,0:T(8,128)S(1)}, f32[2,280,128]{2,1,0:T(8,128)S(1)}, u32[]{:S(2)}, u32[]{:S(2)}) collective-permute-start(f32[2,280,128]{2,1,0:T(8,128)S(1)} %get-tuple-element.46), channel_id=1, source_target_pairs={{0,8},{8,0},{16,24},{24,16},{1,9},{9,1},{17,25},{25,17},{2,10},{10... | collective-permute-start | bytes 860168 | tf_op jit(solution)/shard_map/ppermute | solution.py:45
  27.1 7.7 %collective-permute-start.10 = (f32[2,128,256]{2,1,0:T(8,128)S(1)}, f32[2,128,256]{2,1,0:T(8,128)S(1)}, u32[]{:S(2)}, u32[]{:S(2)}) collective-permute-start(f32[2,128,256]{2,1,0:T(8,128)S(1)} %get-tuple-element.65), channel_id=1, source_target_pairs={{1,2},{2,1},{3,4},{4,3},{5,6},{6,5},{9,10},{10,9},{11,12},{12,11},... | collective-permute-start | bytes 786440 | tf_op jit(solution)/shard_map/ppermute | solution.py:45
  30.6 4.2 %collective-permute-start.11 = (f32[2,128,256]{2,1,0:T(8,128)S(1)}, f32[2,128,256]{2,1,0:T(8,128)S(1)}, u32[]{:S(2)}, u32[]{:S(2)}) collective-permute-start(f32[2,128,256]{2,1,0:T(8,128)S(1)} %get-tuple-element.66), channel_id=1, source_target_pairs={{0,1},{1,0},{2,3},{3,2},{4,5},{5,4},{6,7},{7,6},{8,9},{9,8},{10,11... | collective-permute-start | bytes 786440 | tf_op jit(solution)/shard_map/ppermute | solution.py:45
  30.7 14.7 %collective-permute-start.8 = (f32[4,128,256]{2,1,0:T(8,128)S(1)}, f32[4,128,256]{2,1,0:T(8,128)S(1)}, u32[]{:S(2)}, u32[]{:S(2)}) collective-permute-start(f32[4,128,256]{2,1,0:T(8,128)S(1)} %get-tuple-element.62), channel_id=1, source_target_pairs={{1,2},{2,1},{3,4},{4,3},{5,6},{6,5},{9,10},{10,9},{11,12},{12,11},... | collective-permute-start | bytes 1572872 | tf_op jit(solution)/shard_map/ppermute | solution.py:45
  34.3 11.1 %collective-permute-start.9 = (f32[4,128,256]{2,1,0:T(8,128)S(1)}, f32[4,128,256]{2,1,0:T(8,128)S(1)}, u32[]{:S(2)}, u32[]{:S(2)}) collective-permute-start(f32[4,128,256]{2,1,0:T(8,128)S(1)} %get-tuple-element.63), channel_id=1, source_target_pairs={{0,1},{1,0},{2,3},{3,2},{4,5},{5,4},{6,7},{7,6},{8,9},{9,8},{10,11... | collective-permute-start | bytes 1572872 | tf_op jit(solution)/shard_map/ppermute | solution.py:45
  34.9 11.5 %collective-permute-start.12 = (f32[2,256,128]{2,1,0:T(8,128)S(1)}, f32[2,256,128]{2,1,0:T(8,128)S(1)}, u32[]{:S(2)}, u32[]{:S(2)}) collective-permute-start(f32[2,256,128]{2,1,0:T(8,128)S(1)} %get-tuple-element.67), channel_id=1, source_target_pairs={{0,8},{8,0},{16,24},{24,16},{1,9},{9,1},{17,25},{25,17},{2,10},{10... | collective-permute-start | bytes 786440 | tf_op jit(solution)/shard_map/ppermute | solution.py:45
  36.6 14.0 %collective-permute-start.13 = (f32[2,256,128]{2,1,0:T(8,128)S(1)}, f32[2,256,128]{2,1,0:T(8,128)S(1)}, u32[]{:S(2)}, u32[]{:S(2)}) collective-permute-start(f32[2,256,128]{2,1,0:T(8,128)S(1)} %get-tuple-element.68), channel_id=1, source_target_pairs={{8,16},{16,8},{9,17},{17,9},{10,18},{18,10},{11,19},{19,11},{12,20... | collective-permute-start | bytes 786440 | tf_op jit(solution)/shard_map/ppermute | solution.py:45

commit v6 on v5

--- a/solution.py
+++ b/solution.py
@@ -43,6 +43,17 @@
 
 def swapped(value, axis, first):
     return lax.ppermute(value, axis, swap_pairs(lax.axis_size(axis), first))
+
+
+def around(value, axis):
+    count = lax.axis_size(axis)
+    if count % 2 or count < 4:
+        return swapped(value, axis, 1)
+    out, back = [], []
+    for low in range(1, count - 1, 2):
+        out += [(low, low + 2), (low + 1, low - 1)]
+        back += [(low + 2, low + 1), (low - 1, low)]
+    return lax.ppermute(lax.ppermute(value, axis, out), axis, back)
 
 
 def dot(a, b):
@@ -334,7 +345,7 @@
     for copy in copies:
         copy.wait()
 
-    shifts = []
+    upper, lower = [], []
     for down in (-1, 0, 1):
         for along in (-1, 0, 1):
             if along == 0:
@@ -351,9 +362,11 @@
                 top = r - half + window * down
                 left = c - half + window * along
                 top = jnp.where(valid == 1, top, window)
-                shifts.append((top, left, r, c))
-
-    def rows_at(index, carry):
+                for reached, half_at in ((upper, -1), (lower, 1)):
+                    if down in (0, half_at):
+                        reached.append((top, left, r, c))
+
+    def rows_at(index, carry, shifts):
         start = index * CHUNK
         row = lax.broadcasted_iota(jnp.int32, (CHUNK, window), 0) + start
         col = lax.broadcasted_iota(jnp.int32, (CHUNK, window), 1)
@@ -369,7 +382,8 @@
         scale[pl.ds(pl.multiple_of(start, CHUNK), CHUNK), :] = 1.0 / (total + ridge)
         return carry
 
-    lax.fori_loop(0, window // CHUNK, rows_at, 0)
+    lax.fori_loop(0, half // CHUNK, functools.partial(rows_at, shifts=upper), 0)
+    lax.fori_loop(half // CHUNK, window // CHUNK, functools.partial(rows_at, shifts=lower), 0)
 
 
 def narrow_noted(notes, middle, from_second, from_first, first, second):
@@ -388,6 +402,12 @@
         ref[0, window + 2 * size :] = below
 
 
+def narrow_parts(middle, from_second, from_first, first, second_re, second_im, second):
+    narrow_outer(middle, from_second, from_first, first, second)
+    second_re[0] = second[0]
+    second_im[0] = second[1]
+
+
 def narrow_outer(middle, from_second, from_first, first, second):
     half = first.shape[-1]
     odd_x = lax.rem(lax.axis_index("gx"), 2)
@@ -430,7 +450,7 @@
 
 
 def update_first(
-    begun, first1, second1, object_field, scale, middle1, inner_second, inner_first, out, value, sems
+    begun, first1, second1_re, second1_im, object_field, scale, middle1, inner_second, inner_first, out, value, sems
 ):
     del begun
     window = scale.shape[-1]
@@ -441,7 +461,7 @@
     for part in range(2):
         for received, base in ((inner_first, (1 - odd_y) * half), (inner_second, odd_y * half)):
             rows = pl.ds(pl.multiple_of(base, half), half)
-            outer = jnp.concatenate(sides(odd_x, first1[part, rows], second1[part, rows]), axis=1)
+            outer = jnp.concatenate(sides(odd_x, first1[part, rows], (second1_re, second1_im)[part][0, rows]), axis=1)
             total = middle1[part, rows, half : 3 * half] + received[part] + outer
             value[part, rows] = object_field[0, part, rows] - total * scale[rows]
         copies.append(written(value.at[part], out.at[0], part, sems.at[part]))
@@ -548,12 +568,21 @@
     (total2_second,) = call(
         functools.partial(join, low=True), [strip], [VMEM] * 2, (middle2, got_second2), micros=1.0, name="join3"
     )
-    middle1, total2_second = barrier((middle1, total2_second))
-    first1, second1 = call(
-        narrow_outer, [strip] * 2, [VMEM] * 3, (middle1, from_outer_second, from_outer_first), micros=0.2, name="narrow1"
+    (total2_first,) = call(
+        functools.partial(join, low=False), [strip], [VMEM] * 2, (middle2, got_first2), micros=0.5, name="join2"
+    )
+    middle1, total2_first, total2_second = barrier((middle1, total2_first, total2_second))
+    first1, second1_re, second1_im = call(
+        narrow_parts,
+        [strip] + [(1, window, half)] * 2,
+        [VMEM] * 3,
+        (middle1, from_outer_second, from_outer_first),
+        [pltpu.VMEM(strip, F32)],
+        micros=0.2, name="narrow1",
     )
     got_first1 = swapped(first1, "gx", 0)
-    got_second1 = swapped(second1, "gx", 1)
+    got_second1_im = around(second1_im, "gx")
+    got_second1_re = swapped(second1_re, "gx", 1)
     from_inner_first = swapped(inner_first, "gy", 0)
     from_inner_second = swapped(inner_second, "gy", 1)
 
@@ -563,10 +592,7 @@
         [SMEM] + [VMEM] * 5,
         (positions, probe, from_up2, from_down2, got_first2, got_second2),
         [twice(), pltpu.SMEM((8 * size, half), F32), pltpu.SemaphoreType.DMA((4,))],
-        micros=12.0, name="illuminate",
-    )
-    (total2_first,) = call(
-        functools.partial(join, low=False), [strip], [VMEM] * 2, (middle2, got_first2), micros=0.5, name="join2"
+        micros=2.5, name="illuminate",
     )
     value = pltpu.VMEM(fields_shape[1:], F32)
     (begun,) = call(
@@ -580,8 +606,9 @@
     (new_object,) = call(
         update_first,
         [object_field.shape],
-        [ANY] + [VMEM] * 7,
-        (begun, got_first1, got_second1, object_field, scale, middle1, from_inner_second, from_inner_first),
+        [ANY] + [VMEM] * 8,
+        (begun, got_first1, got_second1_re, got_second1_im, object_field, scale, middle1)
+        + (from_inner_second, from_inner_first),
         [value, pltpu.SemaphoreType.DMA((2,))],
         out_specs=[ANY], aliases={0: 0}, micros=1.0, name="update",
     )

time: 52.2 us -> 51.6 us (0.989)
  the two profiles are of different devices: /device:TPU:11 before, /device:TPU:0 now
where the time goes in v6:
time: 51.6 us; the launch traced here: 51.2 us
  starting transfers between devices  32.5 us (63%)
  Pallas kernels  13.5 us (26%)
  waiting for transfers between devices  3.69 us (7%)
  local copies, waits for them, and re-layouts  1.25 us (2%)
    ppermute x14, starting transfers between devices, swapped(): return lax.ppermute(value, axis, swap_pairs(lax.axis_size(axis), first))  29.2 us
    pallas_call x12, Pallas kernels, call(): pl.pallas_call(body, out_shape=[x if hasattr(x, 'dtype') else jax.ShapeDt...  13.5 us
    ppermute x2, waiting for transfers between devices, around(): return lax.ppermute(lax.ppermute(value, axis, out), axis, back)  3.66 us
    ppermute x2, starting transfers between devices, around(): return lax.ppermute(lax.ppermute(value, axis, out), axis, back)  3.27 us
    unnamed x14, local copies, waits for them, and re-layouts  1.25 us
  transfers between devices with their start and end apart: 16, of which 1 were waited for; matrix products, arithmetic and copies ran while one was open for 0% of the time, Pallas kernels for 25%

profile of v6, /device:TPU:0, one launch (start us, length us, event | category | flops | bytes accessed | tf_op | source)
XLA Modules:
  0.0 51.2 jit_solution(8344088793951987398)
XLA Ops:
  0.0 0.0 copy-start
  0.0 1.2 %copy-done = f32[2,2,256,256]{3,2,1,0:T(8,128)S(1)} copy-done((f32[2,2,256,256]{3,2,1,0:T(8,128)S(1)}, f32[2,2,256,256]{3,2,1,0:T(8,128)}, u32[]{:S(2)}) %copy-start) | copy-done | bytes 1048600
  1.2 0.0 copy-start.1
  1.2 0.0 copy-start.2
  1.2 0.0 copy-start.5
  1.2 0.0 copy-start.6
  1.2 0.1 edges.1
  1.3 0.0 copy-start.4
  1.3 3.0 %collective-permute-start.4 = (f32[2,256,128]{2,1,0:T(8,128)S(1)}, f32[2,256,128]{2,1,0:T(8,128)S(1)}, u32[]{:S(2)}, u32[]{:S(2)}) collective-permute-start(f32[2,256,128]{2,1,0:T(8,128)S(1)} %get-tuple-element.50), channel_id=1, source_target_pairs={{0,8},{8,0},{16,24},{24,16},{1,9},{9,1},{17,25},{25,17},{2,10},{10... | collective-permute-start | bytes 786440 | tf_op jit(solution)/shard_map/ppermute | solution.py:45
  4.3 0.7 %collective-permute-start.5 = (f32[2,256,128]{2,1,0:T(8,128)S(1)}, f32[2,256,128]{2,1,0:T(8,128)S(1)}, u32[]{:S(2)}, u32[]{:S(2)}) collective-permute-start(f32[2,256,128]{2,1,0:T(8,128)S(1)} %get-tuple-element.51), channel_id=1, source_target_pairs={{8,16},{16,8},{9,17},{17,9},{10,18},{18,10},{11,19},{19,11},{12,20... | collective-permute-start | bytes 786440 | tf_op jit(solution)/shard_map/ppermute | solution.py:45
  5.0 0.0 copy-done.1
  5.0 0.0 copy-done.2
  5.0 0.0 copy-done.5
  5.0 0.0 copy-done.6
  5.0 0.0 copy-done.4
  5.0 3.2 %detect.1 = (f32[2,2,256,256]{3,2,1,0:T(8,128)S(1)}, f32[4,136,256]{2,1,0:T(8,128)S(1)}, f32[4,136,256]{2,1,0:T(8,128)S(1)}, f32[2,128,256]{2,1,0:T(8,128)S(1)},...) custom-call(s32[2,1,2]{2,1,0:T(1,128)S(1)} %copy-done.4, ...), custom_call_target="tpu_custom_call" | custom-call | flops 12000000000 | bytes 1 | tf_op jit(solution)/shard_map/detect/pallas_call | solution.py:478
  8.2 0.7 %collective-permute-start = (f32[4,136,256]{2,1,0:T(8,128)S(1)}, f32[4,136,256]{2,1,0:T(8,128)S(1)}, u32[]{:S(2)}, u32[]{:S(2)}) collective-permute-start(f32[4,136,256]{2,1,0:T(8,128)S(1)} %get-tuple-element.39), channel_id=1, source_target_pairs={{1,2},{2,1},{3,4},{4,3},{5,6},{6,5},{9,10},{10,9},{11,12},{12,11},... | collective-permute-start | bytes 1671176 | tf_op jit(solution)/shard_map/ppermute | solution.py:45
  8.9 0.0 copy-start.3
  9.0 3.0 %collective-permute-start.1 = (f32[4,136,256]{2,1,0:T(8,128)S(1)}, f32[4,136,256]{2,1,0:T(8,128)S(1)}, u32[]{:S(2)}, u32[]{:S(2)}) collective-permute-start(f32[4,136,256]{2,1,0:T(8,128)S(1)} %get-tuple-element.40), channel_id=1, source_target_pairs={{0,1},{1,0},{2,3},{3,2},{4,5},{5,4},{6,7},{7,6},{8,9},{9,8},{10,11... | collective-permute-start | bytes 1671176 | tf_op jit(solution)/shard_map/ppermute | solution.py:45
  11.9 0.0 collective-permute-done.4.from_first.halo_first
  11.9 0.0 collective-permute-done.5.from_second.halo_second
  12.0 0.7 %collective-permute-start.6 = (f32[2,128,256]{2,1,0:T(8,128)S(1)}, f32[2,128,256]{2,1,0:T(8,128)S(1)}, u32[]{:S(2)}, u32[]{:S(2)}) collective-permute-start(f32[2,128,256]{2,1,0:T(8,128)S(1)} %get-tuple-element.52), channel_id=1, source_target_pairs={{1,2},{2,1},{3,4},{4,3},{5,6},{6,5},{9,10},{10,9},{11,12},{12,11},... | collective-permute-start | bytes 786440 | tf_op jit(solution)/shard_map/ppermute | solution.py:45
  12.7 3.1 %collective-permute-start.7 = (f32[2,128,256]{2,1,0:T(8,128)S(1)}, f32[2,128,256]{2,1,0:T(8,128)S(1)}, u32[]{:S(2)}, u32[]{:S(2)}) collective-permute-start(f32[2,128,256]{2,1,0:T(8,128)S(1)} %get-tuple-element.53), channel_id=1, source_target_pairs={{0,1},{1,0},{2,3},{3,2},{4,5},{5,4},{6,7},{7,6},{8,9},{9,8},{10,11... | collective-permute-start | bytes 786440 | tf_op jit(solution)/shard_map/ppermute | solution.py:45
  15.7 0.0 copy-done.3
  15.7 1.2 %roll.1 = (f32[2,2,256,256]{3,2,1,0:T(8,128)S(1)}, f32[2,2,256,256]{3,2,1,0:T(8,128)S(1)}) custom-call(s32[2,1,2]{2,1,0:T(1,128)S(1)} %copy-done.4, f32[2,2,256,256]{3,2,1,0:T(8,128)S(1)} %get-tuple-element.41.field, f32[2,256,256]{2,1,0:T(8,128)S(1)} %copy-done.3), custom_call_target="tpu_custom_call" | custom-call | flops 100000000 | bytes 1 | tf_op jit(solution)/shard_map/roll/pallas_call | solution.py:478
  17.0 0.0 collective-permute-done.from_second.down.own_second
  17.0 0.0 collective-permute-done.1.from_first.up.own_first
  17.0 0.1 narrow2.1
  17.1 7.0 %collective-permute-start.2 = (f32[2,280,128]{2,1,0:T(8,128)S(1)}, f32[2,280,128]{2,1,0:T(8,128)S(1)}, u32[]{:S(2)}, u32[]{:S(2)}) collective-permute-start(f32[2,280,128]{2,1,0:T(8,128)S(1)} %get-tuple-element.48), channel_id=1, source_target_pairs={{0,8},{8,0},{16,24},{24,16},{1,9},{9,1},{17,25},{25,17},{2,10},{10... | collective-permute-start | bytes 860168 | tf_op jit(solution)/shard_map/ppermute | solution.py:45
  24.0 0.7 %collective-permute-start.3 = (f32[2,280,128]{2,1,0:T(8,128)S(1)}, f32[2,280,128]{2,1,0:T(8,128)S(1)}, u32[]{:S(2)}, u32[]{:S(2)}) collective-permute-start(f32[2,280,128]{2,1,0:T(8,128)S(1)} %get-tuple-element.49), channel_id=1, source_target_pairs={{8,16},{16,8},{9,17},{17,9},{10,18},{18,10},{11,19},{19,11},{12,20... | collective-permute-start | bytes 860168 | tf_op jit(solution)/shard_map/ppermute | solution.py:45
  24.7 0.0 collective-permute-done.6.corner_second
  24.7 0.0 collective-permute-done.7.corner_first
  24.7 3.1 %propagate.1 = (f32[2,128,256]{2,1,0:T(8,128)S(1)}, f32[2,128,256]{2,1,0:T(8,128)S(1)}, f32[4,128,256]{2,1,0:T(8,128)S(1)}, f32[4,128,256]{2,1,0:T(8,128)S(1)}, f32[2,256,512]{2,1,0:T(8,128)S(1)}) custom-call(s32[4,8,256]{2,1,0:T(8,128)S(1)} %get-tuple-element.55.marks, f32[2,2,256,256]{3,2,1,0:T(8,128)S(1)} %get-tuple-element.56.field, ...), custom_call_target="tpu_custom_call" | custom-call | flops 100000000 | bytes 1 | tf_op jit(solution)/shard_map/propagate/pallas_call | solution.py:478
  27.8 0.7 %collective-permute-start.10 = (f32[2,128,256]{2,1,0:T(8,128)S(1)}, f32[2,128,256]{2,1,0:T(8,128)S(1)}, u32[]{:S(2)}, u32[]{:S(2)}) collective-permute-start(f32[2,128,256]{2,1,0:T(8,128)S(1)} %get-tuple-element.68), channel_id=1, source_target_pairs={{1,2},{2,1},{3,4},{4,3},{5,6},{6,5},{9,10},{10,9},{11,12},{12,11},... | collective-permute-start | bytes 786440 | tf_op jit(solution)/shard_map/ppermute | solution.py:45
  28.5 3.0 %collective-permute-start.11 = (f32[2,128,256]{2,1,0:T(8,128)S(1)}, f32[2,128,256]{2,1,0:T(8,128)S(1)}, u32[]{:S(2)}, u32[]{:S(2)}) collective-permute-start(f32[2,128,256]{2,1,0:T(8,128)S(1)} %get-tuple-element.69), channel_id=1, source_target_pairs={{0,1},{1,0},{2,3},{3,2},{4,5},{5,4},{6,7},{7,6},{8,9},{9,8},{10,11... | collective-permute-start | bytes 786440 | tf_op jit(solution)/shard_map/ppermute | solution.py:45
  31.5 0.7 %collective-permute-start.8 = (f32[4,128,256]{2,1,0:T(8,128)S(1)}, f32[4,128,256]{2,1,0:T(8,128)S(1)}, u32[]{:S(2)}, u32[]{:S(2)}) collective-permute-start(f32[4,128,256]{2,1,0:T(8,128)S(1)} %get-tuple-element.65), channel_id=1, source_target_pairs={{1,2},{2,1},{3,4},{4,3},{5,6},{6,5},{9,10},{10,9},{11,12},{12,11},... | collective-permute-start | bytes 1572872 | tf_op jit(solution)/shard_map/ppermute | solution.py:45
  32.2 0.0 collective-permute-done.2.first.received
  32.2 3.0 %collective-permute-start.9 = (f32[4,128,256]{2,1,0:T(8,128)S(1)}, f32[4,128,256]{2,1,0:T(8,128)S(1)}, u32[]{:S(2)}, u32[]{:S(2)}) collective-permute-start(f32[4,128,256]{2,1,0:T(8,128)S(1)} %get-tuple-element.66), channel_id=1, source_target_pairs={{0,1},{1,0},{2,3},{3,2},{4,5},{5,4},{6,7},{7,6},{8,9},{9,8},{10,11... | collective-permute-start | bytes 1572872 | tf_op jit(solution)/shard_map/ppermute | solution.py:45
  35.3 0.0 collective-permute-done.3.second.received
  35.3 0.1 join3.1.total2_second
  35.3 0.0 collective-permute-done.10.from_second
  35.3 0.0 collective-permute-done.11.from_first
  35.3 0.1 narrow1.1
  35.4 1.3 %collective-permute-start.14 = (f32[1,256,128]{2,1,0:T(8,128)S(1)}, f32[1,256,128]{2,1,0:T(8,128)S(1)}, u32[]{:S(2)}, u32[]{:S(2)}) collective-permute-start(f32[1,256,128]{2,1,0:T(8,128)S(1)} %get-tuple-element.72), channel_id=1, source_target_pairs={{8,24},{16,0},{9,25},{17,1},{10,26},{18,2},{11,27},{19,3},{12,28},... | collective-permute-start | bytes 393224 | tf_op jit(solution)/shard_map/ppermute | solution.py:56
  36.7 2.5 %collective-permute-start.12 = (f32[2,256,128]{2,1,0:T(8,128)S(1)}, f32[2,256,128]{2,1,0:T(8,128)S(1)}, u32[]{:S(2)}, u32[]{:S(2)}) collective-permute-start(f32[2,256,128]{2,1,0:T(8,128)S(1)} %get-tuple-element.70), channel_id=1, source_target_pairs={{0,8},{8,0},{16,24},{24,16},{1,9},{9,1},{17,25},{25,17},{2,10},{10... | collective-permute-start | bytes 786440 | tf_op jit(solution)/shard_map/ppermute | solution.py:45
  39.2 0.7 %collective-permute-start.13 = (f32[1,256,128]{2,1,0:T(8,128)S(1)}, f32[1,256,128]{2,1,0:T(8,128)S(1)}, u32[]{:S(2)}, u32[]{:S(2)}) collective-permute-start(f32[1,256,128]{2,1,0:T(8,128)S(1)} %get-tuple-element.71), channel_id=1, source_target_pairs={{8,16},{16,8},{9,17},{17,9},{10,18},{18,10},{11,19},{19,11},{12,20... | collective-permute-start | bytes 393224 | tf_op jit(solution)/shard_map/ppermute | solution.py:45
  39.9 3.7 %collective-permute-done.14 = f32[1,256,128]{2,1,0:T(8,128)S(1)} collective-permute-done((f32[1,256,128]{2,1,0:T(8,128)S(1)}, f32[1,256,128]{2,1,0:T(8,128)S(1)}, u32[]{:S(2)}, u32[]{:S(2)}) %collective-permute-start.14) | collective-permute-done | bytes 131104 | tf_op jit(solution)/shard_map/ppermute | solution.py:56
  43.5 2.0 %collective-permute-start.15 = (f32[1,256,128]{2,1,0:T(8,128)S(1)}, f32[1,256,128]{2,1,0:T(8,128)S(1)}, u32[]{:S(2)}, u32[]{:S(2)}) collective-permute-start(f32[1,256,128]{2,1,0:T(8,128)S(1)} %collective-permute-done.14), channel_id=1, source_target_pairs={{24,16},{0,8},{25,17},{1,9},{26,18},{2,10},{27,19},{3,11},{28,20},... | collective-permute-start | bytes 393224 | tf_op jit(solution)/shard_map/ppermute | solution.py:56
  45.5 3.8 %illuminate.1.scale = f32[256,256]{1,0:T(8,128)S(1)} custom-call(s32[2,1,2]{2,1,0:T(1,128)S(1)} %copy-done.4, f32[2,256,256]{2,1,0:T(8,128)S(1)} %copy-done.3, f32[4,136,256]{2,1,0:T(8,128)S(1)} %collective-permute-done.1.from_first.up.own_first, f32[4,136,256]{2,1,0:T(8,128)S(1)} %collective-permute-done.from_second.down.own_second, ...), custom_call_target="tpu_custom_call" | custom-call | flops 2500000000 | bytes 1 | tf_op jit(solution)/shard_map/illuminate/pallas_call | solution.py:478
  49.3 0.0 collective-permute-done.8.inner_second
  49.3 0.0 collective-permute-done.9.inner_first
  49.4 1.0 %update2.1.begun = f32[2,2,256,256]{3,2,1,0:T(8,128)} custom-call(f32[2,2,256,256]{3,2,1,0:T(8,128)S(1)} %copy-done.1, f32[256,256]{1,0:T(8,128)S(1)} %illuminate.1.scale, f32[2,256,128]{2,1,0:T(8,128)S(1)} %join2.1.total2_first, f32[2,256,128]{2,1,0:T(8,128)S(1)} %join3.1.total2_second, f32[4,128,256]{2,1,0:T(8,128)S(1)} %collective-permute-done.8.inner_second, ...), custom_call_target="tpu_custom_call" | custom-call | flops 100000000 | bytes 1 | tf_op jit(solution)/shard_map/update2/pallas_call | solution.py:478
  50.3 0.0 collective-permute-done.13.second1_re
  50.3 0.0 collective-permute-done.15.second1_im
  50.3 0.0 collective-permute-done.12.first1
  50.3 0.9 %update.1 = f32[2,2,256,256]{3,2,1,0:T(8,128)} custom-call(f32[2,2,256,256]{3,2,1,0:T(8,128)} %update2.1.begun, f32[2,256,128]{2,1,0:T(8,128)S(1)} %collective-permute-done.12.first1, f32[1,256,128]{2,1,0:T(8,128)S(1)} %collective-permute-done.13.second1_re, f32[1,256,128]{2,1,0:T(8,128)S(1)} %collective-permute-done.15.second1_im, ...), custom_call_target="tpu_custom_call", output_to_operand_aliasing={{}: (0, {})} | custom-call | flops 1000000000 | bytes 1 | tf_op jit(solution)/shard_map/update/pallas_call | solution.py:478
  (2 shorter events, 0.1 us)
Async XLA Ops:
  0.0 1.2 %copy-start = (f32[2,2,256,256]{3,2,1,0:T(8,128)S(1)}, f32[2,2,256,256]{3,2,1,0:T(8,128)}, u32[]{:S(2)}) copy-start(f32[2,2,256,256]{3,2,1,0:T(8,128)} %object_field.9) | copy-start | bytes 3145732
  1.2 3.8 %copy-start.1 = (f32[2,2,256,256]{3,2,1,0:T(8,128)S(1)}, f32[2,2,256,256]{3,2,1,0:T(8,128)}, u32[]{:S(2)}) copy-start(f32[2,2,256,256]{3,2,1,0:T(8,128)} %object_field.9) | copy-start | bytes 3145732
  1.2 3.8 %copy-start.2 = (bf16[4,256,512]{2,1,0:T(8,128)(2,1)S(1)}, bf16[4,256,512]{2,1,0:T(8,128)(2,1)}, u32[]{:S(2)}) copy-start(bf16[4,256,512]{2,1,0:T(8,128)(2,1)} %constant.2.clone.table) | copy-start | bytes 3145732
  1.2 3.8 %copy-start.5 = (bf16[2,1,2,256,256]{4,3,2,1,0:T(8,128)(2,1)S(1)}, bf16[2,1,2,256,256]{4,3,2,1,0:T(8,128)(2,1)}, u32[]{:S(2)}) copy-start(bf16[2,1,2,256,256]{4,3,2,1,0:T(8,128)(2,1)} %residual.1) | copy-start | bytes 1572868
  1.2 3.8 %copy-start.6 = (bf16[2,1,2,256,256]{4,3,2,1,0:T(8,128)(2,1)S(1)}, bf16[2,1,2,256,256]{4,3,2,1,0:T(8,128)(2,1)}, u32[]{:S(2)}) copy-start(bf16[2,1,2,256,256]{4,3,2,1,0:T(8,128)(2,1)} %wave.1) | copy-start | bytes 1572868
  1.3 3.7 %copy-start.4 = (s32[2,1,2]{2,1,0:T(1,128)S(1)}, s32[2,1,2]{2,1,0:T(1,128)}, u32[]{:S(2)}) copy-start(s32[2,1,2]{2,1,0:T(1,128)} %pos.1) | copy-start | bytes 52
  1.3 10.6 %collective-permute-start.4 = (f32[2,256,128]{2,1,0:T(8,128)S(1)}, f32[2,256,128]{2,1,0:T(8,128)S(1)}, u32[]{:S(2)}, u32[]{:S(2)}) collective-permute-start(f32[2,256,128]{2,1,0:T(8,128)S(1)} %get-tuple-element.50), channel_id=1, source_target_pairs={{0,8},{8,0},{16,24},{24,16},{1,9},{9,1},{17,25},{25,17},{2,10},{10... | collective-permute-start | bytes 786440 | tf_op jit(solution)/shard_map/ppermute | solution.py:45
  4.3 7.6 %collective-permute-start.5 = (f32[2,256,128]{2,1,0:T(8,128)S(1)}, f32[2,256,128]{2,1,0:T(8,128)S(1)}, u32[]{:S(2)}, u32[]{:S(2)}) collective-permute-start(f32[2,256,128]{2,1,0:T(8,128)S(1)} %get-tuple-element.51), channel_id=1, source_target_pairs={{8,16},{16,8},{9,17},{17,9},{10,18},{18,10},{11,19},{19,11},{12,20... | collective-permute-start | bytes 786440 | tf_op jit(solution)/shard_map/ppermute | solution.py:45
  8.2 8.7 %collective-permute-start = (f32[4,136,256]{2,1,0:T(8,128)S(1)}, f32[4,136,256]{2,1,0:T(8,128)S(1)}, u32[]{:S(2)}, u32[]{:S(2)}) collective-permute-start(f32[4,136,256]{2,1,0:T(8,128)S(1)} %get-tuple-element.39), channel_id=1, source_target_pairs={{1,2},{2,1},{3,4},{4,3},{5,6},{6,5},{9,10},{10,9},{11,12},{12,11},... | collective-permute-start | bytes 1671176 | tf_op jit(solution)/shard_map/ppermute | solution.py:45
  8.9 6.8 %copy-start.3 = (f32[2,256,256]{2,1,0:T(8,128)S(1)}, f32[2,256,256]{2,1,0:T(8,128)}, u32[]{:S(2)}) copy-start(f32[2,256,256]{2,1,0:T(8,128)} %probe.3) | copy-start | bytes 1572868
  9.0 8.0 %collective-permute-start.1 = (f32[4,136,256]{2,1,0:T(8,128)S(1)}, f32[4,136,256]{2,1,0:T(8,128)S(1)}, u32[]{:S(2)}, u32[]{:S(2)}) collective-permute-start(f32[4,136,256]{2,1,0:T(8,128)S(1)} %get-tuple-element.40), channel_id=1, source_target_pairs={{0,1},{1,0},{2,3},{3,2},{4,5},{5,4},{6,7},{7,6},{8,9},{9,8},{10,11... | collective-permute-start | bytes 1671176 | tf_op jit(solution)/shard_map/ppermute | solution.py:45
  12.0 12.7 %collective-permute-start.6 = (f32[2,128,256]{2,1,0:T(8,128)S(1)}, f32[2,128,256]{2,1,0:T(8,128)S(1)}, u32[]{:S(2)}, u32[]{:S(2)}) collective-permute-start(f32[2,128,256]{2,1,0:T(8,128)S(1)} %get-tuple-element.52), channel_id=1, source_target_pairs={{1,2},{2,1},{3,4},{4,3},{5,6},{6,5},{9,10},{10,9},{11,12},{12,11},... | collective-permute-start | bytes 786440 | tf_op jit(solution)/shard_map/ppermute | solution.py:45
  12.7 12.1 %collective-permute-start.7 = (f32[2,128,256]{2,1,0:T(8,128)S(1)}, f32[2,128,256]{2,1,0:T(8,128)S(1)}, u32[]{:S(2)}, u32[]{:S(2)}) collective-permute-start(f32[2,128,256]{2,1,0:T(8,128)S(1)} %get-tuple-element.53), channel_id=1, source_target_pairs={{0,1},{1,0},{2,3},{3,2},{4,5},{5,4},{6,7},{7,6},{8,9},{9,8},{10,11... | collective-permute-start | bytes 786440 | tf_op jit(solution)/shard_map/ppermute | solution.py:45
  17.1 15.2 %collective-permute-start.2 = (f32[2,280,128]{2,1,0:T(8,128)S(1)}, f32[2,280,128]{2,1,0:T(8,128)S(1)}, u32[]{:S(2)}, u32[]{:S(2)}) collective-permute-start(f32[2,280,128]{2,1,0:T(8,128)S(1)} %get-tuple-element.48), channel_id=1, source_target_pairs={{0,8},{8,0},{16,24},{24,16},{1,9},{9,1},{17,25},{25,17},{2,10},{10... | collective-permute-start | bytes 860168 | tf_op jit(solution)/shard_map/ppermute | solution.py:45
  24.0 11.2 %collective-permute-start.3 = (f32[2,280,128]{2,1,0:T(8,128)S(1)}, f32[2,280,128]{2,1,0:T(8,128)S(1)}, u32[]{:S(2)}, u32[]{:S(2)}) collective-permute-start(f32[2,280,128]{2,1,0:T(8,128)S(1)} %get-tuple-element.49), channel_id=1, source_target_pairs={{8,16},{16,8},{9,17},{17,9},{10,18},{18,10},{11,19},{19,11},{12,20... | collective-permute-start | bytes 860168 | tf_op jit(solution)/shard_map/ppermute | solution.py:45
  27.8 7.5 %collective-permute-start.10 = (f32[2,128,256]{2,1,0:T(8,128)S(1)}, f32[2,128,256]{2,1,0:T(8,128)S(1)}, u32[]{:S(2)}, u32[]{:S(2)}) collective-permute-start(f32[2,128,256]{2,1,0:T(8,128)S(1)} %get-tuple-element.68), channel_id=1, source_target_pairs={{1,2},{2,1},{3,4},{4,3},{5,6},{6,5},{9,10},{10,9},{11,12},{12,11},... | collective-permute-start | bytes 786440 | tf_op jit(solution)/shard_map/ppermute | solution.py:45
  28.5 6.8 %collective-permute-start.11 = (f32[2,128,256]{2,1,0:T(8,128)S(1)}, f32[2,128,256]{2,1,0:T(8,128)S(1)}, u32[]{:S(2)}, u32[]{:S(2)}) collective-permute-start(f32[2,128,256]{2,1,0:T(8,128)S(1)} %get-tuple-element.69), channel_id=1, source_target_pairs={{0,1},{1,0},{2,3},{3,2},{4,5},{5,4},{6,7},{7,6},{8,9},{9,8},{10,11... | collective-permute-start | bytes 786440 | tf_op jit(solution)/shard_map/ppermute | solution.py:45
  31.5 17.8 %collective-permute-start.8 = (f32[4,128,256]{2,1,0:T(8,128)S(1)}, f32[4,128,256]{2,1,0:T(8,128)S(1)}, u32[]{:S(2)}, u32[]{:S(2)}) collective-permute-start(f32[4,128,256]{2,1,0:T(8,128)S(1)} %get-tuple-element.65), channel_id=1, source_target_pairs={{1,2},{2,1},{3,4},{4,3},{5,6},{6,5},{9,10},{10,9},{11,12},{12,11},... | collective-permute-start | bytes 1572872 | tf_op jit(solution)/shard_map/ppermute | solution.py:45
  32.2 17.1 %collective-permute-start.9 = (f32[4,128,256]{2,1,0:T(8,128)S(1)}, f32[4,128,256]{2,1,0:T(8,128)S(1)}, u32[]{:S(2)}, u32[]{:S(2)}) collective-permute-start(f32[4,128,256]{2,1,0:T(8,128)S(1)} %get-tuple-element.66), channel_id=1, source_target_pairs={{0,1},{1,0},{2,3},{3,2},{4,5},{5,4},{6,7},{7,6},{8,9},{9,8},{10,11... | collective-permute-start | bytes 1572872 | tf_op jit(solution)/shard_map/ppermute | solution.py:45
  35.4 8.1 %collective-permute-start.14 = (f32[1,256,128]{2,1,0:T(8,128)S(1)}, f32[1,256,128]{2,1,0:T(8,128)S(1)}, u32[]{:S(2)}, u32[]{:S(2)}) collective-permute-start(f32[1,256,128]{2,1,0:T(8,128)S(1)} %get-tuple-element.72), channel_id=1, source_target_pairs={{8,24},{16,0},{9,25},{17,1},{10,26},{18,2},{11,27},{19,3},{12,28},... | collective-permute-start | bytes 393224 | tf_op jit(solution)/shard_map/ppermute | solution.py:56
  36.7 13.6 %collective-permute-start.12 = (f32[2,256,128]{2,1,0:T(8,128)S(1)}, f32[2,256,128]{2,1,0:T(8,128)S(1)}, u32[]{:S(2)}, u32[]{:S(2)}) collective-permute-start(f32[2,256,128]{2,1,0:T(8,128)S(1)} %get-tuple-element.70), channel_id=1, source_target_pairs={{0,8},{8,0},{16,24},{24,16},{1,9},{9,1},{17,25},{25,17},{2,10},{10... | collective-permute-start | bytes 786440 | tf_op jit(solution)/shard_map/ppermute | solution.py:45
  39.2 11.1 %collective-permute-start.13 = (f32[1,256,128]{2,1,0:T(8,128)S(1)}, f32[1,256,128]{2,1,0:T(8,128)S(1)}, u32[]{:S(2)}, u32[]{:S(2)}) collective-permute-start(f32[1,256,128]{2,1,0:T(8,128)S(1)} %get-tuple-element.71), channel_id=1, source_target_pairs={{8,16},{16,8},{9,17},{17,9},{10,18},{18,10},{11,19},{19,11},{12,20... | collective-permute-start | bytes 393224 | tf_op jit(solution)/shard_map/ppermute | solution.py:45
  43.5 6.8 %collective-permute-start.15 = (f32[1,256,128]{2,1,0:T(8,128)S(1)}, f32[1,256,128]{2,1,0:T(8,128)S(1)}, u32[]{:S(2)}, u32[]{:S(2)}) collective-permute-start(f32[1,256,128]{2,1,0:T(8,128)S(1)} %collective-permute-done.14), channel_id=1, source_target_pairs={{24,16},{0,8},{25,17},{1,9},{26,18},{2,10},{27,19},{3,11},{28,20},... | collective-permute-start | bytes 393224 | tf_op jit(solution)/shard_map/ppermute | solution.py:56

commit v7 on v6

--- a/solution.py
+++ b/solution.py
@@ -370,16 +370,21 @@
         start = index * CHUNK
         row = lax.broadcasted_iota(jnp.int32, (CHUNK, window), 0) + start
         col = lax.broadcasted_iota(jnp.int32, (CHUNK, window), 1)
-        total = jnp.zeros((CHUNK, window), F32)
+        here = pl.ds(pl.multiple_of(start, CHUNK), CHUNK)
+        scale[here, :] = jnp.zeros((CHUNK, window), F32)
         for top, left, r, c in shifts:
-            turn = lax.rem(2 * window - half - r, window)
-            rest = lax.rem(turn, 8)
-            value = twice[pl.ds(pl.multiple_of(turn - rest + start, 8), CHUNK + 8), :]
-            value = pltpu.roll(value, lax.rem(CHUNK + 8 - rest, CHUNK + 8), 0)[:CHUNK]
-            value = pltpu.roll(value, lax.rem(c + half, window), 1)
-            inside = (row >= top) & (row < top + window) & (col >= left) & (col < left + window)
-            total += jnp.where(inside, value, 0.0)
-        scale[pl.ds(pl.multiple_of(start, CHUNK), CHUNK), :] = 1.0 / (total + ridge)
+
+            @pl.when((top < start + CHUNK) & (top + window > start) & (left < window) & (left + window > 0))
+            def _():
+                turn = lax.rem(2 * window - half - r, window)
+                rest = lax.rem(turn, 8)
+                value = twice[pl.ds(pl.multiple_of(turn - rest + start, 8), CHUNK + 8), :]
+                value = pltpu.roll(value, lax.rem(CHUNK + 8 - rest, CHUNK + 8), 0)[:CHUNK]
+                value = pltpu.roll(value, lax.rem(c + half, window), 1)
+                inside = (row >= top) & (row < top + window) & (col >= left) & (col < left + window)
+                scale[here, :] += jnp.where(inside, value, 0.0)
+
+        scale[here, :] = 1.0 / (scale[here, :] + ridge)
         return carry
 
     lax.fori_loop(0, half // CHUNK, functools.partial(rows_at, shifts=upper), 0)

time: 51.6 us -> 52.3 us (1.014)
  Pallas kernels: 13.5 us -> 14.2 us
    pallas_call x12, Pallas kernels: 13.5 us -> 14.2 us  [call(): pl.pallas_call(body, out_shape=[x if hasattr(x, 'dtype') else jax.ShapeDt...]
  transfers between devices with their start and end apart: 16 -> 16, of which waited for: 1 -> 1; matrix products, arithmetic and copies ran while one was open for 0% -> 0% of each run, Pallas kernels for 25% -> 26%
where the time goes in v7:
time: 52.3 us; the launch traced here: 51.9 us
  starting transfers between devices  32.5 us (62%)
  Pallas kernels  14.2 us (27%)
  waiting for transfers between devices  3.69 us (7%)
  local copies, waits for them, and re-layouts  1.25 us (2%)
    ppermute x14, starting transfers between devices, swapped(): return lax.ppermute(value, axis, swap_pairs(lax.axis_size(axis), first))  29.2 us
    pallas_call x12, Pallas kernels, call(): pl.pallas_call(body, out_shape=[x if hasattr(x, 'dtype') else jax.ShapeDt...  14.2 us
    ppermute x2, waiting for transfers between devices, around(): return lax.ppermute(lax.ppermute(value, axis, out), axis, back)  3.66 us
    ppermute x2, starting transfers between devices, around(): return lax.ppermute(lax.ppermute(value, axis, out), axis, back)  3.27 us
    unnamed x14, local copies, waits for them, and re-layouts  1.25 us
  transfers between devices with their start and end apart: 16, of which 1 were waited for; matrix products, arithmetic and copies ran while one was open for 0% of the time, Pallas kernels for 26%

profile of v7, /device:TPU:0, one launch (start us, length us, event | category | flops | bytes accessed | tf_op | source)
XLA Modules:
  0.0 51.9 jit_solution(3400330316989842527)
XLA Ops:
  0.0 0.0 copy-start
  0.0 1.2 %copy-done = f32[2,2,256,256]{3,2,1,0:T(8,128)S(1)} copy-done((f32[2,2,256,256]{3,2,1,0:T(8,128)S(1)}, f32[2,2,256,256]{3,2,1,0:T(8,128)}, u32[]{:S(2)}) %copy-start) | copy-done | bytes 1048600
  1.2 0.0 copy-start.1
  1.2 0.0 copy-start.2
  1.2 0.0 copy-start.5
  1.2 0.0 copy-start.6
  1.2 0.1 edges.1
  1.3 0.0 copy-start.4
  1.3 3.0 %collective-permute-start.4 = (f32[2,256,128]{2,1,0:T(8,128)S(1)}, f32[2,256,128]{2,1,0:T(8,128)S(1)}, u32[]{:S(2)}, u32[]{:S(2)}) collective-permute-start(f32[2,256,128]{2,1,0:T(8,128)S(1)} %get-tuple-element.50), channel_id=1, source_target_pairs={{0,8},{8,0},{16,24},{24,16},{1,9},{9,1},{17,25},{25,17},{2,10},{10... | collective-permute-start | bytes 786440 | tf_op jit(solution)/shard_map/ppermute | solution.py:45
  4.3 0.7 %collective-permute-start.5 = (f32[2,256,128]{2,1,0:T(8,128)S(1)}, f32[2,256,128]{2,1,0:T(8,128)S(1)}, u32[]{:S(2)}, u32[]{:S(2)}) collective-permute-start(f32[2,256,128]{2,1,0:T(8,128)S(1)} %get-tuple-element.51), channel_id=1, source_target_pairs={{8,16},{16,8},{9,17},{17,9},{10,18},{18,10},{11,19},{19,11},{12,20... | collective-permute-start | bytes 786440 | tf_op jit(solution)/shard_map/ppermute | solution.py:45
  5.0 0.0 copy-done.1
  5.0 0.0 copy-done.2
  5.0 0.0 copy-done.5
  5.0 0.0 copy-done.6
  5.0 0.0 copy-done.4
  5.0 3.2 %detect.1 = (f32[2,2,256,256]{3,2,1,0:T(8,128)S(1)}, f32[4,136,256]{2,1,0:T(8,128)S(1)}, f32[4,136,256]{2,1,0:T(8,128)S(1)}, f32[2,128,256]{2,1,0:T(8,128)S(1)},...) custom-call(s32[2,1,2]{2,1,0:T(1,128)S(1)} %copy-done.4, ...), custom_call_target="tpu_custom_call" | custom-call | flops 12000000000 | bytes 1 | tf_op jit(solution)/shard_map/detect/pallas_call | solution.py:483
  8.2 0.7 %collective-permute-start = (f32[4,136,256]{2,1,0:T(8,128)S(1)}, f32[4,136,256]{2,1,0:T(8,128)S(1)}, u32[]{:S(2)}, u32[]{:S(2)}) collective-permute-start(f32[4,136,256]{2,1,0:T(8,128)S(1)} %get-tuple-element.39), channel_id=1, source_target_pairs={{1,2},{2,1},{3,4},{4,3},{5,6},{6,5},{9,10},{10,9},{11,12},{12,11},... | collective-permute-start | bytes 1671176 | tf_op jit(solution)/shard_map/ppermute | solution.py:45
  8.9 0.0 copy-start.3
  9.0 3.0 %collective-permute-start.1 = (f32[4,136,256]{2,1,0:T(8,128)S(1)}, f32[4,136,256]{2,1,0:T(8,128)S(1)}, u32[]{:S(2)}, u32[]{:S(2)}) collective-permute-start(f32[4,136,256]{2,1,0:T(8,128)S(1)} %get-tuple-element.40), channel_id=1, source_target_pairs={{0,1},{1,0},{2,3},{3,2},{4,5},{5,4},{6,7},{7,6},{8,9},{9,8},{10,11... | collective-permute-start | bytes 1671176 | tf_op jit(solution)/shard_map/ppermute | solution.py:45
  11.9 0.0 collective-permute-done.4.from_first.halo_first
  11.9 0.0 collective-permute-done.5.from_second.halo_second
  12.0 0.7 %collective-permute-start.6 = (f32[2,128,256]{2,1,0:T(8,128)S(1)}, f32[2,128,256]{2,1,0:T(8,128)S(1)}, u32[]{:S(2)}, u32[]{:S(2)}) collective-permute-start(f32[2,128,256]{2,1,0:T(8,128)S(1)} %get-tuple-element.52), channel_id=1, source_target_pairs={{1,2},{2,1},{3,4},{4,3},{5,6},{6,5},{9,10},{10,9},{11,12},{12,11},... | collective-permute-start | bytes 786440 | tf_op jit(solution)/shard_map/ppermute | solution.py:45
  12.7 3.1 %collective-permute-start.7 = (f32[2,128,256]{2,1,0:T(8,128)S(1)}, f32[2,128,256]{2,1,0:T(8,128)S(1)}, u32[]{:S(2)}, u32[]{:S(2)}) collective-permute-start(f32[2,128,256]{2,1,0:T(8,128)S(1)} %get-tuple-element.53), channel_id=1, source_target_pairs={{0,1},{1,0},{2,3},{3,2},{4,5},{5,4},{6,7},{7,6},{8,9},{9,8},{10,11... | collective-permute-start | bytes 786440 | tf_op jit(solution)/shard_map/ppermute | solution.py:45
  15.7 0.0 copy-done.3
  15.7 1.2 %roll.1 = (f32[2,2,256,256]{3,2,1,0:T(8,128)S(1)}, f32[2,2,256,256]{3,2,1,0:T(8,128)S(1)}) custom-call(s32[2,1,2]{2,1,0:T(1,128)S(1)} %copy-done.4, f32[2,2,256,256]{3,2,1,0:T(8,128)S(1)} %get-tuple-element.41.field, f32[2,256,256]{2,1,0:T(8,128)S(1)} %copy-done.3), custom_call_target="tpu_custom_call" | custom-call | flops 100000000 | bytes 1 | tf_op jit(solution)/shard_map/roll/pallas_call | solution.py:483
  17.0 0.0 collective-permute-done.from_second.down.own_second
  17.0 0.0 collective-permute-done.1.from_first.up.own_first
  17.0 0.1 narrow2.1
  17.1 7.0 %collective-permute-start.2 = (f32[2,280,128]{2,1,0:T(8,128)S(1)}, f32[2,280,128]{2,1,0:T(8,128)S(1)}, u32[]{:S(2)}, u32[]{:S(2)}) collective-permute-start(f32[2,280,128]{2,1,0:T(8,128)S(1)} %get-tuple-element.48), channel_id=1, source_target_pairs={{0,8},{8,0},{16,24},{24,16},{1,9},{9,1},{17,25},{25,17},{2,10},{10... | collective-permute-start | bytes 860168 | tf_op jit(solution)/shard_map/ppermute | solution.py:45
  24.0 0.7 %collective-permute-start.3 = (f32[2,280,128]{2,1,0:T(8,128)S(1)}, f32[2,280,128]{2,1,0:T(8,128)S(1)}, u32[]{:S(2)}, u32[]{:S(2)}) collective-permute-start(f32[2,280,128]{2,1,0:T(8,128)S(1)} %get-tuple-element.49), channel_id=1, source_target_pairs={{8,16},{16,8},{9,17},{17,9},{10,18},{18,10},{11,19},{19,11},{12,20... | collective-permute-start | bytes 860168 | tf_op jit(solution)/shard_map/ppermute | solution.py:45
  24.7 0.0 collective-permute-done.6.corner_second
  24.7 0.0 collective-permute-done.7.corner_first
  24.7 3.1 %propagate.1 = (f32[2,128,256]{2,1,0:T(8,128)S(1)}, f32[2,128,256]{2,1,0:T(8,128)S(1)}, f32[4,128,256]{2,1,0:T(8,128)S(1)}, f32[4,128,256]{2,1,0:T(8,128)S(1)}, f32[2,256,512]{2,1,0:T(8,128)S(1)}) custom-call(s32[4,8,256]{2,1,0:T(8,128)S(1)} %get-tuple-element.55.marks, f32[2,2,256,256]{3,2,1,0:T(8,128)S(1)} %get-tuple-element.56.field, ...), custom_call_target="tpu_custom_call" | custom-call | flops 100000000 | bytes 1 | tf_op jit(solution)/shard_map/propagate/pallas_call | solution.py:483
  27.8 0.7 %collective-permute-start.10 = (f32[2,128,256]{2,1,0:T(8,128)S(1)}, f32[2,128,256]{2,1,0:T(8,128)S(1)}, u32[]{:S(2)}, u32[]{:S(2)}) collective-permute-start(f32[2,128,256]{2,1,0:T(8,128)S(1)} %get-tuple-element.68), channel_id=1, source_target_pairs={{1,2},{2,1},{3,4},{4,3},{5,6},{6,5},{9,10},{10,9},{11,12},{12,11},... | collective-permute-start | bytes 786440 | tf_op jit(solution)/shard_map/ppermute | solution.py:45
  28.5 3.0 %collective-permute-start.11 = (f32[2,128,256]{2,1,0:T(8,128)S(1)}, f32[2,128,256]{2,1,0:T(8,128)S(1)}, u32[]{:S(2)}, u32[]{:S(2)}) collective-permute-start(f32[2,128,256]{2,1,0:T(8,128)S(1)} %get-tuple-element.69), channel_id=1, source_target_pairs={{0,1},{1,0},{2,3},{3,2},{4,5},{5,4},{6,7},{7,6},{8,9},{9,8},{10,11... | collective-permute-start | bytes 786440 | tf_op jit(solution)/shard_map/ppermute | solution.py:45
  31.5 0.7 %collective-permute-start.8 = (f32[4,128,256]{2,1,0:T(8,128)S(1)}, f32[4,128,256]{2,1,0:T(8,128)S(1)}, u32[]{:S(2)}, u32[]{:S(2)}) collective-permute-start(f32[4,128,256]{2,1,0:T(8,128)S(1)} %get-tuple-element.65), channel_id=1, source_target_pairs={{1,2},{2,1},{3,4},{4,3},{5,6},{6,5},{9,10},{10,9},{11,12},{12,11},... | collective-permute-start | bytes 1572872 | tf_op jit(solution)/shard_map/ppermute | solution.py:45
  32.2 0.0 collective-permute-done.2.first.received
  32.2 3.0 %collective-permute-start.9 = (f32[4,128,256]{2,1,0:T(8,128)S(1)}, f32[4,128,256]{2,1,0:T(8,128)S(1)}, u32[]{:S(2)}, u32[]{:S(2)}) collective-permute-start(f32[4,128,256]{2,1,0:T(8,128)S(1)} %get-tuple-element.66), channel_id=1, source_target_pairs={{0,1},{1,0},{2,3},{3,2},{4,5},{5,4},{6,7},{7,6},{8,9},{9,8},{10,11... | collective-permute-start | bytes 1572872 | tf_op jit(solution)/shard_map/ppermute | solution.py:45
  35.3 0.0 collective-permute-done.3.second.received
  35.3 0.1 join3.1.total2_second
  35.3 0.0 collective-permute-done.10.from_second
  35.3 0.0 collective-permute-done.11.from_first
  35.3 0.1 narrow1.1
  35.4 1.3 %collective-permute-start.14 = (f32[1,256,128]{2,1,0:T(8,128)S(1)}, f32[1,256,128]{2,1,0:T(8,128)S(1)}, u32[]{:S(2)}, u32[]{:S(2)}) collective-permute-start(f32[1,256,128]{2,1,0:T(8,128)S(1)} %get-tuple-element.72), channel_id=1, source_target_pairs={{8,24},{16,0},{9,25},{17,1},{10,26},{18,2},{11,27},{19,3},{12,28},... | collective-permute-start | bytes 393224 | tf_op jit(solution)/shard_map/ppermute | solution.py:56
  36.7 2.5 %collective-permute-start.12 = (f32[2,256,128]{2,1,0:T(8,128)S(1)}, f32[2,256,128]{2,1,0:T(8,128)S(1)}, u32[]{:S(2)}, u32[]{:S(2)}) collective-permute-start(f32[2,256,128]{2,1,0:T(8,128)S(1)} %get-tuple-element.70), channel_id=1, source_target_pairs={{0,8},{8,0},{16,24},{24,16},{1,9},{9,1},{17,25},{25,17},{2,10},{10... | collective-permute-start | bytes 786440 | tf_op jit(solution)/shard_map/ppermute | solution.py:45
  39.2 0.7 %collective-permute-start.13 = (f32[1,256,128]{2,1,0:T(8,128)S(1)}, f32[1,256,128]{2,1,0:T(8,128)S(1)}, u32[]{:S(2)}, u32[]{:S(2)}) collective-permute-start(f32[1,256,128]{2,1,0:T(8,128)S(1)} %get-tuple-element.71), channel_id=1, source_target_pairs={{8,16},{16,8},{9,17},{17,9},{10,18},{18,10},{11,19},{19,11},{12,20... | collective-permute-start | bytes 393224 | tf_op jit(solution)/shard_map/ppermute | solution.py:45
  39.9 3.7 %collective-permute-done.14 = f32[1,256,128]{2,1,0:T(8,128)S(1)} collective-permute-done((f32[1,256,128]{2,1,0:T(8,128)S(1)}, f32[1,256,128]{2,1,0:T(8,128)S(1)}, u32[]{:S(2)}, u32[]{:S(2)}) %collective-permute-start.14) | collective-permute-done | bytes 131104 | tf_op jit(solution)/shard_map/ppermute | solution.py:56
  43.5 2.0 %collective-permute-start.15 = (f32[1,256,128]{2,1,0:T(8,128)S(1)}, f32[1,256,128]{2,1,0:T(8,128)S(1)}, u32[]{:S(2)}, u32[]{:S(2)}) collective-permute-start(f32[1,256,128]{2,1,0:T(8,128)S(1)} %collective-permute-done.14), channel_id=1, source_target_pairs={{24,16},{0,8},{25,17},{1,9},{26,18},{2,10},{27,19},{3,11},{28,20},... | collective-permute-start | bytes 393224 | tf_op jit(solution)/shard_map/ppermute | solution.py:56
  45.5 4.5 %illuminate.1.scale = f32[256,256]{1,0:T(8,128)S(1)} custom-call(s32[2,1,2]{2,1,0:T(1,128)S(1)} %copy-done.4, f32[2,256,256]{2,1,0:T(8,128)S(1)} %copy-done.3, f32[4,136,256]{2,1,0:T(8,128)S(1)} %collective-permute-done.1.from_first.up.own_first, f32[4,136,256]{2,1,0:T(8,128)S(1)} %collective-permute-done.from_second.down.own_second, ...), custom_call_target="tpu_custom_call" | custom-call | flops 2500000000 | bytes 1 | tf_op jit(solution)/shard_map/illuminate/pallas_call | solution.py:483
  50.0 0.0 collective-permute-done.8.inner_second
  50.0 0.0 collective-permute-done.9.inner_first
  50.0 1.0 %update2.1.begun = f32[2,2,256,256]{3,2,1,0:T(8,128)} custom-call(f32[2,2,256,256]{3,2,1,0:T(8,128)S(1)} %copy-done.1, f32[256,256]{1,0:T(8,128)S(1)} %illuminate.1.scale, f32[2,256,128]{2,1,0:T(8,128)S(1)} %join2.1.total2_first, f32[2,256,128]{2,1,0:T(8,128)S(1)} %join3.1.total2_second, f32[4,128,256]{2,1,0:T(8,128)S(1)} %collective-permute-done.8.inner_second, ...), custom_call_target="tpu_custom_call" | custom-call | flops 100000000 | bytes 1 | tf_op jit(solution)/shard_map/update2/pallas_call | solution.py:483
  51.0 0.0 collective-permute-done.13.second1_re
  51.0 0.0 collective-permute-done.15.second1_im
  51.0 0.0 collective-permute-done.12.first1
  51.0 0.9 %update.1 = f32[2,2,256,256]{3,2,1,0:T(8,128)} custom-call(f32[2,2,256,256]{3,2,1,0:T(8,128)} %update2.1.begun, f32[2,256,128]{2,1,0:T(8,128)S(1)} %collective-permute-done.12.first1, f32[1,256,128]{2,1,0:T(8,128)S(1)} %collective-permute-done.13.second1_re, f32[1,256,128]{2,1,0:T(8,128)S(1)} %collective-permute-done.15.second1_im, ...), custom_call_target="tpu_custom_call", output_to_operand_aliasing={{}: (0, {})} | custom-call | flops 1000000000 | bytes 1 | tf_op jit(solution)/shard_map/update/pallas_call | solution.py:483
  (2 shorter events, 0.1 us)
Async XLA Ops:
  0.0 1.2 %copy-start = (f32[2,2,256,256]{3,2,1,0:T(8,128)S(1)}, f32[2,2,256,256]{3,2,1,0:T(8,128)}, u32[]{:S(2)}) copy-start(f32[2,2,256,256]{3,2,1,0:T(8,128)} %object_field.9) | copy-start | bytes 3145732
  1.2 3.8 %copy-start.1 = (f32[2,2,256,256]{3,2,1,0:T(8,128)S(1)}, f32[2,2,256,256]{3,2,1,0:T(8,128)}, u32[]{:S(2)}) copy-start(f32[2,2,256,256]{3,2,1,0:T(8,128)} %object_field.9) | copy-start | bytes 3145732
  1.2 3.8 %copy-start.2 = (bf16[4,256,512]{2,1,0:T(8,128)(2,1)S(1)}, bf16[4,256,512]{2,1,0:T(8,128)(2,1)}, u32[]{:S(2)}) copy-start(bf16[4,256,512]{2,1,0:T(8,128)(2,1)} %constant.2.clone.table) | copy-start | bytes 3145732
  1.2 3.8 %copy-start.5 = (bf16[2,1,2,256,256]{4,3,2,1,0:T(8,128)(2,1)S(1)}, bf16[2,1,2,256,256]{4,3,2,1,0:T(8,128)(2,1)}, u32[]{:S(2)}) copy-start(bf16[2,1,2,256,256]{4,3,2,1,0:T(8,128)(2,1)} %residual.1) | copy-start | bytes 1572868
  1.2 3.8 %copy-start.6 = (bf16[2,1,2,256,256]{4,3,2,1,0:T(8,128)(2,1)S(1)}, bf16[2,1,2,256,256]{4,3,2,1,0:T(8,128)(2,1)}, u32[]{:S(2)}) copy-start(bf16[2,1,2,256,256]{4,3,2,1,0:T(8,128)(2,1)} %wave.1) | copy-start | bytes 1572868
  1.3 3.7 %copy-start.4 = (s32[2,1,2]{2,1,0:T(1,128)S(1)}, s32[2,1,2]{2,1,0:T(1,128)}, u32[]{:S(2)}) copy-start(s32[2,1,2]{2,1,0:T(1,128)} %pos.1) | copy-start | bytes 52
  1.3 10.6 %collective-permute-start.4 = (f32[2,256,128]{2,1,0:T(8,128)S(1)}, f32[2,256,128]{2,1,0:T(8,128)S(1)}, u32[]{:S(2)}, u32[]{:S(2)}) collective-permute-start(f32[2,256,128]{2,1,0:T(8,128)S(1)} %get-tuple-element.50), channel_id=1, source_target_pairs={{0,8},{8,0},{16,24},{24,16},{1,9},{9,1},{17,25},{25,17},{2,10},{10... | collective-permute-start | bytes 786440 | tf_op jit(solution)/shard_map/ppermute | solution.py:45
  4.3 7.6 %collective-permute-start.5 = (f32[2,256,128]{2,1,0:T(8,128)S(1)}, f32[2,256,128]{2,1,0:T(8,128)S(1)}, u32[]{:S(2)}, u32[]{:S(2)}) collective-permute-start(f32[2,256,128]{2,1,0:T(8,128)S(1)} %get-tuple-element.51), channel_id=1, source_target_pairs={{8,16},{16,8},{9,17},{17,9},{10,18},{18,10},{11,19},{19,11},{12,20... | collective-permute-start | bytes 786440 | tf_op jit(solution)/shard_map/ppermute | solution.py:45
  8.2 8.7 %collective-permute-start = (f32[4,136,256]{2,1,0:T(8,128)S(1)}, f32[4,136,256]{2,1,0:T(8,128)S(1)}, u32[]{:S(2)}, u32[]{:S(2)}) collective-permute-start(f32[4,136,256]{2,1,0:T(8,128)S(1)} %get-tuple-element.39), channel_id=1, source_target_pairs={{1,2},{2,1},{3,4},{4,3},{5,6},{6,5},{9,10},{10,9},{11,12},{12,11},... | collective-permute-start | bytes 1671176 | tf_op jit(solution)/shard_map/ppermute | solution.py:45
  8.9 6.8 %copy-start.3 = (f32[2,256,256]{2,1,0:T(8,128)S(1)}, f32[2,256,256]{2,1,0:T(8,128)}, u32[]{:S(2)}) copy-start(f32[2,256,256]{2,1,0:T(8,128)} %probe.3) | copy-start | bytes 1572868
  9.0 8.0 %collective-permute-start.1 = (f32[4,136,256]{2,1,0:T(8,128)S(1)}, f32[4,136,256]{2,1,0:T(8,128)S(1)}, u32[]{:S(2)}, u32[]{:S(2)}) collective-permute-start(f32[4,136,256]{2,1,0:T(8,128)S(1)} %get-tuple-element.40), channel_id=1, source_target_pairs={{0,1},{1,0},{2,3},{3,2},{4,5},{5,4},{6,7},{7,6},{8,9},{9,8},{10,11... | collective-permute-start | bytes 1671176 | tf_op jit(solution)/shard_map/ppermute | solution.py:45
  12.0 12.7 %collective-permute-start.6 = (f32[2,128,256]{2,1,0:T(8,128)S(1)}, f32[2,128,256]{2,1,0:T(8,128)S(1)}, u32[]{:S(2)}, u32[]{:S(2)}) collective-permute-start(f32[2,128,256]{2,1,0:T(8,128)S(1)} %get-tuple-element.52), channel_id=1, source_target_pairs={{1,2},{2,1},{3,4},{4,3},{5,6},{6,5},{9,10},{10,9},{11,12},{12,11},... | collective-permute-start | bytes 786440 | tf_op jit(solution)/shard_map/ppermute | solution.py:45
  12.7 12.1 %collective-permute-start.7 = (f32[2,128,256]{2,1,0:T(8,128)S(1)}, f32[2,128,256]{2,1,0:T(8,128)S(1)}, u32[]{:S(2)}, u32[]{:S(2)}) collective-permute-start(f32[2,128,256]{2,1,0:T(8,128)S(1)} %get-tuple-element.53), channel_id=1, source_target_pairs={{0,1},{1,0},{2,3},{3,2},{4,5},{5,4},{6,7},{7,6},{8,9},{9,8},{10,11... | collective-permute-start | bytes 786440 | tf_op jit(solution)/shard_map/ppermute | solution.py:45
  17.1 15.2 %collective-permute-start.2 = (f32[2,280,128]{2,1,0:T(8,128)S(1)}, f32[2,280,128]{2,1,0:T(8,128)S(1)}, u32[]{:S(2)}, u32[]{:S(2)}) collective-permute-start(f32[2,280,128]{2,1,0:T(8,128)S(1)} %get-tuple-element.48), channel_id=1, source_target_pairs={{0,8},{8,0},{16,24},{24,16},{1,9},{9,1},{17,25},{25,17},{2,10},{10... | collective-permute-start | bytes 860168 | tf_op jit(solution)/shard_map/ppermute | solution.py:45
  24.0 11.2 %collective-permute-start.3 = (f32[2,280,128]{2,1,0:T(8,128)S(1)}, f32[2,280,128]{2,1,0:T(8,128)S(1)}, u32[]{:S(2)}, u32[]{:S(2)}) collective-permute-start(f32[2,280,128]{2,1,0:T(8,128)S(1)} %get-tuple-element.49), channel_id=1, source_target_pairs={{8,16},{16,8},{9,17},{17,9},{10,18},{18,10},{11,19},{19,11},{12,20... | collective-permute-start | bytes 860168 | tf_op jit(solution)/shard_map/ppermute | solution.py:45
  27.8 7.5 %collective-permute-start.10 = (f32[2,128,256]{2,1,0:T(8,128)S(1)}, f32[2,128,256]{2,1,0:T(8,128)S(1)}, u32[]{:S(2)}, u32[]{:S(2)}) collective-permute-start(f32[2,128,256]{2,1,0:T(8,128)S(1)} %get-tuple-element.68), channel_id=1, source_target_pairs={{1,2},{2,1},{3,4},{4,3},{5,6},{6,5},{9,10},{10,9},{11,12},{12,11},... | collective-permute-start | bytes 786440 | tf_op jit(solution)/shard_map/ppermute | solution.py:45
  28.5 6.8 %collective-permute-start.11 = (f32[2,128,256]{2,1,0:T(8,128)S(1)}, f32[2,128,256]{2,1,0:T(8,128)S(1)}, u32[]{:S(2)}, u32[]{:S(2)}) collective-permute-start(f32[2,128,256]{2,1,0:T(8,128)S(1)} %get-tuple-element.69), channel_id=1, source_target_pairs={{0,1},{1,0},{2,3},{3,2},{4,5},{5,4},{6,7},{7,6},{8,9},{9,8},{10,11... | collective-permute-start | bytes 786440 | tf_op jit(solution)/shard_map/ppermute | solution.py:45
  31.5 18.5 %collective-permute-start.8 = (f32[4,128,256]{2,1,0:T(8,128)S(1)}, f32[4,128,256]{2,1,0:T(8,128)S(1)}, u32[]{:S(2)}, u32[]{:S(2)}) collective-permute-start(f32[4,128,256]{2,1,0:T(8,128)S(1)} %get-tuple-element.65), channel_id=1, source_target_pairs={{1,2},{2,1},{3,4},{4,3},{5,6},{6,5},{9,10},{10,9},{11,12},{12,11},... | collective-permute-start | bytes 1572872 | tf_op jit(solution)/shard_map/ppermute | solution.py:45
  32.2 17.8 %collective-permute-start.9 = (f32[4,128,256]{2,1,0:T(8,128)S(1)}, f32[4,128,256]{2,1,0:T(8,128)S(1)}, u32[]{:S(2)}, u32[]{:S(2)}) collective-permute-start(f32[4,128,256]{2,1,0:T(8,128)S(1)} %get-tuple-element.66), channel_id=1, source_target_pairs={{0,1},{1,0},{2,3},{3,2},{4,5},{5,4},{6,7},{7,6},{8,9},{9,8},{10,11... | collective-permute-start | bytes 1572872 | tf_op jit(solution)/shard_map/ppermute | solution.py:45
  35.4 8.1 %collective-permute-start.14 = (f32[1,256,128]{2,1,0:T(8,128)S(1)}, f32[1,256,128]{2,1,0:T(8,128)S(1)}, u32[]{:S(2)}, u32[]{:S(2)}) collective-permute-start(f32[1,256,128]{2,1,0:T(8,128)S(1)} %get-tuple-element.72), channel_id=1, source_target_pairs={{8,24},{16,0},{9,25},{17,1},{10,26},{18,2},{11,27},{19,3},{12,28},... | collective-permute-start | bytes 393224 | tf_op jit(solution)/shard_map/ppermute | solution.py:56
  36.7 14.3 %collective-permute-start.12 = (f32[2,256,128]{2,1,0:T(8,128)S(1)}, f32[2,256,128]{2,1,0:T(8,128)S(1)}, u32[]{:S(2)}, u32[]{:S(2)}) collective-permute-start(f32[2,256,128]{2,1,0:T(8,128)S(1)} %get-tuple-element.70), channel_id=1, source_target_pairs={{0,8},{8,0},{16,24},{24,16},{1,9},{9,1},{17,25},{25,17},{2,10},{10... | collective-permute-start | bytes 786440 | tf_op jit(solution)/shard_map/ppermute | solution.py:45
  39.2 11.8 %collective-permute-start.13 = (f32[1,256,128]{2,1,0:T(8,128)S(1)}, f32[1,256,128]{2,1,0:T(8,128)S(1)}, u32[]{:S(2)}, u32[]{:S(2)}) collective-permute-start(f32[1,256,128]{2,1,0:T(8,128)S(1)} %get-tuple-element.71), channel_id=1, source_target_pairs={{8,16},{16,8},{9,17},{17,9},{10,18},{18,10},{11,19},{19,11},{12,20... | collective-permute-start | bytes 393224 | tf_op jit(solution)/shard_map/ppermute | solution.py:45
  43.5 7.4 %collective-permute-start.15 = (f32[1,256,128]{2,1,0:T(8,128)S(1)}, f32[1,256,128]{2,1,0:T(8,128)S(1)}, u32[]{:S(2)}, u32[]{:S(2)}) collective-permute-start(f32[1,256,128]{2,1,0:T(8,128)S(1)} %collective-permute-done.14), channel_id=1, source_target_pairs={{24,16},{0,8},{25,17},{1,9},{26,18},{2,10},{27,19},{3,11},{28,20},... | collective-permute-start | bytes 393224 | tf_op jit(solution)/shard_map/ppermute | solution.py:56

commit v8 on v6

--- a/solution.py
+++ b/solution.py
@@ -364,21 +364,27 @@
                 top = jnp.where(valid == 1, top, window)
                 for reached, half_at in ((upper, -1), (lower, 1)):
                     if down in (0, half_at):
-                        reached.append((top, left, r, c))
+                        reached.append((top, left, r, c, along))
 
     def rows_at(index, carry, shifts):
         start = index * CHUNK
         row = lax.broadcasted_iota(jnp.int32, (CHUNK, window), 0) + start
         col = lax.broadcasted_iota(jnp.int32, (CHUNK, window), 1)
-        total = jnp.zeros((CHUNK, window), F32)
-        for top, left, r, c in shifts:
+        totals = [jnp.zeros((CHUNK, half), F32)] * 2
+        for top, left, r, c, along in shifts:
             turn = lax.rem(2 * window - half - r, window)
             rest = lax.rem(turn, 8)
             value = twice[pl.ds(pl.multiple_of(turn - rest + start, 8), CHUNK + 8), :]
             value = pltpu.roll(value, lax.rem(CHUNK + 8 - rest, CHUNK + 8), 0)[:CHUNK]
             value = pltpu.roll(value, lax.rem(c + half, window), 1)
-            inside = (row >= top) & (row < top + window) & (col >= left) & (col < left + window)
-            total += jnp.where(inside, value, 0.0)
+            for side in range(2):
+                if along == (1, -1)[side]:
+                    continue
+                cols = slice(side * half, (side + 1) * half)
+                inside = (row[:, cols] >= top) & (row[:, cols] < top + window)
+                inside &= (col[:, cols] >= left) & (col[:, cols] < left + window)
+                totals[side] += jnp.where(inside, value[:, cols], 0.0)
+        total = jnp.concatenate(totals, axis=1)
         scale[pl.ds(pl.multiple_of(start, CHUNK), CHUNK), :] = 1.0 / (total + ridge)
         return carry
 

time: 51.6 us -> 51.5 us (level)
  transfers between devices with their start and end apart: 16 -> 16, of which waited for: 1 -> 1; matrix products, arithmetic and copies ran while one was open for 0% -> 0% of each run, Pallas kernels for 25% -> 24%
where the time goes in v8:
time: 51.5 us; the launch traced here: 51.1 us
  starting transfers between devices  32.5 us (63%)
  Pallas kernels  13.4 us (26%)
  waiting for transfers between devices  3.69 us (7%)
  local copies, waits for them, and re-layouts  1.25 us (2%)
    ppermute x14, starting transfers between devices, swapped(): return lax.ppermute(value, axis, swap_pairs(lax.axis_size(axis), first))  29.2 us
    pallas_call x12, Pallas kernels, call(): pl.pallas_call(body, out_shape=[x if hasattr(x, 'dtype') else jax.ShapeDt...  13.4 us
    ppermute x2, waiting for transfers between devices, around(): return lax.ppermute(lax.ppermute(value, axis, out), axis, back)  3.66 us
    ppermute x2, starting transfers between devices, around(): return lax.ppermute(lax.ppermute(value, axis, out), axis, back)  3.27 us
    unnamed x14, local copies, waits for them, and re-layouts  1.25 us
  transfers between devices with their start and end apart: 16, of which 1 were waited for; matrix products, arithmetic and copies ran while one was open for 0% of the time, Pallas kernels for 24%

profile of v8, /device:TPU:0, one launch (start us, length us, event | category | flops | bytes accessed | tf_op | source)
XLA Modules:
  0.0 51.1 jit_solution(1775594382493207587)
XLA Ops:
  0.0 0.0 copy-start
  0.0 1.2 %copy-done = f32[2,2,256,256]{3,2,1,0:T(8,128)S(1)} copy-done((f32[2,2,256,256]{3,2,1,0:T(8,128)S(1)}, f32[2,2,256,256]{3,2,1,0:T(8,128)}, u32[]{:S(2)}) %copy-start) | copy-done | bytes 1048600
  1.2 0.0 copy-start.1
  1.2 0.0 copy-start.2
  1.2 0.0 copy-start.5
  1.2 0.0 copy-start.6
  1.2 0.1 edges.1
  1.3 0.0 copy-start.4
  1.3 3.0 %collective-permute-start.4 = (f32[2,256,128]{2,1,0:T(8,128)S(1)}, f32[2,256,128]{2,1,0:T(8,128)S(1)}, u32[]{:S(2)}, u32[]{:S(2)}) collective-permute-start(f32[2,256,128]{2,1,0:T(8,128)S(1)} %get-tuple-element.50), channel_id=1, source_target_pairs={{0,8},{8,0},{16,24},{24,16},{1,9},{9,1},{17,25},{25,17},{2,10},{10... | collective-permute-start | bytes 786440 | tf_op jit(solution)/shard_map/ppermute | solution.py:45
  4.3 0.7 %collective-permute-start.5 = (f32[2,256,128]{2,1,0:T(8,128)S(1)}, f32[2,256,128]{2,1,0:T(8,128)S(1)}, u32[]{:S(2)}, u32[]{:S(2)}) collective-permute-start(f32[2,256,128]{2,1,0:T(8,128)S(1)} %get-tuple-element.51), channel_id=1, source_target_pairs={{8,16},{16,8},{9,17},{17,9},{10,18},{18,10},{11,19},{19,11},{12,20... | collective-permute-start | bytes 786440 | tf_op jit(solution)/shard_map/ppermute | solution.py:45
  5.0 0.0 copy-done.1
  5.0 0.0 copy-done.2
  5.0 0.0 copy-done.5
  5.0 0.0 copy-done.6
  5.0 0.0 copy-done.4
  5.0 3.2 %detect.1 = (f32[2,2,256,256]{3,2,1,0:T(8,128)S(1)}, f32[4,136,256]{2,1,0:T(8,128)S(1)}, f32[4,136,256]{2,1,0:T(8,128)S(1)}, f32[2,128,256]{2,1,0:T(8,128)S(1)},...) custom-call(s32[2,1,2]{2,1,0:T(1,128)S(1)} %copy-done.4, ...), custom_call_target="tpu_custom_call" | custom-call | flops 12000000000 | bytes 1 | tf_op jit(solution)/shard_map/detect/pallas_call | solution.py:484
  8.2 0.7 %collective-permute-start = (f32[4,136,256]{2,1,0:T(8,128)S(1)}, f32[4,136,256]{2,1,0:T(8,128)S(1)}, u32[]{:S(2)}, u32[]{:S(2)}) collective-permute-start(f32[4,136,256]{2,1,0:T(8,128)S(1)} %get-tuple-element.39), channel_id=1, source_target_pairs={{1,2},{2,1},{3,4},{4,3},{5,6},{6,5},{9,10},{10,9},{11,12},{12,11},... | collective-permute-start | bytes 1671176 | tf_op jit(solution)/shard_map/ppermute | solution.py:45
  8.9 0.0 copy-start.3
  9.0 3.0 %collective-permute-start.1 = (f32[4,136,256]{2,1,0:T(8,128)S(1)}, f32[4,136,256]{2,1,0:T(8,128)S(1)}, u32[]{:S(2)}, u32[]{:S(2)}) collective-permute-start(f32[4,136,256]{2,1,0:T(8,128)S(1)} %get-tuple-element.40), channel_id=1, source_target_pairs={{0,1},{1,0},{2,3},{3,2},{4,5},{5,4},{6,7},{7,6},{8,9},{9,8},{10,11... | collective-permute-start | bytes 1671176 | tf_op jit(solution)/shard_map/ppermute | solution.py:45
  11.9 0.0 collective-permute-done.4.from_first.halo_first
  11.9 0.0 collective-permute-done.5.from_second.halo_second
  12.0 0.7 %collective-permute-start.6 = (f32[2,128,256]{2,1,0:T(8,128)S(1)}, f32[2,128,256]{2,1,0:T(8,128)S(1)}, u32[]{:S(2)}, u32[]{:S(2)}) collective-permute-start(f32[2,128,256]{2,1,0:T(8,128)S(1)} %get-tuple-element.52), channel_id=1, source_target_pairs={{1,2},{2,1},{3,4},{4,3},{5,6},{6,5},{9,10},{10,9},{11,12},{12,11},... | collective-permute-start | bytes 786440 | tf_op jit(solution)/shard_map/ppermute | solution.py:45
  12.7 3.1 %collective-permute-start.7 = (f32[2,128,256]{2,1,0:T(8,128)S(1)}, f32[2,128,256]{2,1,0:T(8,128)S(1)}, u32[]{:S(2)}, u32[]{:S(2)}) collective-permute-start(f32[2,128,256]{2,1,0:T(8,128)S(1)} %get-tuple-element.53), channel_id=1, source_target_pairs={{0,1},{1,0},{2,3},{3,2},{4,5},{5,4},{6,7},{7,6},{8,9},{9,8},{10,11... | collective-permute-start | bytes 786440 | tf_op jit(solution)/shard_map/ppermute | solution.py:45
  15.7 0.0 copy-done.3
  15.7 1.2 %roll.1 = (f32[2,2,256,256]{3,2,1,0:T(8,128)S(1)}, f32[2,2,256,256]{3,2,1,0:T(8,128)S(1)}) custom-call(s32[2,1,2]{2,1,0:T(1,128)S(1)} %copy-done.4, f32[2,2,256,256]{3,2,1,0:T(8,128)S(1)} %get-tuple-element.41.field, f32[2,256,256]{2,1,0:T(8,128)S(1)} %copy-done.3), custom_call_target="tpu_custom_call" | custom-call | flops 100000000 | bytes 1 | tf_op jit(solution)/shard_map/roll/pallas_call | solution.py:484
  17.0 0.0 collective-permute-done.from_second.down.own_second
  17.0 0.0 collective-permute-done.1.from_first.up.own_first
  17.0 0.1 narrow2.1
  17.1 7.0 %collective-permute-start.2 = (f32[2,280,128]{2,1,0:T(8,128)S(1)}, f32[2,280,128]{2,1,0:T(8,128)S(1)}, u32[]{:S(2)}, u32[]{:S(2)}) collective-permute-start(f32[2,280,128]{2,1,0:T(8,128)S(1)} %get-tuple-element.48), channel_id=1, source_target_pairs={{0,8},{8,0},{16,24},{24,16},{1,9},{9,1},{17,25},{25,17},{2,10},{10... | collective-permute-start | bytes 860168 | tf_op jit(solution)/shard_map/ppermute | solution.py:45
  24.0 0.7 %collective-permute-start.3 = (f32[2,280,128]{2,1,0:T(8,128)S(1)}, f32[2,280,128]{2,1,0:T(8,128)S(1)}, u32[]{:S(2)}, u32[]{:S(2)}) collective-permute-start(f32[2,280,128]{2,1,0:T(8,128)S(1)} %get-tuple-element.49), channel_id=1, source_target_pairs={{8,16},{16,8},{9,17},{17,9},{10,18},{18,10},{11,19},{19,11},{12,20... | collective-permute-start | bytes 860168 | tf_op jit(solution)/shard_map/ppermute | solution.py:45
  24.7 0.0 collective-permute-done.6.corner_second
  24.7 0.0 collective-permute-done.7.corner_first
  24.7 3.1 %propagate.1 = (f32[2,128,256]{2,1,0:T(8,128)S(1)}, f32[2,128,256]{2,1,0:T(8,128)S(1)}, f32[4,128,256]{2,1,0:T(8,128)S(1)}, f32[4,128,256]{2,1,0:T(8,128)S(1)}, f32[2,256,512]{2,1,0:T(8,128)S(1)}) custom-call(s32[4,8,256]{2,1,0:T(8,128)S(1)} %get-tuple-element.55.marks, f32[2,2,256,256]{3,2,1,0:T(8,128)S(1)} %get-tuple-element.56.field, ...), custom_call_target="tpu_custom_call" | custom-call | flops 100000000 | bytes 1 | tf_op jit(solution)/shard_map/propagate/pallas_call | solution.py:484
  27.8 0.7 %collective-permute-start.10 = (f32[2,128,256]{2,1,0:T(8,128)S(1)}, f32[2,128,256]{2,1,0:T(8,128)S(1)}, u32[]{:S(2)}, u32[]{:S(2)}) collective-permute-start(f32[2,128,256]{2,1,0:T(8,128)S(1)} %get-tuple-element.68), channel_id=1, source_target_pairs={{1,2},{2,1},{3,4},{4,3},{5,6},{6,5},{9,10},{10,9},{11,12},{12,11},... | collective-permute-start | bytes 786440 | tf_op jit(solution)/shard_map/ppermute | solution.py:45
  28.5 3.0 %collective-permute-start.11 = (f32[2,128,256]{2,1,0:T(8,128)S(1)}, f32[2,128,256]{2,1,0:T(8,128)S(1)}, u32[]{:S(2)}, u32[]{:S(2)}) collective-permute-start(f32[2,128,256]{2,1,0:T(8,128)S(1)} %get-tuple-element.69), channel_id=1, source_target_pairs={{0,1},{1,0},{2,3},{3,2},{4,5},{5,4},{6,7},{7,6},{8,9},{9,8},{10,11... | collective-permute-start | bytes 786440 | tf_op jit(solution)/shard_map/ppermute | solution.py:45
  31.5 0.7 %collective-permute-start.8 = (f32[4,128,256]{2,1,0:T(8,128)S(1)}, f32[4,128,256]{2,1,0:T(8,128)S(1)}, u32[]{:S(2)}, u32[]{:S(2)}) collective-permute-start(f32[4,128,256]{2,1,0:T(8,128)S(1)} %get-tuple-element.65), channel_id=1, source_target_pairs={{1,2},{2,1},{3,4},{4,3},{5,6},{6,5},{9,10},{10,9},{11,12},{12,11},... | collective-permute-start | bytes 1572872 | tf_op jit(solution)/shard_map/ppermute | solution.py:45
  32.2 0.0 collective-permute-done.2.first.received
  32.2 3.0 %collective-permute-start.9 = (f32[4,128,256]{2,1,0:T(8,128)S(1)}, f32[4,128,256]{2,1,0:T(8,128)S(1)}, u32[]{:S(2)}, u32[]{:S(2)}) collective-permute-start(f32[4,128,256]{2,1,0:T(8,128)S(1)} %get-tuple-element.66), channel_id=1, source_target_pairs={{0,1},{1,0},{2,3},{3,2},{4,5},{5,4},{6,7},{7,6},{8,9},{9,8},{10,11... | collective-permute-start | bytes 1572872 | tf_op jit(solution)/shard_map/ppermute | solution.py:45
  35.3 0.0 collective-permute-done.3.second.received
  35.3 0.1 join3.1.total2_second
  35.3 0.0 collective-permute-done.10.from_second
  35.3 0.0 collective-permute-done.11.from_first
  35.3 0.1 narrow1.1
  35.4 1.3 %collective-permute-start.14 = (f32[1,256,128]{2,1,0:T(8,128)S(1)}, f32[1,256,128]{2,1,0:T(8,128)S(1)}, u32[]{:S(2)}, u32[]{:S(2)}) collective-permute-start(f32[1,256,128]{2,1,0:T(8,128)S(1)} %get-tuple-element.72), channel_id=1, source_target_pairs={{8,24},{16,0},{9,25},{17,1},{10,26},{18,2},{11,27},{19,3},{12,28},... | collective-permute-start | bytes 393224 | tf_op jit(solution)/shard_map/ppermute | solution.py:56
  36.7 2.5 %collective-permute-start.12 = (f32[2,256,128]{2,1,0:T(8,128)S(1)}, f32[2,256,128]{2,1,0:T(8,128)S(1)}, u32[]{:S(2)}, u32[]{:S(2)}) collective-permute-start(f32[2,256,128]{2,1,0:T(8,128)S(1)} %get-tuple-element.70), channel_id=1, source_target_pairs={{0,8},{8,0},{16,24},{24,16},{1,9},{9,1},{17,25},{25,17},{2,10},{10... | collective-permute-start | bytes 786440 | tf_op jit(solution)/shard_map/ppermute | solution.py:45
  39.2 0.7 %collective-permute-start.13 = (f32[1,256,128]{2,1,0:T(8,128)S(1)}, f32[1,256,128]{2,1,0:T(8,128)S(1)}, u32[]{:S(2)}, u32[]{:S(2)}) collective-permute-start(f32[1,256,128]{2,1,0:T(8,128)S(1)} %get-tuple-element.71), channel_id=1, source_target_pairs={{8,16},{16,8},{9,17},{17,9},{10,18},{18,10},{11,19},{19,11},{12,20... | collective-permute-start | bytes 393224 | tf_op jit(solution)/shard_map/ppermute | solution.py:45
  39.9 3.7 %collective-permute-done.14 = f32[1,256,128]{2,1,0:T(8,128)S(1)} collective-permute-done((f32[1,256,128]{2,1,0:T(8,128)S(1)}, f32[1,256,128]{2,1,0:T(8,128)S(1)}, u32[]{:S(2)}, u32[]{:S(2)}) %collective-permute-start.14) | collective-permute-done | bytes 131104 | tf_op jit(solution)/shard_map/ppermute | solution.py:56
  43.5 2.0 %collective-permute-start.15 = (f32[1,256,128]{2,1,0:T(8,128)S(1)}, f32[1,256,128]{2,1,0:T(8,128)S(1)}, u32[]{:S(2)}, u32[]{:S(2)}) collective-permute-start(f32[1,256,128]{2,1,0:T(8,128)S(1)} %collective-permute-done.14), channel_id=1, source_target_pairs={{24,16},{0,8},{25,17},{1,9},{26,18},{2,10},{27,19},{3,11},{28,20},... | collective-permute-start | bytes 393224 | tf_op jit(solution)/shard_map/ppermute | solution.py:56
  45.5 3.7 %illuminate.1.scale = f32[256,256]{1,0:T(8,128)S(1)} custom-call(s32[2,1,2]{2,1,0:T(1,128)S(1)} %copy-done.4, f32[2,256,256]{2,1,0:T(8,128)S(1)} %copy-done.3, f32[4,136,256]{2,1,0:T(8,128)S(1)} %collective-permute-done.1.from_first.up.own_first, f32[4,136,256]{2,1,0:T(8,128)S(1)} %collective-permute-done.from_second.down.own_second, ...), custom_call_target="tpu_custom_call" | custom-call | flops 2500000000 | bytes 1 | tf_op jit(solution)/shard_map/illuminate/pallas_call | solution.py:484
  49.2 0.0 collective-permute-done.8.inner_second
  49.2 0.0 collective-permute-done.9.inner_first
  49.2 1.0 %update2.1.begun = f32[2,2,256,256]{3,2,1,0:T(8,128)} custom-call(f32[2,2,256,256]{3,2,1,0:T(8,128)S(1)} %copy-done.1, f32[256,256]{1,0:T(8,128)S(1)} %illuminate.1.scale, f32[2,256,128]{2,1,0:T(8,128)S(1)} %join2.1.total2_first, f32[2,256,128]{2,1,0:T(8,128)S(1)} %join3.1.total2_second, f32[4,128,256]{2,1,0:T(8,128)S(1)} %collective-permute-done.8.inner_second, ...), custom_call_target="tpu_custom_call" | custom-call | flops 100000000 | bytes 1 | tf_op jit(solution)/shard_map/update2/pallas_call | solution.py:484
  50.2 0.0 collective-permute-done.13.second1_re
  50.2 0.0 collective-permute-done.15.second1_im
  50.2 0.0 collective-permute-done.12.first1
  50.2 0.9 %update.1 = f32[2,2,256,256]{3,2,1,0:T(8,128)} custom-call(f32[2,2,256,256]{3,2,1,0:T(8,128)} %update2.1.begun, f32[2,256,128]{2,1,0:T(8,128)S(1)} %collective-permute-done.12.first1, f32[1,256,128]{2,1,0:T(8,128)S(1)} %collective-permute-done.13.second1_re, f32[1,256,128]{2,1,0:T(8,128)S(1)} %collective-permute-done.15.second1_im, ...), custom_call_target="tpu_custom_call", output_to_operand_aliasing={{}: (0, {})} | custom-call | flops 1000000000 | bytes 1 | tf_op jit(solution)/shard_map/update/pallas_call | solution.py:484
  (2 shorter events, 0.1 us)
Async XLA Ops:
  0.0 1.2 %copy-start = (f32[2,2,256,256]{3,2,1,0:T(8,128)S(1)}, f32[2,2,256,256]{3,2,1,0:T(8,128)}, u32[]{:S(2)}) copy-start(f32[2,2,256,256]{3,2,1,0:T(8,128)} %object_field.9) | copy-start | bytes 3145732
  1.2 3.8 %copy-start.1 = (f32[2,2,256,256]{3,2,1,0:T(8,128)S(1)}, f32[2,2,256,256]{3,2,1,0:T(8,128)}, u32[]{:S(2)}) copy-start(f32[2,2,256,256]{3,2,1,0:T(8,128)} %object_field.9) | copy-start | bytes 3145732
  1.2 3.8 %copy-start.2 = (bf16[4,256,512]{2,1,0:T(8,128)(2,1)S(1)}, bf16[4,256,512]{2,1,0:T(8,128)(2,1)}, u32[]{:S(2)}) copy-start(bf16[4,256,512]{2,1,0:T(8,128)(2,1)} %constant.2.clone.table) | copy-start | bytes 3145732
  1.2 3.8 %copy-start.5 = (bf16[2,1,2,256,256]{4,3,2,1,0:T(8,128)(2,1)S(1)}, bf16[2,1,2,256,256]{4,3,2,1,0:T(8,128)(2,1)}, u32[]{:S(2)}) copy-start(bf16[2,1,2,256,256]{4,3,2,1,0:T(8,128)(2,1)} %residual.1) | copy-start | bytes 1572868
  1.2 3.8 %copy-start.6 = (bf16[2,1,2,256,256]{4,3,2,1,0:T(8,128)(2,1)S(1)}, bf16[2,1,2,256,256]{4,3,2,1,0:T(8,128)(2,1)}, u32[]{:S(2)}) copy-start(bf16[2,1,2,256,256]{4,3,2,1,0:T(8,128)(2,1)} %wave.1) | copy-start | bytes 1572868
  1.3 3.7 %copy-start.4 = (s32[2,1,2]{2,1,0:T(1,128)S(1)}, s32[2,1,2]{2,1,0:T(1,128)}, u32[]{:S(2)}) copy-start(s32[2,1,2]{2,1,0:T(1,128)} %pos.1) | copy-start | bytes 52
  1.3 10.6 %collective-permute-start.4 = (f32[2,256,128]{2,1,0:T(8,128)S(1)}, f32[2,256,128]{2,1,0:T(8,128)S(1)}, u32[]{:S(2)}, u32[]{:S(2)}) collective-permute-start(f32[2,256,128]{2,1,0:T(8,128)S(1)} %get-tuple-element.50), channel_id=1, source_target_pairs={{0,8},{8,0},{16,24},{24,16},{1,9},{9,1},{17,25},{25,17},{2,10},{10... | collective-permute-start | bytes 786440 | tf_op jit(solution)/shard_map/ppermute | solution.py:45
  4.3 7.6 %collective-permute-start.5 = (f32[2,256,128]{2,1,0:T(8,128)S(1)}, f32[2,256,128]{2,1,0:T(8,128)S(1)}, u32[]{:S(2)}, u32[]{:S(2)}) collective-permute-start(f32[2,256,128]{2,1,0:T(8,128)S(1)} %get-tuple-element.51), channel_id=1, source_target_pairs={{8,16},{16,8},{9,17},{17,9},{10,18},{18,10},{11,19},{19,11},{12,20... | collective-permute-start | bytes 786440 | tf_op jit(solution)/shard_map/ppermute | solution.py:45
  8.2 8.7 %collective-permute-start = (f32[4,136,256]{2,1,0:T(8,128)S(1)}, f32[4,136,256]{2,1,0:T(8,128)S(1)}, u32[]{:S(2)}, u32[]{:S(2)}) collective-permute-start(f32[4,136,256]{2,1,0:T(8,128)S(1)} %get-tuple-element.39), channel_id=1, source_target_pairs={{1,2},{2,1},{3,4},{4,3},{5,6},{6,5},{9,10},{10,9},{11,12},{12,11},... | collective-permute-start | bytes 1671176 | tf_op jit(solution)/shard_map/ppermute | solution.py:45
  8.9 6.8 %copy-start.3 = (f32[2,256,256]{2,1,0:T(8,128)S(1)}, f32[2,256,256]{2,1,0:T(8,128)}, u32[]{:S(2)}) copy-start(f32[2,256,256]{2,1,0:T(8,128)} %probe.3) | copy-start | bytes 1572868
  9.0 8.0 %collective-permute-start.1 = (f32[4,136,256]{2,1,0:T(8,128)S(1)}, f32[4,136,256]{2,1,0:T(8,128)S(1)}, u32[]{:S(2)}, u32[]{:S(2)}) collective-permute-start(f32[4,136,256]{2,1,0:T(8,128)S(1)} %get-tuple-element.40), channel_id=1, source_target_pairs={{0,1},{1,0},{2,3},{3,2},{4,5},{5,4},{6,7},{7,6},{8,9},{9,8},{10,11... | collective-permute-start | bytes 1671176 | tf_op jit(solution)/shard_map/ppermute | solution.py:45
  12.0 12.7 %collective-permute-start.6 = (f32[2,128,256]{2,1,0:T(8,128)S(1)}, f32[2,128,256]{2,1,0:T(8,128)S(1)}, u32[]{:S(2)}, u32[]{:S(2)}) collective-permute-start(f32[2,128,256]{2,1,0:T(8,128)S(1)} %get-tuple-element.52), channel_id=1, source_target_pairs={{1,2},{2,1},{3,4},{4,3},{5,6},{6,5},{9,10},{10,9},{11,12},{12,11},... | collective-permute-start | bytes 786440 | tf_op jit(solution)/shard_map/ppermute | solution.py:45
  12.7 12.1 %collective-permute-start.7 = (f32[2,128,256]{2,1,0:T(8,128)S(1)}, f32[2,128,256]{2,1,0:T(8,128)S(1)}, u32[]{:S(2)}, u32[]{:S(2)}) collective-permute-start(f32[2,128,256]{2,1,0:T(8,128)S(1)} %get-tuple-element.53), channel_id=1, source_target_pairs={{0,1},{1,0},{2,3},{3,2},{4,5},{5,4},{6,7},{7,6},{8,9},{9,8},{10,11... | collective-permute-start | bytes 786440 | tf_op jit(solution)/shard_map/ppermute | solution.py:45
  17.1 15.2 %collective-permute-start.2 = (f32[2,280,128]{2,1,0:T(8,128)S(1)}, f32[2,280,128]{2,1,0:T(8,128)S(1)}, u32[]{:S(2)}, u32[]{:S(2)}) collective-permute-start(f32[2,280,128]{2,1,0:T(8,128)S(1)} %get-tuple-element.48), channel_id=1, source_target_pairs={{0,8},{8,0},{16,24},{24,16},{1,9},{9,1},{17,25},{25,17},{2,10},{10... | collective-permute-start | bytes 860168 | tf_op jit(solution)/shard_map/ppermute | solution.py:45
  24.0 11.2 %collective-permute-start.3 = (f32[2,280,128]{2,1,0:T(8,128)S(1)}, f32[2,280,128]{2,1,0:T(8,128)S(1)}, u32[]{:S(2)}, u32[]{:S(2)}) collective-permute-start(f32[2,280,128]{2,1,0:T(8,128)S(1)} %get-tuple-element.49), channel_id=1, source_target_pairs={{8,16},{16,8},{9,17},{17,9},{10,18},{18,10},{11,19},{19,11},{12,20... | collective-permute-start | bytes 860168 | tf_op jit(solution)/shard_map/ppermute | solution.py:45
  27.8 7.5 %collective-permute-start.10 = (f32[2,128,256]{2,1,0:T(8,128)S(1)}, f32[2,128,256]{2,1,0:T(8,128)S(1)}, u32[]{:S(2)}, u32[]{:S(2)}) collective-permute-start(f32[2,128,256]{2,1,0:T(8,128)S(1)} %get-tuple-element.68), channel_id=1, source_target_pairs={{1,2},{2,1},{3,4},{4,3},{5,6},{6,5},{9,10},{10,9},{11,12},{12,11},... | collective-permute-start | bytes 786440 | tf_op jit(solution)/shard_map/ppermute | solution.py:45
  28.5 6.8 %collective-permute-start.11 = (f32[2,128,256]{2,1,0:T(8,128)S(1)}, f32[2,128,256]{2,1,0:T(8,128)S(1)}, u32[]{:S(2)}, u32[]{:S(2)}) collective-permute-start(f32[2,128,256]{2,1,0:T(8,128)S(1)} %get-tuple-element.69), channel_id=1, source_target_pairs={{0,1},{1,0},{2,3},{3,2},{4,5},{5,4},{6,7},{7,6},{8,9},{9,8},{10,11... | collective-permute-start | bytes 786440 | tf_op jit(solution)/shard_map/ppermute | solution.py:45
  31.5 17.7 %collective-permute-start.8 = (f32[4,128,256]{2,1,0:T(8,128)S(1)}, f32[4,128,256]{2,1,0:T(8,128)S(1)}, u32[]{:S(2)}, u32[]{:S(2)}) collective-permute-start(f32[4,128,256]{2,1,0:T(8,128)S(1)} %get-tuple-element.65), channel_id=1, source_target_pairs={{1,2},{2,1},{3,4},{4,3},{5,6},{6,5},{9,10},{10,9},{11,12},{12,11},... | collective-permute-start | bytes 1572872 | tf_op jit(solution)/shard_map/ppermute | solution.py:45
  32.2 17.0 %collective-permute-start.9 = (f32[4,128,256]{2,1,0:T(8,128)S(1)}, f32[4,128,256]{2,1,0:T(8,128)S(1)}, u32[]{:S(2)}, u32[]{:S(2)}) collective-permute-start(f32[4,128,256]{2,1,0:T(8,128)S(1)} %get-tuple-element.66), channel_id=1, source_target_pairs={{0,1},{1,0},{2,3},{3,2},{4,5},{5,4},{6,7},{7,6},{8,9},{9,8},{10,11... | collective-permute-start | bytes 1572872 | tf_op jit(solution)/shard_map/ppermute | solution.py:45
  35.4 8.1 %collective-permute-start.14 = (f32[1,256,128]{2,1,0:T(8,128)S(1)}, f32[1,256,128]{2,1,0:T(8,128)S(1)}, u32[]{:S(2)}, u32[]{:S(2)}) collective-permute-start(f32[1,256,128]{2,1,0:T(8,128)S(1)} %get-tuple-element.72), channel_id=1, source_target_pairs={{8,24},{16,0},{9,25},{17,1},{10,26},{18,2},{11,27},{19,3},{12,28},... | collective-permute-start | bytes 393224 | tf_op jit(solution)/shard_map/ppermute | solution.py:56
  36.7 13.5 %collective-permute-start.12 = (f32[2,256,128]{2,1,0:T(8,128)S(1)}, f32[2,256,128]{2,1,0:T(8,128)S(1)}, u32[]{:S(2)}, u32[]{:S(2)}) collective-permute-start(f32[2,256,128]{2,1,0:T(8,128)S(1)} %get-tuple-element.70), channel_id=1, source_target_pairs={{0,8},{8,0},{16,24},{24,16},{1,9},{9,1},{17,25},{25,17},{2,10},{10... | collective-permute-start | bytes 786440 | tf_op jit(solution)/shard_map/ppermute | solution.py:45
  39.2 11.0 %collective-permute-start.13 = (f32[1,256,128]{2,1,0:T(8,128)S(1)}, f32[1,256,128]{2,1,0:T(8,128)S(1)}, u32[]{:S(2)}, u32[]{:S(2)}) collective-permute-start(f32[1,256,128]{2,1,0:T(8,128)S(1)} %get-tuple-element.71), channel_id=1, source_target_pairs={{8,16},{16,8},{9,17},{17,9},{10,18},{18,10},{11,19},{19,11},{12,20... | collective-permute-start | bytes 393224 | tf_op jit(solution)/shard_map/ppermute | solution.py:45
  43.5 6.7 %collective-permute-start.15 = (f32[1,256,128]{2,1,0:T(8,128)S(1)}, f32[1,256,128]{2,1,0:T(8,128)S(1)}, u32[]{:S(2)}, u32[]{:S(2)}) collective-permute-start(f32[1,256,128]{2,1,0:T(8,128)S(1)} %collective-permute-done.14), channel_id=1, source_target_pairs={{24,16},{0,8},{25,17},{1,9},{26,18},{2,10},{27,19},{3,11},{28,20},... | collective-permute-start | bytes 393224 | tf_op jit(solution)/shard_map/ppermute | solution.py:56
